TPU v7x, 32 devices: a whole 2x2x4 slice. The times are simulated.
32 devices in a mesh: grp: 1, row: 32 (over z, y, x, core).
Axes of the slice: x: 2, y: 2, z: 4, core: 2. Of those that a mesh axis runs over, the one named last changes fastest.
Arguments:
- pair: float32 [128, 128, 128], P(('grp', 'row')), may hold values from -6 to 6
- single: float32 [128, 384], P(('grp', 'row')), may hold values from -6 to 6
- quats: float32 [3, 128], P(None, ('grp', 'row')), may hold values from -6 to 6
- translate: float32 [3, 128], P(None, ('grp', 'row')), may hold values from -12 to 12
- res_mask: int32 [128], P(('grp', 'row')), may hold values 0 or 1
- chain_ids: int32 [128], P(('grp', 'row')), may hold values from 0 to 3, never falling along the last dimension, each value on 1 to 64 neighbouring positions
- tri_weight: bfloat16 [128, 640], replicated, may hold values from -0.5 to 0.5
- tri_out_weight: bfloat16 [128, 128], replicated, may hold values from -0.5 to 0.5
- qkv_weight: bfloat16 [384, 1152], replicated, may hold values from -0.3125 to 0.3125
- bias_weight: float32 [128, 12], replicated, may hold values from -0.5 to 0.5
- head_gamma: float32 [12], replicated, may hold values from 0.05 to 1
- chain_bias: float32 [2, 12], replicated, may hold values from -4 to 4
- out_weight: bfloat16 [2112, 384], replicated, may hold values from -0.125 to 0.125
- frame_weight: float32 [384, 6], replicated, may hold values from -0.3125 to 0.3125
Outputs:
- pair_out: float32 [128, 128, 128], P(('grp', 'row'))
- single_out: float32 [128, 384], P(('grp', 'row'))
- rotation_out: float32 [9, 128], P(None, ('grp', 'row'))
- translation_out: float32 [3, 128], P(None, ('grp', 'row'))
Inputs may be any that keep to these rules, and one draw needn't show every extreme that they name: `chain_ids`: chains are contiguous runs of residues, the longest 128 // 2.
All inputs are finite; a program needn't handle non-finite values. No bound on the sum of `res_mask` on one device may be relied on, other than what follows from the above.
Results may differ from a plain program's by a relative error of at most 0.0078.
Values may be sent and summed in bfloat16 or wider, within the bound.
No kernel may reach another device: no remote copies, remote signals or barrier semaphores. Data moves between devices by JAX's collectives and lax.ppermute only.
A program may use at most 64 MiB of HBM per device.

v0:
```python
import math

import jax
import jax.numpy as jnp
from jax import lax
from jax.sharding import PartitionSpec as P

CH = 128
H = 12
CHEAD = 16
PQ = 4
PV = 8
ITERS = 2


highest = lax.Precision.HIGHEST
epsilon = 1e-05
mask_fill = 100000.0


def layer_norm(values):
    center = values - jnp.mean(values, axis=-1, keepdims=True)
    spread = jnp.mean(center * center, axis=-1, keepdims=True)
    return center * lax.rsqrt(spread + epsilon)


def quat_rotation(vector):
    inverse_norm = lax.rsqrt(1.0 + jnp.sum(vector * vector, axis=0))
    axis_one = vector[0] * inverse_norm
    axis_two = vector[1] * inverse_norm
    axis_three = vector[2] * inverse_norm
    entries = [
        1.0 - 2.0 * (axis_two * axis_two + axis_three * axis_three),
        2.0 * (axis_one * axis_two - inverse_norm * axis_three),
        2.0 * (axis_one * axis_three + inverse_norm * axis_two),
        2.0 * (axis_one * axis_two + inverse_norm * axis_three),
        1.0 - 2.0 * (axis_one * axis_one + axis_three * axis_three),
        2.0 * (axis_two * axis_three - inverse_norm * axis_one),
        2.0 * (axis_one * axis_three - inverse_norm * axis_two),
        2.0 * (axis_two * axis_three + inverse_norm * axis_one),
        1.0 - 2.0 * (axis_one * axis_one + axis_two * axis_two),
    ]
    return jnp.stack(entries, axis=0)


def rotate(rotation, points):
    output_rows = []
    for target in range(3):
        summed = (
            rotation[target * 3][:, None] * points[:, 0]
            + rotation[target * 3 + 1][:, None] * points[:, 1]
            + rotation[target * 3 + 2][:, None] * points[:, 2]
        )
        output_rows.append(summed)
    return jnp.stack(output_rows, axis=1)


def rotate_back(rotation, points):
    output_rows = []
    for target in range(3):
        summed = (
            rotation[target][:, None] * points[:, 0]
            + rotation[3 + target][:, None] * points[:, 1]
            + rotation[6 + target][:, None] * points[:, 2]
        )
        output_rows.append(summed)
    return jnp.stack(output_rows, axis=1)


def compose(rotation, step_rotation):
    entries = []
    for target in range(3):
        for column in range(3):
            entries.append(
                rotation[target * 3] * step_rotation[column]
                + rotation[target * 3 + 1] * step_rotation[3 + column]
                + rotation[target * 3 + 2] * step_rotation[6 + column]
            )
    return jnp.stack(entries, axis=0)


def project_single(single_state, rotation, translation, qkv_weight):
    row_count = single_state.shape[0]
    projected = jnp.dot(
        single_state.astype(jnp.bfloat16), qkv_weight, preferred_element_type=jnp.float32
    )
    head_width = H * CHEAD
    queries = projected[:, :head_width].reshape(row_count, H, CHEAD)
    key_part = projected[:, head_width : 3 * head_width]
    point_start = 3 * head_width
    query_local = projected[:, point_start : point_start + 3 * H * PQ].reshape(row_count, 3, H * PQ)
    key_local = projected[:, point_start + 3 * H * PQ : point_start + 6 * H * PQ].reshape(
        row_count, 3, H * PQ
    )
    value_local = projected[:, point_start + 6 * H * PQ :].reshape(row_count, 3, H * PV)
    offset_global = translation.T[:, :, None]
    query_global = rotate(rotation, query_local) + offset_global
    key_global = rotate(rotation, key_local) + offset_global
    value_global = rotate(rotation, value_local) + offset_global
    key_rows = jnp.concatenate(
        [key_part, key_global.reshape(row_count, -1), value_global.reshape(row_count, -1)], axis=1
    )
    return (queries, query_global, key_rows)


def attend(
    queries,
    query_global,
    rotation_own,
    translate_own,
    pair_bias,
    pair_half,
    chain_own,
    key_rows,
    mask_all,
    chain_all,
    head_gamma,
    chain_bias,
):
    row_count = queries.shape[0]
    head_width = H * CHEAD
    key_heads = key_rows[:, :head_width].reshape(-1, H, CHEAD)
    values_all = key_rows[:, head_width : 2 * head_width].reshape(-1, H, CHEAD)
    point_start = 2 * head_width
    key_global = key_rows[:, point_start : point_start + 3 * H * PQ].reshape(-1, 3, H, PQ)
    value_global = key_rows[:, point_start + 3 * H * PQ :].reshape(-1, 3, H, PV)
    query_points = query_global.reshape(row_count, 3, H, PQ)
    scalar_dots = jnp.einsum("ihc,jhc->hij", queries, key_heads, precision=highest) / math.sqrt(
        CHEAD
    )
    difference = query_points[:, None] - key_global[None, :]
    distance = jnp.transpose(jnp.sum(difference * difference, axis=(2, 4)), (2, 0, 1))
    point_weight = head_gamma * (math.sqrt(2.0 / (9.0 * PQ)) * 0.5)
    same_chain = chain_own[:, None] == chain_all[None, :]
    chain_term = jnp.where(
        same_chain[None], chain_bias[1][:, None, None], chain_bias[0][:, None, None]
    )
    logits = math.sqrt(1.0 / 3.0) * (
        scalar_dots + jnp.transpose(pair_bias, (2, 0, 1)) - point_weight[:, None, None] * distance
    )
    logits = logits + chain_term + mask_fill * (mask_all - 1.0)[None, None, :]
    attention = jax.nn.softmax(logits, axis=-1)
    out_scalar = jnp.einsum("hij,jhc->ihc", attention, values_all, precision=highest)
    out_global = jnp.einsum("hij,jahv->iahv", attention, value_global, precision=highest)
    relative = out_global - translate_own.T[:, :, None, None]
    out_local = rotate_back(rotation_own, relative.reshape(row_count, 3, H * PV))
    out_norm = jnp.sqrt(jnp.sum(out_local * out_local, axis=1) + 1e-08)
    out_pair = jnp.einsum(
        "hij,ijc->ihc",
        attention.astype(jnp.bfloat16),
        pair_half,
        preferred_element_type=jnp.float32,
    )
    return jnp.concatenate(
        [
            out_scalar.reshape(row_count, -1),
            out_local.reshape(row_count, -1),
            out_norm,
            out_pair.reshape(row_count, -1),
        ],
        axis=1,
    )


def channel_product(pieces):
    return jnp.einsum("ikgc,jkgc->ijgc", pieces[0], pieces[1], preferred_element_type=jnp.float32)


def local(
    pair,
    single,
    quats,
    translate,
    res_mask,
    chain_ids,
    tri_weight,
    tri_out_weight,
    qkv_weight,
    bias_weight,
    head_gamma,
    chain_bias,
    out_weight,
    frame_weight,
):
    row_count = pair.shape[0]
    mask_all, chain_all = (
        lax.all_gather(res_mask, "row", axis=0, tiled=True),
        lax.all_gather(chain_ids, "row", axis=0, tiled=True),
    )
    mask_float = mask_all.astype(jnp.float32)
    own_mask = res_mask.astype(jnp.float32)
    normed = layer_norm(pair).astype(jnp.bfloat16)
    projected = jnp.dot(normed, tri_weight, preferred_element_type=jnp.float32)
    pair_mask = own_mask[:, None, None] * mask_float[None, :, None]
    left_side = (
        jax.nn.sigmoid(projected[..., :CH]) * projected[..., CH : 2 * CH] * pair_mask
    ).astype(jnp.bfloat16)
    right_side = (
        jax.nn.sigmoid(projected[..., 2 * CH : 3 * CH])
        * projected[..., 3 * CH : 4 * CH]
        * pair_mask
    ).astype(jnp.bfloat16)
    out_gate = jax.nn.sigmoid(projected[..., 4 * CH :])
    groups = lax.axis_size("row")
    block_width = CH // groups
    left_blocks = left_side.reshape(row_count, left_side.shape[1], groups, block_width)
    right_blocks = right_side.reshape(row_count, right_side.shape[1], groups, block_width)
    formed = channel_product(
        (
            lax.all_to_all(left_blocks, "row", split_axis=2, concat_axis=0, tiled=True),
            lax.all_to_all(right_blocks, "row", split_axis=2, concat_axis=0, tiled=True),
        )
    )
    product = lax.all_to_all(formed, "row", split_axis=0, concat_axis=2, tiled=True)
    product = product.reshape(row_count, left_side.shape[1], CH)
    update = jnp.dot(
        layer_norm(product).astype(jnp.bfloat16), tri_out_weight, preferred_element_type=jnp.float32
    )
    pair_out = pair + out_gate * update
    normed_pair = layer_norm(pair_out)
    pair_bias = jnp.dot(
        normed_pair, bias_weight, precision=highest, preferred_element_type=jnp.float32
    )
    pair_half = normed_pair.astype(jnp.bfloat16)
    single_state = single
    rotation = quat_rotation(quats)
    translation = translate
    for iteration in range(ITERS):
        queries, query_global, key_rows = project_single(
            single_state, rotation, translation, qkv_weight
        )
        key_all = lax.all_gather(key_rows, "row", axis=0, tiled=True)
        combined = attend(
            queries,
            query_global,
            rotation,
            translation,
            pair_bias,
            pair_half,
            chain_ids,
            key_all,
            mask_float,
            chain_all,
            head_gamma,
            chain_bias,
        )
        update = jnp.dot(
            combined.astype(jnp.bfloat16), out_weight, preferred_element_type=jnp.float32
        )
        single_state = layer_norm(single_state + update)
        frame_update = jnp.dot(
            single_state, frame_weight, precision=highest, preferred_element_type=jnp.float32
        )
        shift_step = rotate(rotation, frame_update[:, 3:][:, :, None])[:, :, 0].T
        translation = translation + shift_step
        rotation = compose(rotation, quat_rotation(frame_update[:, :3].T))
    return (pair_out, single_state, rotation, translation)


def solution(mesh):
    placed = (
        P(("grp", "row"), None, None),
        P(("grp", "row"), None),
        P(None, ("grp", "row")),
        P(None, ("grp", "row")),
        P(("grp", "row")),
        P(("grp", "row")),
        P(),
        P(),
        P(),
        P(),
        P(),
        P(),
        P(),
        P(),
    )
    return jax.shard_map(
        local,
        mesh=mesh,
        in_specs=placed,
        out_specs=(
            P(("grp", "row"), None, None),
            P(("grp", "row"), None),
            P(None, ("grp", "row")),
            P(None, ("grp", "row")),
        ),
        check_vma=False,
    )
```

profile of v0, /device:TPU:0, one launch (start us, length us, event | category | flops | bytes accessed | tf_op | source)
XLA Modules:
  0.0 202.8 jit_solution(16813609036361687536)
XLA Ops:
  0.7 1.2 reduce_sum.171
  1.9 1.2 multiply_reduce_fusion.4
  3.1 0.7 convert_element_type.36
  3.8 0.8 dynamic-update-slice
  4.6 0.8 dynamic-update-slice.1
  5.4 42.0 %all-reduce.2 = (s32[128]{0:T(128)S(1)}, s32[128]{0:T(128)S(1)}) all-reduce(s32[128]{0:T(128)S(1)} %dynamic-update-slice, s32[128]{0:T(128)S(1)} %dynamic-update-slice.1), channel_id=1, replica_groups=mesh['grp'=1,'row'=32] {'row'}, use_global_device_ids=true, to_apply=%add | all-reduce | flops 256 | bytes 2048
  47.4 1.4 fusion.33
  49.2 0.7 copy.226
  50.0 4.4 %all-to-all-start = ((bf16[4,128,32,4]{1,3,0,2:T(4,128)(2,1)}), bf16[4,128,32,4]{1,3,0,2:T(4,128)(2,1)S(1)}, u32[]{:S(2)}, u32[]{:S(2)}) async-start(bf16[4,128,32,4]{1,3,0,2:T(4,128)(2,1)} %copy.226), calls=%async_computation | async-start | bytes 262144 | tf_op jit(solution)/shard_map/all_to_all | solution.py:211
  55.0 1.4 fusion.65
  57.1 0.5 add_multiply_fusion.18
  57.7 0.6 fusion.79
  59.1 0.6 broadcast_compare_fusion
  59.9 0.5 broadcast_multiply_fusion.6
  60.7 0.7 copy.229
  62.6 5.3 %all-to-all-start.1 = ((bf16[4,128,32,4]{1,3,0,2:T(4,128)(2,1)}), bf16[4,128,32,4]{1,3,0,2:T(4,128)(2,1)S(1)}, u32[]{:S(2)}, u32[]{:S(2)}) async-start(bf16[4,128,32,4]{1,3,0,2:T(4,128)(2,1)} %copy.229), calls=%async_computation.1 | async-start | bytes 262144 | tf_op jit(solution)/shard_map/all_to_all | solution.py:210
  67.9 45.7 %all-gather = f32[32,4,816]{2,1,0:T(4,128)} all-gather(f32[1,4,816]{2,1,0:T(4,128)S(1)} %maximum_bitcast_fusion), channel_id=1, replica_groups=mesh['grp'=1,'row'=32] {'row'}, dimensions={0}, use_global_device_ids=true | all-gather | bytes 430848 | tf_op jit(solution)/shard_map/all_gather | solution.py:232
  113.6 1.9 reshape.2053
  115.5 0.9 slice.355
  116.5 0.7 copy.251
  117.3 1.8 fusion.75
  119.4 0.8 copy.231
  120.3 3.3 %all-to-all-start.2 = ((f32[128,128,1,4]{1,3,2,0:T(4,128)}), f32[128,128,1,4]{1,3,2,0:T(4,128)}, u32[]{:S(2)}, u32[]{:S(2)}) async-start(f32[128,128,1,4]{1,3,2,0:T(4,128)} %copy.231), calls=%async_computation.2 | async-start | bytes 524288 | tf_op jit(solution)/shard_map/all_to_all | solution.py:214
  123.6 1.8 multiply_reduce_fusion.1
  125.3 0.7 slice.349
  126.0 1.0 slice.356
  127.1 1.3 copy.265
  128.4 1.0 copy.242
  129.4 1.7 copy.243
  131.1 0.7 reshape.2029
  131.8 0.8 copy.254
  132.5 0.7 copy.284
  133.3 0.8 copy.319
  134.0 0.8 copy.318
  134.8 0.7 copy.317
  135.4 1.3 slice_bitcast_fusion.5
  136.8 0.6 add_multiply_fusion.1
  137.4 1.0 copy.232
  138.4 0.9 copy.233
  139.2 0.7 reduce_sum.173
  140.0 0.8 broadcast_multiply_fusion.2
  141.0 1.3 fusion.81
  143.8 1.5 fusion.2
  145.4 0.8 multiply_add_fusion.29
  150.5 43.1 %all-gather.1 = f32[32,4,816]{2,1,0:T(4,128)S(1)} all-gather(f32[1,4,816]{2,1,0:T(4,128)S(1)} %maximum_bitcast_fusion.1), channel_id=1, replica_groups=mesh['grp'=1,'row'=32] {'row'}, dimensions={0}, use_global_device_ids=true | all-gather | bytes 430848 | tf_op jit(solution)/shard_map/all_gather | solution.py:232
  196.6 1.5 fusion.1
  201.2 0.7 copy.306
  202.1 0.7 stack.49
  (273 shorter events, 16.2 us)
Async XLA Ops:
  0.6 146.7 %copy-start = (bf16[2112,384]{1,0:T(8,128)(2,1)S(1)}, bf16[2112,384]{1,0:T(8,128)(2,1)}, u32[]{:S(2)}) copy-start(bf16[2112,384]{1,0:T(8,128)(2,1)} %param.26) | copy-start | bytes 4866052
  47.4 7.0 %copy-start.9 = (f32[3,4]{1,0:T(4,128)S(1)}, f32[3,4]{1,0:T(4,128)}, u32[]{:S(2)}) copy-start(f32[3,4]{1,0:T(4,128)} %param.16) | copy-start | bytes 148
  47.4 7.6 %copy-start.11 = (f32[4,384]{1,0:T(4,128)S(1)}, f32[4,384]{1,0:T(4,128)}, u32[]{:S(2)}) copy-start(f32[4,384]{1,0:T(4,128)} %param.15) | copy-start | bytes 18436
  48.8 9.5 %copy-start.14 = (f32[3,4]{1,0:T(4,128)S(1)}, f32[3,4]{1,0:T(4,128)}, u32[]{:S(2)}) copy-start(f32[3,4]{1,0:T(4,128)} %param.17) | copy-start | bytes 148
  48.9 10.2 %copy-start.58 = (s32[4]{0:T(128)S(1)}, s32[4]{0:T(128)}, u32[]{:S(2)}) copy-start(s32[4]{0:T(128)} %param.19) | copy-start | bytes 52
  48.9 11.0 %copy-start.59 = (f32[12]{0:T(128)S(1)}, f32[12]{0:T(128)}, u32[]{:S(2)}) copy-start(f32[12]{0:T(128)} %param.24) | copy-start | bytes 148
  50.0 12.6 %all-to-all-start = ((bf16[4,128,32,4]{1,3,0,2:T(4,128)(2,1)}), bf16[4,128,32,4]{1,3,0,2:T(4,128)(2,1)S(1)}, u32[]{:S(2)}, u32[]{:S(2)}) async-start(bf16[4,128,32,4]{1,3,0,2:T(4,128)(2,1)} %copy.226), calls=%async_computation | async-start | bytes 262144 | tf_op jit(solution)/shard_map/all_to_all | solution.py:211
  54.4 3.3 %copy-start.35 = (f32[4]{0:T(128)}, f32[4]{0:T(128)S(1)}, u32[]{:S(2)}) copy-start(f32[4]{0:T(128)S(1)} %multiply_reduce_fusion.11) | copy-start | bytes 52
  54.4 5.4 %copy-start.20 = (f32[4]{0:T(128)}, f32[4]{0:T(128)S(1)}, u32[]{:S(2)}) copy-start(f32[4]{0:T(128)S(1)} %get-tuple-element.131) | copy-start | bytes 52
  54.4 5.4 %copy-start.22 = (f32[4]{0:T(128)}, f32[4]{0:T(128)S(1)}, u32[]{:S(2)}) copy-start(f32[4]{0:T(128)S(1)} %get-tuple-element.132) | copy-start | bytes 52
  54.4 5.4 %copy-start.24 = (f32[4]{0:T(128)}, f32[4]{0:T(128)S(1)}, u32[]{:S(2)}) copy-start(f32[4]{0:T(128)S(1)} %get-tuple-element.133) | copy-start | bytes 52
  54.5 5.4 %copy-start.26 = (f32[4]{0:T(128)}, f32[4]{0:T(128)S(1)}, u32[]{:S(2)}) copy-start(f32[4]{0:T(128)S(1)} %get-tuple-element.134) | copy-start | bytes 52
  54.5 6.1 %copy-start.28 = (f32[4]{0:T(128)}, f32[4]{0:T(128)S(1)}, u32[]{:S(2)}) copy-start(f32[4]{0:T(128)S(1)} %get-tuple-element.135) | copy-start | bytes 52
  54.5 6.1 %copy-start.30 = (f32[4]{0:T(128)}, f32[4]{0:T(128)S(1)}, u32[]{:S(2)}) copy-start(f32[4]{0:T(128)S(1)} %get-tuple-element.136) | copy-start | bytes 52
  54.5 6.1 %copy-start.32 = (f32[4]{0:T(128)}, f32[4]{0:T(128)S(1)}, u32[]{:S(2)}) copy-start(f32[4]{0:T(128)S(1)} %get-tuple-element.137) | copy-start | bytes 52
  55.0 6.8 %copy-start.16 = (f32[4]{0:T(128)}, f32[4]{0:T(128)S(1)}, u32[]{:S(2)}) copy-start(f32[4]{0:T(128)S(1)} %get-tuple-element.138) | copy-start | bytes 52
  55.0 6.9 %copy-start.18 = (f32[4]{0:T(128)}, f32[4]{0:T(128)S(1)}, u32[]{:S(2)}) copy-start(f32[4]{0:T(128)S(1)} %get-tuple-element.139) | copy-start | bytes 52
  62.6 56.6 %all-to-all-start.1 = ((bf16[4,128,32,4]{1,3,0,2:T(4,128)(2,1)}), bf16[4,128,32,4]{1,3,0,2:T(4,128)(2,1)S(1)}, u32[]{:S(2)}, u32[]{:S(2)}) async-start(bf16[4,128,32,4]{1,3,0,2:T(4,128)(2,1)} %copy.229), calls=%async_computation.1 | async-start | bytes 262144 | tf_op jit(solution)/shard_map/all_to_all | solution.py:210
  120.3 17.1 %all-to-all-start.2 = ((f32[128,128,1,4]{1,3,2,0:T(4,128)}), f32[128,128,1,4]{1,3,2,0:T(4,128)}, u32[]{:S(2)}, u32[]{:S(2)}) async-start(f32[128,128,1,4]{1,3,2,0:T(4,128)} %copy.231), calls=%async_computation.2 | async-start | bytes 524288 | tf_op jit(solution)/shard_map/all_to_all | solution.py:214
  123.6 17.4 %copy-start.3 = (f32[4,128,128]{2,1,0:T(8,128)S(1)}, f32[4,128,128]{2,1,0:T(8,128)}, u32[]{:S(2)}) copy-start(f32[4,128,128]{2,1,0:T(8,128)} %param.14) | copy-start | bytes 786436
  140.0 3.1 %copy-start.6 = (f32[4,128,12]{1,2,0:T(8,128)S(1)}, f32[4,128,12]{1,2,0:T(8,128)}, u32[]{:S(2)}) copy-start(f32[4,128,12]{1,2,0:T(8,128)} %multiply_reduce_fusion.1) | copy-start | bytes 73732
  140.0 3.1 %copy-start.7 = (f32[4,12,16]{2,1,0:T(8,128)S(1)}, f32[4,12,16]{2,1,0:T(8,128)}, u32[]{:S(2)}) copy-start(f32[4,12,16]{2,1,0:T(8,128)} %reshape.2029) | copy-start | bytes 9220
  140.0 3.1 %copy-start.48 = (f32[12]{0:T(128)S(1)}, f32[12]{0:T(128)}, u32[]{:S(2)}) copy-start(f32[12]{0:T(128)} %get-tuple-element.159) | copy-start | bytes 148
  140.0 3.1 %copy-start.50 = (f32[12]{0:T(128)S(1)}, f32[12]{0:T(128)}, u32[]{:S(2)}) copy-start(f32[12]{0:T(128)} %get-tuple-element.160) | copy-start | bytes 148
  140.0 3.1 %copy-start.52 = (f32[128]{0:T(128)S(1)}, f32[128]{0:T(128)}, u32[]{:S(2)}) copy-start(f32[128]{0:T(128)} %add_multiply_fusion.18) | copy-start | bytes 1540
  140.0 3.1 %copy-start.54 = (pred[4,128]{1,0:T(4,128)(4,1)S(1)}, pred[4,128]{1,0:T(4,128)(4,1)}, u32[]{:S(2)}) copy-start(pred[4,128]{1,0:T(4,128)(4,1)} %broadcast_compare_fusion) | copy-start | bytes 1540
  140.0 3.1 %copy-start.56 = (f32[12]{0:T(128)S(1)}, f32[12]{0:T(128)}, u32[]{:S(2)}) copy-start(f32[12]{0:T(128)} %broadcast_multiply_fusion.6) | copy-start | bytes 148
  140.0 3.8 %copy-start.4 = (f32[128,288]{0,1:T(8,128)S(1)}, f32[128,288]{0,1:T(8,128)}, u32[]{:S(2)}) copy-start(f32[128,288]{0,1:T(8,128)} %copy.254) | copy-start | bytes 442372
  140.0 3.8 %copy-start.15 = (f32[3,4]{1,0:T(4,128)S(1)}, f32[3,4]{1,0:T(4,128)}, u32[]{:S(2)}) copy-start(f32[3,4]{1,0:T(4,128)} %param.17) | copy-start | bytes 148
  142.3 56.7 %copy-start.1 = (f32[4,128,128]{2,1,0:T(8,128)}, f32[4,128,128]{2,1,0:T(8,128)S(1)}, u32[]{:S(2)}) copy-start(f32[4,128,128]{2,1,0:T(8,128)S(1)} %get-tuple-element.164) | copy-start | bytes 786436
  142.3 5.0 %copy-start.12 = (f32[4,384]{1,0:T(4,128)S(1)}, f32[4,384]{1,0:T(4,128)}, u32[]{:S(2)}) copy-start(f32[4,384]{1,0:T(4,128)} %param.15) | copy-start | bytes 18436
  143.1 4.9 %copy-start.37 = (f32[384,6]{0,1:T(8,128)S(1)}, f32[384,6]{0,1:T(8,128)}, u32[]{:S(2)}) copy-start(f32[384,6]{0,1:T(8,128)} %param.27) | copy-start | bytes 27652
  143.2 5.2 %copy-start.2 = (bf16[384,1152]{1,0:T(8,128)(2,1)S(1)}, bf16[384,1152]{1,0:T(8,128)(2,1)}, u32[]{:S(2)}) copy-start(bf16[384,1152]{1,0:T(8,128)(2,1)} %param.22) | copy-start | bytes 2654212
  146.6 3.2 %copy-start.34 = (f32[3,4]{0,1:T(4,128)S(1)}, f32[3,4]{0,1:T(4,128)}, u32[]{:S(2)}) copy-start(f32[3,4]{0,1:T(4,128)} %copy.265) | copy-start | bytes 148
  146.6 3.1 %copy-start.17 = (f32[4]{0:T(128)S(1)}, f32[4]{0:T(128)}, u32[]{:S(2)}) copy-start(f32[4]{0:T(128)} %copy-done.16) | copy-start | bytes 52
  146.6 3.1 %copy-start.19 = (f32[4]{0:T(128)S(1)}, f32[4]{0:T(128)}, u32[]{:S(2)}) copy-start(f32[4]{0:T(128)} %copy-done.18) | copy-start | bytes 52
  146.6 3.1 %copy-start.21 = (f32[4]{0:T(128)S(1)}, f32[4]{0:T(128)}, u32[]{:S(2)}) copy-start(f32[4]{0:T(128)} %copy-done.20) | copy-start | bytes 52
  146.6 3.1 %copy-start.23 = (f32[4]{0:T(128)S(1)}, f32[4]{0:T(128)}, u32[]{:S(2)}) copy-start(f32[4]{0:T(128)} %copy-done.22) | copy-start | bytes 52
  146.6 3.1 %copy-start.25 = (f32[4]{0:T(128)S(1)}, f32[4]{0:T(128)}, u32[]{:S(2)}) copy-start(f32[4]{0:T(128)} %copy-done.24) | copy-start | bytes 52
  196.5 5.4 %copy-start.38 = (f32[1,4]{0,1:T(4,128)S(1)}, f32[1,4]{0,1:T(4,128)}, u32[]{:S(2)}) copy-start(f32[1,4]{0,1:T(4,128)} %get-tuple-element.86) | copy-start | bytes 52
  196.5 5.4 %copy-start.39 = (f32[1,4]{0,1:T(4,128)S(1)}, f32[1,4]{0,1:T(4,128)}, u32[]{:S(2)}) copy-start(f32[1,4]{0,1:T(4,128)} %get-tuple-element.87) | copy-start | bytes 52
  196.5 5.3 %copy-start.40 = (f32[1,4]{0,1:T(4,128)S(1)}, f32[1,4]{0,1:T(4,128)}, u32[]{:S(2)}) copy-start(f32[1,4]{0,1:T(4,128)} %get-tuple-element.118) | copy-start | bytes 52
  196.5 5.5 %copy-start.42 = (f32[1,4]{0,1:T(4,128)S(1)}, f32[1,4]{0,1:T(4,128)}, u32[]{:S(2)}) copy-start(f32[1,4]{0,1:T(4,128)} %get-tuple-element.85) | copy-start | bytes 52
  196.5 5.5 %copy-start.43 = (f32[1,4]{0,1:T(4,128)S(1)}, f32[1,4]{0,1:T(4,128)}, u32[]{:S(2)}) copy-start(f32[1,4]{0,1:T(4,128)} %get-tuple-element.88) | copy-start | bytes 52
  196.5 5.5 %copy-start.44 = (f32[1,4]{0,1:T(4,128)S(1)}, f32[1,4]{0,1:T(4,128)}, u32[]{:S(2)}) copy-start(f32[1,4]{0,1:T(4,128)} %get-tuple-element.89) | copy-start | bytes 52
  196.6 5.5 %copy-start.45 = (f32[1,4]{0,1:T(4,128)S(1)}, f32[1,4]{0,1:T(4,128)}, u32[]{:S(2)}) copy-start(f32[1,4]{0,1:T(4,128)} %get-tuple-element.90) | copy-start | bytes 52
  196.6 5.5 %copy-start.46 = (f32[1,4]{0,1:T(4,128)S(1)}, f32[1,4]{0,1:T(4,128)}, u32[]{:S(2)}) copy-start(f32[1,4]{0,1:T(4,128)} %get-tuple-element.116) | copy-start | bytes 52
  196.6 5.5 %copy-start.47 = (f32[1,4]{0,1:T(4,128)S(1)}, f32[1,4]{0,1:T(4,128)}, u32[]{:S(2)}) copy-start(f32[1,4]{0,1:T(4,128)} %get-tuple-element.117) | copy-start | bytes 52
  (15 other events, 38.2 us)
where the time goes:
time: 204 us; the launch traced here: 203 us
  blocking collectives  131 us (64%)
  local copies, waits for them, and re-layouts  31.7 us (16%)
  other arithmetic  14 us (7%)
  starting transfers between devices  13 us (6%)
  matrix products  11 us (5%)
    all_gather x2, blocking collectives, local(): key_all = lax.all_gather(key_rows, 'row', axis=0, tiled=True)  88.8 us
    unnamed x1, blocking collectives  42 us
    unnamed x139, local copies, waits for them, and re-layouts  9.32 us
    all_to_all x1, starting transfers between devices, local(): lax.all_to_all(left_blocks, 'row', split_axis=2, concat_axis=0, tiled=True)  5.32 us
    all_to_all x1, starting transfers between devices, local(): lax.all_to_all(right_blocks, 'row', split_axis=2, concat_axis=0, tiled=True)  4.4 us
  transfers between devices with their start and end apart: 3, of which 1 were waited for; matrix products, arithmetic and copies ran while one was open for 13% of the time, Pallas kernels for 0%

commit v1 on v0

v1 whole, which is shorter than its diff:
```python
import functools
import math

import jax
import jax.numpy as jnp
from jax import lax
from jax.experimental import pallas as pl
from jax.experimental.pallas import tpu as pltpu
from jax.sharding import PartitionSpec as P

CH = 128
CS = 384
H = 12
HP = 16
CHEAD = 16
PQ = 4
PV = 8
SLOT = 512
IP = 8
MASK_AT = 12
CHAIN_AT = 13

f32 = jnp.float32
bf16 = jnp.bfloat16
highest = lax.Precision.HIGHEST
epsilon = 1e-05
mask_fill = 100000.0
third = math.sqrt(1.0 / 3.0)


def layer_norm(values, axis=-1):
    center = values - jnp.mean(values, axis=axis, keepdims=True)
    spread = jnp.mean(center * center, axis=axis, keepdims=True)
    return center * lax.rsqrt(spread + epsilon)


def quat_entries(one, two, three, real):
    return [
        1.0 - 2.0 * (two * two + three * three),
        2.0 * (one * two - real * three),
        2.0 * (one * three + real * two),
        2.0 * (one * two + real * three),
        1.0 - 2.0 * (one * one + three * three),
        2.0 * (two * three - real * one),
        2.0 * (one * three - real * two),
        2.0 * (two * three + real * one),
        1.0 - 2.0 * (one * one + two * two),
    ]


def dot(a, b, precision=None):
    return lax.dot_general(
        a, b, (((1,), (0,)), ((), ())), precision=precision, preferred_element_type=f32
    )


def dot_nt(a, b, precision=None):
    return lax.dot_general(
        a, b, (((1,), (1,)), ((), ())), precision=precision, preferred_element_type=f32
    )


def dot_tn(a, b):
    return lax.dot_general(a, b, (((0,), (0,)), ((), ())), preferred_element_type=f32)


def log2(number):
    assert number & (number - 1) == 0
    return number.bit_length() - 1


def grid_of(shape):
    return lax.broadcasted_iota(jnp.int32, shape, 0), lax.broadcasted_iota(jnp.int32, shape, 1)


def onehot(match):
    return jnp.where(match, 1.0, 0.0).astype(bf16)


def swap_rows(count, minor_count):
    row, column = grid_of((count, count))
    major_count = count // minor_count
    minor = row >> log2(major_count)
    major = row & (major_count - 1)
    return onehot(column == major * minor_count + minor)


def spread_rows(slots, w, r):
    rows = 2 * w
    lanes = r * SLOT // rows
    x, i = grid_of((16, 16))
    q = x & (rows - 1)
    if lanes <= SLOT:
        total = None
        for t in range(SLOT // lanes):
            one = dot(onehot((q == t * r + i) & (i < r)), slots[:, t * lanes : (t + 1) * lanes])
            total = one if total is None else total + one
        return total.astype(bf16)
    return jnp.concatenate(
        [dot(onehot(i == t * rows + q), slots) for t in range(lanes // SLOT)], axis=1
    ).astype(bf16)


def natural_rows(x_ref, first, w, r, n, start=0, stop=SLOT):
    rows = 2 * w
    lanes = r * SLOT // rows
    count = n * r
    j, x = grid_of((count, n * rows))
    s = x >> log2(rows)
    q = x & (rows - 1)
    if lanes <= SLOT:
        pieces = []
        for t in range(SLOT // lanes):
            low, high = max(start, t * lanes), min(stop, (t + 1) * lanes)
            if low < high:
                values = x_ref[:, first + low - t * lanes : first + high - t * lanes]
                pieces.append(dot(onehot((j == s * r + q - t * r) & ((q >> log2(r)) == t)), values))
        return (pieces[0] if len(pieces) == 1 else jnp.concatenate(pieces, axis=1)).astype(bf16)
    total = None
    for t in range(lanes // SLOT):
        values = x_ref[:, first + t * SLOT + start : first + t * SLOT + stop]
        one = dot(onehot(j == s * r + t * rows + q), values)
        total = one if total is None else total + one
    return total.astype(bf16)


def frame_pieces(frame):
    high = frame.astype(bf16).astype(f32)
    rest = frame - high
    middle = rest.astype(bf16).astype(f32)
    low = (rest - middle).astype(bf16).astype(f32)
    return high + pltpu.roll(middle, 32, 1) + pltpu.roll(low, 64, 1)


def slots_of(state, frame):
    both = jnp.concatenate([state, frame_pieces(frame)], axis=1)
    return jnp.concatenate([both, jnp.zeros_like(both)], axis=0).astype(bf16)


def fill_rows(out_ref, first, tile):
    lanes = tile.shape[1]
    for t in range(out_ref.shape[0] // 16):
        out_ref[t * 16 : (t + 1) * 16, first : first + lanes] = tile


def piece_select(row_count, transposed=False):
    if transposed:
        lane, entry = grid_of((128, row_count))
    else:
        entry, lane = grid_of((row_count, 128))
    return onehot(((lane & 31) == entry) & (lane < 96))


def gate_kernel(
    w, n, pair_ref, tri_ref, single_ref, quats_ref, translate_ref, mask_ref, chain_ref, send_ref, frame_ref, scr
):
    r, count, _ = pair_ref.shape
    scr[...] = jnp.zeros_like(scr)
    quats = quats_ref[...]
    real = lax.rsqrt(1.0 + jnp.sum(quats * quats, axis=0, keepdims=True))
    unit = quats * real
    entries = quat_entries(unit[0:1], unit[1:2], unit[2:3], real)
    for at, entry in enumerate(entries):
        scr[at : at + 1, 0:r] = entry
    scr[9:12, 0:r] = translate_ref[...]
    frame = scr[...].T[0:IP, :]
    row, lane = grid_of((IP, 128))
    for i in range(r):
        frame = jnp.where((row == i) & (lane == MASK_AT), mask_ref[i].astype(f32), frame)
        frame = jnp.where((row == i) & (lane == CHAIN_AT), chain_ref[i].astype(f32), frame)
    frame_ref[...] = frame
    state = jnp.concatenate([single_ref[...], jnp.zeros((IP - r, CS), f32)], axis=0)
    fill_rows(send_ref, r * count, spread_rows(slots_of(state, frame), w, r))

    row, column = grid_of((2 * CH, 2 * CH))
    d = row >> log2(2 * w)
    side = (row >> log2(w)) & 1
    take = onehot(column == side * CH + d * w + (row & (w - 1)))
    gate_weight = jnp.concatenate([tri_ref[:, 0:CH], tri_ref[:, 2 * CH : 3 * CH]], axis=1)
    value_weight = jnp.concatenate([tri_ref[:, CH : 2 * CH], tri_ref[:, 3 * CH : 4 * CH]], axis=1)
    gate_weight = dot_nt(take, gate_weight).astype(bf16)
    value_weight = dot_nt(take, value_weight).astype(bf16)
    for i in range(r):
        normed = layer_norm(pair_ref[i]).astype(bf16)
        gates = dot_nt(gate_weight, normed)
        values = dot_nt(value_weight, normed)
        side_values = jax.nn.sigmoid(gates) * values * mask_ref[i].astype(f32)
        send_ref[:, i * count : (i + 1) * count] = side_values.astype(bf16)


def product_kernel(w, n, r, recv_ref, send_ref):
    count = n * r
    rows = 2 * w
    pieces = natural_rows(recv_ref, r * count, w, r, n, CS, SLOT)
    mask = dot_nt(piece_select(16), pieces)[MASK_AT : MASK_AT + 1, :]
    mask = jnp.concatenate([mask] * r, axis=1)
    order = swap_rows(n * rows, rows)
    sides = (dot(order, recv_ref[:, 0 : r * count]) * mask).astype(bf16)
    row, column = grid_of((count, count))
    to_natural = onehot(row == (column & (n - 1)) * r + (column >> log2(n)))

    def stacked(block):
        part = sides[block * n : (block + 1) * n]
        return jnp.concatenate([part[:, i * count : (i + 1) * count] for i in range(r)], axis=0)

    half = r // 2
    products = []
    for c in range(w):
        right = dot(to_natural, stacked(w + c)).astype(bf16)
        products.append(dot_nt(stacked(c), right).astype(bf16))
    blocks = []
    for high in range(2):
        for c in range(w):
            first = high * half
            blocks.append(
                jnp.concatenate(
                    [products[c][(first + low) * n : (first + low + 1) * n] for low in range(half)], axis=1
                )
            )
    send_ref[...] = dot(swap_rows(n * rows, n), jnp.concatenate(blocks, axis=0)).astype(bf16)


def head_masks():
    h, lane = grid_of((HP, 256))
    scalar = jnp.where((lane >> log2(CHEAD)) == h, 1.0, 0.0)
    scalar = jnp.where(h < H, scalar, 0.0)
    h, lane = grid_of((HP, 128))
    query = jnp.where(((lane >> log2(PQ)) == h) & (h < H), 1.0, 0.0)
    value = jnp.where(((lane >> log2(PV)) == h) & (h < H), 1.0, 0.0)
    return scalar, query, value


def logits_and_values(r, slots, state, frame, chain_ref, key_weight, query_weight, columns):
    pieces = slots[:, CS:SLOT]
    entry = dot(pieces, piece_select(128, True))
    rows = dot_nt(piece_select(16), pieces)
    keys = dot(slots[:, 0:CS], key_weight)
    local = [keys[:, 512 + 256 * a : 768 + 256 * a] for a in range(3)]
    placed = []
    for a in range(3):
        placed.append(
            entry[:, 3 * a : 3 * a + 1] * local[0]
            + entry[:, 3 * a + 1 : 3 * a + 2] * local[1]
            + entry[:, 3 * a + 2 : 3 * a + 3] * local[2]
            + entry[:, 9 + a : 10 + a]
        )
    values = jnp.concatenate([keys[:, 256:512]] + [p[:, 0:128] for p in placed], axis=1)
    key_points = [p[:, 128:256] for p in placed]
    key_side = jnp.concatenate([keys[:, 0:256]] + key_points + [p * p for p in key_points], axis=1)

    both = jnp.concatenate([state, jnp.zeros_like(state)], axis=0).astype(bf16)
    own = dot(both, query_weight)[0:IP]
    own_local = [own[:, 256 + 128 * a : 384 + 128 * a] for a in range(3)]
    own_points = []
    for a in range(3):
        own_points.append(
            frame[:, 3 * a : 3 * a + 1] * own_local[0]
            + frame[:, 3 * a + 1 : 3 * a + 2] * own_local[1]
            + frame[:, 3 * a + 2 : 3 * a + 3] * own_local[2]
            + frame[:, 9 + a : 10 + a]
        )
    scalar_mask, query_mask, _ = head_masks()
    weight = columns[:, 0:1]
    query_rows = []
    constants = []
    for i in range(r):
        scalar = own[i : i + 1, 0:256] * (third / math.sqrt(CHEAD)) * scalar_mask
        points = [p[i : i + 1] * query_mask for p in own_points]
        query_rows.append(
            jnp.concatenate(
                [scalar] + [2.0 * weight * p for p in points] + [-weight * query_mask] * 3, axis=1
            )
        )
        length = points[0] * points[0] + points[1] * points[1] + points[2] * points[2]
        own_chain = chain_ref[i].astype(f32)
        same = rows[CHAIN_AT : CHAIN_AT + 1, :] == own_chain
        constants.append(
            jnp.where(same, columns[:, 2:3], columns[:, 1:2])
            + mask_fill * (rows[MASK_AT : MASK_AT + 1, :] - 1.0)
            - weight * jnp.sum(length, axis=1, keepdims=True)
        )
    logits = dot_nt(jnp.concatenate(query_rows, axis=0), key_side, highest)
    return logits + jnp.concatenate(constants, axis=0), values


def attend(r, logits, values, pair_half, state, frame, out_weight, frame_weight):
    top = jnp.max(logits, axis=1, keepdims=True)
    raised = jnp.exp(logits - top)
    attention = raised / jnp.sum(raised, axis=1, keepdims=True)
    summed = dot(attention, values, highest)
    scalar_mask, _, value_mask = head_masks()
    masks = jnp.concatenate([scalar_mask, value_mask, value_mask, value_mask], axis=1)
    summed = summed * jnp.concatenate([masks] * r, axis=0)
    row, column = grid_of((IP, r * HP))
    gathered = dot(jnp.where((column >> log2(HP)) == row, 1.0, 0.0), summed, highest)
    relative = [
        gathered[:, 256 + 128 * a : 256 + 128 * a + H * PV] - frame[:, 9 + a : 10 + a] for a in range(3)
    ]
    out_local = [
        frame[:, a : a + 1] * relative[0]
        + frame[:, 3 + a : 4 + a] * relative[1]
        + frame[:, 6 + a : 7 + a] * relative[2]
        for a in range(3)
    ]
    out_norm = jnp.sqrt(
        out_local[0] * out_local[0] + out_local[1] * out_local[1] + out_local[2] * out_local[2] + 1e-08
    )
    half = attention.astype(bf16)
    out_pair = jnp.concatenate(
        [dot(half[i * HP : (i + 1) * HP], pair_half[i]) for i in range(r)], axis=0
    ).astype(bf16)
    row, column = grid_of((H * IP, r * HP))
    by_head = dot(onehot(column == (row & (IP - 1)) * HP + (row >> log2(IP))), out_pair)
    combined = jnp.concatenate(
        [gathered[:, 0 : H * CHEAD]]
        + out_local
        + [out_norm]
        + [by_head[h * IP : (h + 1) * IP] for h in range(H)],
        axis=1,
    )
    combined = jnp.concatenate([combined, jnp.zeros_like(combined)], axis=0).astype(bf16)
    state = layer_norm(state + dot(combined, out_weight)[0:IP])
    update = dot(state, frame_weight, highest)
    quat = [update[:, a : a + 1] for a in range(3)]
    real = lax.rsqrt(1.0 + (quat[0] * quat[0] + quat[1] * quat[1] + quat[2] * quat[2]))
    step = quat_entries(quat[0] * real, quat[1] * real, quat[2] * real, real)
    old = [frame[:, e : e + 1] for e in range(9)]
    columns = []
    for target in range(3):
        for column in range(3):
            columns.append(
                old[target * 3] * step[column]
                + old[target * 3 + 1] * step[3 + column]
                + old[target * 3 + 2] * step[6 + column]
            )
    for target in range(3):
        columns.append(
            frame[:, 9 + target : 10 + target]
            + old[target * 3] * update[:, 3:4]
            + old[target * 3 + 1] * update[:, 4:5]
            + old[target * 3 + 2] * update[:, 5:6]
        )
    _, lane = grid_of((IP, 128))
    for at, column in enumerate(columns):
        frame = jnp.where(lane == at, column, frame)
    return state, frame


def pad_state(single_ref):
    r = single_ref.shape[0]
    return jnp.concatenate([single_ref[...], jnp.zeros((IP - r, CS), f32)], axis=0)


def prepare_kernel(
    w, n, recv_ref, pair_ref, gate_weight_ref, single_ref, frame_ref, chain_ref, key_ref, query_ref, columns_ref,
    gate_ref, logits_ref, values_ref,
):
    r, count, _ = pair_ref.shape
    slots = natural_rows(recv_ref, r * count, w, r, n)
    logits, values = logits_and_values(
        r, slots, pad_state(single_ref), frame_ref[...], chain_ref, key_ref[...], query_ref[...], columns_ref[...]
    )
    logits_ref[...] = logits
    values_ref[...] = values
    for i in range(r):
        normed = layer_norm(pair_ref[i]).astype(bf16)
        gate_ref[i] = jax.nn.sigmoid(dot(normed, gate_weight_ref[...]))


def update_kernel(
    w, n, recv_ref, pair_ref, gate_ref, logits_ref, values_ref, tri_out_ref, bias_weight_ref, single_ref, frame_ref,
    out_weight_ref, frame_weight_ref, pair_out_ref, half_ref, bias_ref, state_ref, new_frame_ref, send_ref,
):
    r, count, _ = pair_ref.shape
    half = r // 2
    row, column = grid_of((2 * CH, 2 * CH))
    c = row & (CH - 1)
    take = onehot(column == (c >> log2(w)) * 2 * w + (row >> log2(CH)) * w + (c & (w - 1)))
    product = dot(take, recv_ref[...])
    biases = []
    halves = []
    for high in range(2):
        normed = layer_norm(product[high * CH : (high + 1) * CH], axis=0).astype(bf16)
        update = dot_tn(normed, tri_out_ref[...])
        for low in range(half):
            i = high * half + low
            pair_out = pair_ref[i] + gate_ref[i] * update[low * count : (low + 1) * count]
            pair_out_ref[i] = pair_out
            normed_pair = layer_norm(pair_out)
            biases.append(dot_nt(bias_weight_ref[...], normed_pair, highest) * third)
            halves.append(normed_pair.astype(bf16))
            half_ref[i] = halves[-1]
    bias = jnp.concatenate(biases, axis=0)
    bias_ref[...] = bias
    state, frame = attend(
        r, logits_ref[...] + bias, values_ref[...], halves, pad_state(single_ref), frame_ref[...],
        out_weight_ref[...], frame_weight_ref[...],
    )
    state_ref[...] = state
    new_frame_ref[...] = frame
    fill_rows(send_ref, 0, spread_rows(slots_of(state, frame), w, r))


def last_kernel(
    w, n, recv_ref, half_ref, bias_ref, state_ref, frame_ref, chain_ref, key_ref, query_ref, columns_ref,
    out_weight_ref, frame_weight_ref, single_out_ref, rotation_ref, translation_ref, scr,
):
    r = half_ref.shape[0]
    slots = natural_rows(recv_ref, 0, w, r, n)
    state, frame = state_ref[...], frame_ref[...]
    logits, values = logits_and_values(
        r, slots, state, frame, chain_ref, key_ref[...], query_ref[...], columns_ref[...]
    )
    state, frame = attend(
        r, logits + bias_ref[...], values, [half_ref[i] for i in range(r)], state, frame,
        out_weight_ref[...], frame_weight_ref[...],
    )
    single_out_ref[...] = state[0:r]
    scr[...] = jnp.concatenate([frame, jnp.zeros((128 - IP, 128), f32)], axis=0).T
    rotation_ref[...] = scr[0:9, 0:r]
    translation_ref[...] = scr[9:12, 0:r]


VMEM = pl.BlockSpec(memory_space=pltpu.VMEM)
SMEM = pl.BlockSpec(memory_space=pltpu.SMEM)


def call(body, name, outs, args, small=(), scratch=(), limit=32, flops=0, moved=0):
    return pl.pallas_call(
        body,
        name=name,
        out_shape=[jax.ShapeDtypeStruct(s, d) for s, d in outs],
        in_specs=[SMEM if at in small else VMEM for at in range(len(args))],
        out_specs=[VMEM] * len(outs),
        scratch_shapes=list(scratch),
        compiler_params=pltpu.CompilerParams(vmem_limit_bytes=limit * 2**20),
        cost_estimate=pl.CostEstimate(flops=flops, bytes_accessed=moved, transcendentals=0),
    )(*args)


def pad_lanes(block, width):
    return jnp.pad(block, ((0, 0), (0, width - block.shape[1])))


def local(
    pair, single, quats, translate, res_mask, chain_ids, tri_weight, tri_out_weight, qkv_weight, bias_weight,
    head_gamma, chain_bias, out_weight, frame_weight,
):
    n = lax.axis_size("row")
    r, count, _ = pair.shape
    w = CH // n
    rows = 2 * w
    lanes = r * SLOT // rows
    scale = count // 128
    limit = 24 if scale == 1 else 56

    def exchange(sent):
        width = sent.shape[1]
        got = lax.all_to_all(sent.reshape(n, rows, width), "row", 0, 0, tiled=True)
        return got.reshape(n * rows, width)

    sent, frame = call(
        functools.partial(gate_kernel, w, n),
        "gate",
        [((n * rows, r * count + lanes), bf16), ((IP, 128), f32)],
        [pair, tri_weight, single, quats, translate, res_mask, chain_ids],
        small=(5, 6),
        scratch=[pltpu.VMEM((128, 128), f32)],
        limit=limit,
    )
    received = exchange(sent)

    width = H * CHEAD
    start = 3 * width
    query_points = qkv_weight[:, start : start + 3 * H * PQ]
    key_points = qkv_weight[:, start + 3 * H * PQ : start + 6 * H * PQ]
    value_points = qkv_weight[:, start + 6 * H * PQ :]
    key_weight = [pad_lanes(qkv_weight[:, width : 2 * width], 256), pad_lanes(qkv_weight[:, 2 * width : start], 256)]
    query_weight = [pad_lanes(qkv_weight[:, :width], 256)]
    for a in range(3):
        key_weight.append(pad_lanes(value_points[:, a * H * PV : (a + 1) * H * PV], 128))
        key_weight.append(pad_lanes(key_points[:, a * H * PQ : (a + 1) * H * PQ], 128))
        query_weight.append(pad_lanes(query_points[:, a * H * PQ : (a + 1) * H * PQ], 128))
    key_weight = jnp.concatenate(key_weight, axis=1)
    query_weight = jnp.concatenate(query_weight, axis=1)
    point_weight = head_gamma * (math.sqrt(2.0 / (9.0 * PQ)) * 0.5 * third)
    columns = jnp.stack([point_weight, chain_bias[0], chain_bias[1]], axis=1)
    columns = jnp.pad(columns, ((0, HP - H), (0, 125)))
    bias_rows = jnp.pad(bias_weight.T, ((0, HP - H), (0, 0)))
    gate_weight = tri_weight[:, 4 * CH :]

    (formed,) = call(
        functools.partial(product_kernel, w, n, r),
        "product",
        [((n * rows, (r // 2) * count), bf16)],
        [received],
        limit=limit,
    )
    products = exchange(formed)
    gate, logits, values = call(
        functools.partial(prepare_kernel, w, n),
        "prepare",
        [((r, count, CH), f32), ((r * HP, count), f32), ((count, 640), f32)],
        [received, pair, gate_weight, single, frame, chain_ids, key_weight, query_weight, columns],
        small=(5,),
        limit=limit,
        flops=2 * count * CS * 1280,
        moved=8 * 2**20,
    )
    pair_out, pair_half, bias, state, frame, sent = call(
        functools.partial(update_kernel, w, n),
        "update",
        [
            ((r, count, CH), f32),
            ((r, count, CH), bf16),
            ((r * HP, count), f32),
            ((IP, CS), f32),
            ((IP, 128), f32),
            ((n * rows, lanes), bf16),
        ],
        [products, pair, gate, logits, values, tri_out_weight, bias_rows, single, frame, out_weight, frame_weight],
        limit=limit,
    )
    received = exchange(sent)
    single_out, rotation, translation = call(
        functools.partial(last_kernel, w, n),
        "last",
        [((r, CS), f32), ((9, r), f32), ((3, r), f32)],
        [received, pair_half, bias, state, frame, chain_ids, key_weight, query_weight, columns, out_weight, frame_weight],
        small=(5,),
        scratch=[pltpu.VMEM((128, 128), f32)],
        limit=limit,
    )
    return (pair_out, single_out, rotation, translation)


def solution(mesh):
    rows = ("grp", "row")
    placed = (P(rows, None, None), P(rows, None), P(None, rows), P(None, rows), P(rows), P(rows)) + (P(),) * 8
    return jax.shard_map(
        local,
        mesh=mesh,
        in_specs=placed,
        out_specs=(P(rows, None, None), P(rows, None), P(None, rows), P(None, rows)),
        check_vma=False,
    )
```

time: 204 us -> 71.1 us (0.35)
  blocking collectives: 131 us -> 13.7 us
  Pallas kernels: 0 us -> 14.8 us
  local copies, waits for them, and re-layouts: 31.7 us -> 17.4 us
  other arithmetic: 14 us -> 1.97 us
  matrix products: 11 us -> 0 us
  waiting for transfers between devices: 0.53 us -> 10.9 us
  starting transfers between devices: 13 us -> 10.6 us
    all_gather x2 -> x0, blocking collectives: 88.8 us -> none  [local(): key_all = lax.all_gather(key_rows, 'row', axis=0, tiled=True)]
    unnamed x1 -> x0, blocking collectives: 42 us -> none
    pallas_call x0 -> x5, Pallas kernels: none -> 14.8 us  [call(): pl.pallas_call(body, name=name, out_shape=[jax.ShapeDtypeStruct(s, d) for...]
    all_to_all x0 -> x1, blocking collectives: none -> 13.7 us  [exchange(): got = lax.all_to_all(sent.reshape(n, rows, width), 'row', 0, 0, tiled=True)]
    dot_general x18 -> x0, matrix products: 11 us -> none  [the longest x2 2.96 us: attend(): jnp.einsum('hij,jahv->iahv', attention, value_global, precision=highest)]
    all_to_all x3 -> x2, waiting for transfers between devices: 0.53 us -> 10.9 us  [exchange(): got = lax.all_to_all(sent.reshape(n, rows, width), 'row', 0, 0, tiled=True)]
    slice x26 -> x4, local copies, waits for them, and re-layouts: 10.5 us -> 1.94 us  [the longest x1 0.91 us: local(): query_points[:, a * H * PQ:(a + 1) * H * PQ]]
    reduce_sum x16 -> x0, other arithmetic: 6.54 us -> none  [the longest x2 2 us: attend(): jnp.sum(difference * difference, axis=(2, 4))]
  transfers between devices with their start and end apart: 3 -> 2, of which waited for: 1 -> 2; matrix products, arithmetic and copies ran while one was open for 13% -> 7% of each run, Pallas kernels for 0% -> 3%
where the time goes in v1:
time: 71.1 us; the launch traced here: 70.3 us
  local copies, waits for them, and re-layouts  17.4 us (24%)
  Pallas kernels  14.8 us (21%)
  blocking collectives  13.7 us (19%)
  waiting for transfers between devices  10.9 us (15%)
  starting transfers between devices  10.6 us (15%)
  other arithmetic  1.97 us (3%)
  between operations  0.85 us (1%)
    unnamed x61, local copies, waits for them, and re-layouts  15.3 us
    pallas_call x5, Pallas kernels, call(): pl.pallas_call(body, name=name, out_shape=[jax.ShapeDtypeStruct(s, d) for...  14.8 us
    all_to_all x1, blocking collectives, exchange(): got = lax.all_to_all(sent.reshape(n, rows, width), 'row', 0, 0, tiled=True)  13.7 us
    all_to_all x2, waiting for transfers between devices, exchange(): got = lax.all_to_all(sent.reshape(n, rows, width), 'row', 0, 0, tiled=True)  10.9 us
    all_to_all x2, starting transfers between devices, exchange(): got = lax.all_to_all(sent.reshape(n, rows, width), 'row', 0, 0, tiled=True)  10.6 us
  transfers between devices with their start and end apart: 2, of which 2 were waited for; matrix products, arithmetic and copies ran while one was open for 7% of the time, Pallas kernels for 3%

profile of v1, /device:TPU:0, one launch (start us, length us, event | category | flops | bytes accessed | tf_op | source)
XLA Modules:
  0.0 70.3 jit_solution(13457685034658228373)
XLA Ops:
  0.6 0.0 copy-start.1
  0.6 0.9 %copy-done.1 = f32[4,128,128]{2,1,0:T(8,128)S(1)} copy-done((f32[4,128,128]{2,1,0:T(8,128)S(1)}, f32[4,128,128]{2,1,0:T(8,128)}, u32[]{:S(2)}) %copy-start.1) | copy-done | bytes 262168
  1.6 0.9 %copy-done.9 = bf16[128,640]{1,0:T(8,128)(2,1)S(1)} copy-done((bf16[128,640]{1,0:T(8,128)(2,1)S(1)}, bf16[128,640]{1,0:T(8,128)(2,1)}, u32[]{:S(2)}) %copy-start.9) | copy-done | bytes 163864
  2.5 0.7 copy-done.10
  3.2 0.7 copy-done.15
  3.9 0.7 copy-done.17
  4.5 0.7 copy-done.18
  5.2 0.7 copy-done.19
  5.9 2.0 %gate.1 = (bf16[256,768]{1,0:T(8,128)(2,1)}, f32[8,128]{1,0:T(8,128)S(1)}) custom-call(f32[4,128,128]{2,1,0:T(8,128)S(1)} %copy-done.1, bf16[128,640]{1,0:T(8,128)(2,1)S(1)} %copy-done.9, f32[4,384]{1,0:T(4,128)S(1)} %copy-done.10, f32[3,4]{1,0:T(4,128)S(1)} %copy-done.17, f32[3,4]{1,0:T(4,128)S(1)} %copy-done.18, s32[4]{0:T(128)S(1)} %copy-done.19, ...), custom_call_target="tpu_custom_call" | custom-call | tf_op jit(solution)/shard_map/gate/pallas_call | solution.py:429
  7.9 7.3 %all-to-all-start = ((bf16[32,8,768]{2,1,0:T(8,128)(2,1)}), bf16[32,8,768]{2,1,0:T(8,128)(2,1)S(1)}, u32[]{:S(2)}, u32[]{:S(2)}) async-start(bf16[32,8,768]{2,1,0:T(8,128)(2,1)} %bitcast), calls=%async_computation | async-start | bytes 786432 | tf_op jit(solution)/shard_map/all_to_all | solution.py:459
  15.2 0.0 copy-done.20
  15.2 0.9 %fusion.8 = (bf16[384,48]{1,0:T(8,128)(2,1)}, bf16[384,48]{1,0:T(8,128)(2,1)S(1)}, bf16[384,48]{1,0:T(8,128)(2,1)S(1)}, bf16[384,48]{1,0:T(8,128)(2,1)S(1)}, bf1...) fusion(bf16[384,1152]{1,0:T(8,128)(2,1)S(1)} %copy-done.20), kind=kLoop, calls=%fused_computation.26 | loop fusion | bytes 442368 | tf_op jit(solution)/shard_map/slice | solution.py:483
  16.1 0.1 fusion.10
  16.3 0.1 fusion.9
  16.4 0.0 copy-start.21
  16.4 0.0 copy-start.22
  16.6 0.0 copy-start.11
  16.6 0.0 copy-start.16
  16.8 0.0 copy-done.25
  16.8 0.0 copy-done.23
  16.8 0.0 copy-done.24
  16.8 0.7 slice_select_fusion
  17.5 10.9 %all-to-all-done = bf16[32,8,768]{2,1,0:T(8,128)(2,1)S(1)} async-done(((bf16[32,8,768]{2,1,0:T(8,128)(2,1)}), bf16[32,8,768]{2,1,0:T(8,128)(2,1)S(1)}, u32[]{:S(2)}, u32[]{:S(2)}) %all-to-all-start) | async-done | bytes 393248 | tf_op jit(solution)/shard_map/all_to_all | solution.py:459
  28.4 1.7 %product.1 = bf16[256,256]{1,0:T(8,128)(2,1)} custom-call(bf16[256,768]{1,0:T(8,128)(2,1)S(1)} %bitcast.13), custom_call_target="tpu_custom_call" | custom-call | tf_op jit(solution)/shard_map/product/pallas_call | solution.py:429
  30.0 3.3 %all-to-all-start.1 = ((bf16[32,8,256]{2,1,0:T(8,128)(2,1)}), bf16[32,8,256]{2,1,0:T(8,128)(2,1)}, u32[]{:S(2)}, u32[]{:S(2)}) async-start(bf16[32,8,256]{2,1,0:T(8,128)(2,1)} %bitcast.2), calls=%async_computation.1 | async-start | bytes 262144 | tf_op jit(solution)/shard_map/all_to_all | solution.py:459
  33.3 0.8 %slice.58.gate_weight_ref = bf16[128,128]{1,0:T(8,128)(2,1)S(1)} slice(bf16[128,640]{1,0:T(8,128)(2,1)} %tri_ref.1), slice={[0:128], [512:640]} | slice | bytes 65536 | tf_op jit(solution)/shard_map/slice | solution.py:490
  34.1 0.1 copy.24
  34.2 0.0 copy-done.21
  34.2 0.8 %copy.25.frame_weight_ref = f32[384,6]{1,0:T(8,128)} copy(f32[384,6]{0,1:T(8,128)S(1)} %copy-done.21) | data formatting | bytes 18432 | tf_op args[13]
  35.1 0.0 copy-start
  35.1 1.3 %fusion.6.query_ref = bf16[384,640]{1,0:T(8,128)(2,1)S(1)} fusion(bf16[384,48]{1,0:T(8,128)(2,1)} %get-tuple-element.44, bf16[384,48]{1,0:T(8,128)(2,1)} %get-tuple-element.45, bf16[384,48]{1,0:T(8,128)(2,1)} %get-tuple-element.40, bf16[384,256]{1,0:T(8,128)(2,1)} %slice_select_fusion), kind=kLoop, calls=%fused_computation.11 | loop fusion | flops 4423680 | bytes 798720 | tf_op jit(solution)/shard_map/concatenate | solution.py:485
  36.4 0.0 copy-start.2
  36.4 0.9 %copy-done.2 = f32[4,128,128]{2,1,0:T(8,128)S(1)} copy-done((f32[4,128,128]{2,1,0:T(8,128)S(1)}, f32[4,128,128]{2,1,0:T(8,128)}, u32[]{:S(2)}) %copy-start.2) | copy-done | bytes 262168
  37.3 2.1 %prepare.1 = (f32[4,128,128]{2,1,0:T(8,128)S(1)}, f32[64,128]{1,0:T(8,128)S(1)}, f32[128,640]{1,0:T(8,128)S(1)}) custom-call(bf16[256,768]{1,0:T(8,128)(2,1)S(1)} %bitcast.14, f32[4,128,128]{2,1,0:T(8,128)S(1)} %copy-done.2, bf16[128,128]{1,0:T(8,128)(2,1)S(1)} %slice.58.gate_weight_ref, f32[4,384]{1,0:T(4,128)S(1)} %copy-done.11, ...), custom_call_target="tpu_custom_call" | custom-call | flops 125829120 | bytes 8388608 | tf_op jit(solution)/shard_map/prepare/pallas_call | solution.py:429
  39.4 0.7 %copy-done.5 = f32[128,640]{1,0:T(8,128)} copy-done((f32[128,640]{1,0:T(8,128)}, f32[128,640]{1,0:T(8,128)S(1)}, u32[]{:S(2)}) %copy-start.5) | copy-done | bytes 327704
  40.1 0.7 copy-done.7
  40.8 0.6 copy-done.13
  41.4 0.1 all-to-all-done.1
  41.5 0.9 %copy-done.3 = f32[4,128,128]{2,1,0:T(8,128)S(1)} copy-done((f32[4,128,128]{2,1,0:T(8,128)S(1)}, f32[4,128,128]{2,1,0:T(8,128)}, u32[]{:S(2)}) %copy-start.3) | copy-done | bytes 262168
  42.5 0.9 %copy-done.4 = f32[384,6]{1,0:T(8,128)S(1)} copy-done((f32[384,6]{1,0:T(8,128)S(1)}, f32[384,6]{1,0:T(8,128)}, u32[]{:S(2)}) %copy-start.4) | copy-done | bytes 9240
  43.4 1.0 %copy-done.6 = f32[128,640]{1,0:T(8,128)S(1)} copy-done((f32[128,640]{1,0:T(8,128)S(1)}, f32[128,640]{1,0:T(8,128)}, u32[]{:S(2)}) %copy-start.6) | copy-done | bytes 327704
  44.4 0.9 %copy-done.8 = f32[4,128,128]{2,1,0:T(8,128)S(1)} copy-done((f32[4,128,128]{2,1,0:T(8,128)S(1)}, f32[4,128,128]{2,1,0:T(8,128)}, u32[]{:S(2)}) %copy-start.8) | copy-done | bytes 262168
  45.3 0.8 %copy-done.12 = bf16[128,128]{1,0:T(8,128)(2,1)S(1)} copy-done((bf16[128,128]{1,0:T(8,128)(2,1)S(1)}, bf16[128,128]{1,0:T(8,128)(2,1)}, u32[]{:S(2)}) %copy-start.12) | copy-done | bytes 32792
  46.1 0.8 %copy-done.14 = f32[64,128]{1,0:T(8,128)S(1)} copy-done((f32[64,128]{1,0:T(8,128)S(1)}, f32[64,128]{1,0:T(8,128)}, u32[]{:S(2)}) %copy-start.14) | copy-done | bytes 32792
  46.8 4.6 %update.1 = (f32[4,128,128]{2,1,0:T(8,128)}, bf16[4,128,128]{2,1,0:T(8,128)(2,1)S(1)}, f32[64,128]{1,0:T(8,128)S(1)}, f32[8,384]{1,0:T(8,128)S(1)}, f32[8,128]{1,0:T(8,128)S(1)}, /*index=5*/bf16[256,256]{1,0:T(8,128)(2,1)S(1)}) custom-call(bf16[256,256]{1,0:T(8,128)(2,1)} %bitcast.3.recv_ref, f32[4,128,128]{2,1,0:T(8,128)S(1)} %copy-done.3, ...), custom_call_target="tpu_custom_call" | custom-call | tf_op jit(solution)/shard_map/update/pallas_call | solution.py:429
  51.5 13.7 %all_to_all.15 = bf16[32,8,256]{2,1,0:T(8,128)(2,1)S(1)} all-to-all(bf16[32,8,256]{2,1,0:T(8,128)(2,1)S(1)} %bitcast.16), channel_id=1, replica_groups=mesh['grp'=1,'row'=32] {'row'}, dimensions={0} | all-to-all | bytes 262144 | tf_op jit(solution)/shard_map/all_to_all | solution.py:459
  65.2 4.4 %last.1 = (f32[4,384]{1,0:T(4,128)}, f32[9,4]{1,0:T(8,128)S(1)}, f32[3,4]{1,0:T(4,128)}) custom-call(bf16[256,256]{1,0:T(8,128)(2,1)S(1)} %bitcast.15, bf16[4,128,128]{2,1,0:T(8,128)(2,1)S(1)} %get-tuple-element.25.half_ref, f32[64,128]{1,0:T(8,128)S(1)} %get-tuple-element.26.bias_ref, f32[8,384]{1,0:T(8,128)S(1)} %get-tuple-element.27.state_ref, ...), custom_call_target="tpu_custom_call" | custom-call | tf_op jit(solution)/shard_map/last/pallas_call | solution.py:429
  69.6 0.7 copy.27
  (36 shorter events, 0.4 us)
Async XLA Ops:
  0.6 1.0 %copy-start.1 = (f32[4,128,128]{2,1,0:T(8,128)S(1)}, f32[4,128,128]{2,1,0:T(8,128)}, u32[]{:S(2)}) copy-start(f32[4,128,128]{2,1,0:T(8,128)} %pair_ref.5) | copy-start | bytes 786436
  1.6 0.9 %copy-start.9 = (bf16[128,640]{1,0:T(8,128)(2,1)S(1)}, bf16[128,640]{1,0:T(8,128)(2,1)}, u32[]{:S(2)}) copy-start(bf16[128,640]{1,0:T(8,128)(2,1)} %tri_ref.1) | copy-start | bytes 491524
  2.5 0.7 copy-start.10
  3.2 0.7 copy-start.15
  3.8 0.7 copy-start.17
  4.5 0.7 copy-start.18
  5.2 0.7 copy-start.19
  5.9 9.3 %copy-start.20 = (bf16[384,1152]{1,0:T(8,128)(2,1)S(1)}, bf16[384,1152]{1,0:T(8,128)(2,1)}, u32[]{:S(2)}) copy-start(bf16[384,1152]{1,0:T(8,128)(2,1)} %param.22) | copy-start | bytes 2654212
  7.9 20.5 %all-to-all-start = ((bf16[32,8,768]{2,1,0:T(8,128)(2,1)}), bf16[32,8,768]{2,1,0:T(8,128)(2,1)S(1)}, u32[]{:S(2)}, u32[]{:S(2)}) async-start(bf16[32,8,768]{2,1,0:T(8,128)(2,1)} %bitcast), calls=%async_computation | async-start | bytes 786432 | tf_op jit(solution)/shard_map/all_to_all | solution.py:459
  16.1 0.7 copy-start.25
  16.1 0.7 copy-start.23
  16.1 0.7 copy-start.24
  16.4 17.8 %copy-start.21 = (f32[384,6]{0,1:T(8,128)S(1)}, f32[384,6]{0,1:T(8,128)}, u32[]{:S(2)}) copy-start(f32[384,6]{0,1:T(8,128)} %param.27) | copy-start | bytes 27652
  16.4 18.6 %copy-start.22 = (f32[128,12]{0,1:T(8,128)S(1)}, f32[128,12]{0,1:T(8,128)}, u32[]{:S(2)}) copy-start(f32[128,12]{0,1:T(8,128)} %param.23) | copy-start | bytes 18436
  16.6 19.7 %copy-start.11 = (f32[4,384]{1,0:T(4,128)S(1)}, f32[4,384]{1,0:T(4,128)}, u32[]{:S(2)}) copy-start(f32[4,384]{1,0:T(4,128)} %single_ref.5) | copy-start | bytes 18436
  16.6 19.7 %copy-start.16 = (s32[4]{0:T(128)S(1)}, s32[4]{0:T(128)}, u32[]{:S(2)}) copy-start(s32[4]{0:T(128)} %chain_ref.5) | copy-start | bytes 52
  30.0 11.5 %all-to-all-start.1 = ((bf16[32,8,256]{2,1,0:T(8,128)(2,1)}), bf16[32,8,256]{2,1,0:T(8,128)(2,1)}, u32[]{:S(2)}, u32[]{:S(2)}) async-start(bf16[32,8,256]{2,1,0:T(8,128)(2,1)} %bitcast.2), calls=%async_computation.1 | async-start | bytes 262144 | tf_op jit(solution)/shard_map/all_to_all | solution.py:459
  35.1 6.4 %copy-start = (bf16[2112,384]{1,0:T(8,128)(2,1)S(1)}, bf16[2112,384]{1,0:T(8,128)(2,1)}, u32[]{:S(2)}) copy-start(bf16[2112,384]{1,0:T(8,128)(2,1)} %out_weight_ref.3) | copy-start | bytes 4866052
  36.4 1.0 %copy-start.2 = (f32[4,128,128]{2,1,0:T(8,128)S(1)}, f32[4,128,128]{2,1,0:T(8,128)}, u32[]{:S(2)}) copy-start(f32[4,128,128]{2,1,0:T(8,128)} %pair_ref.5) | copy-start | bytes 786436
  39.4 0.7 %copy-start.5 = (f32[128,640]{1,0:T(8,128)}, f32[128,640]{1,0:T(8,128)S(1)}, u32[]{:S(2)}) copy-start(f32[128,640]{1,0:T(8,128)S(1)} %get-tuple-element.22.values_ref) | copy-start | bytes 983044
  40.1 0.7 copy-start.7
  40.8 0.6 copy-start.13
  41.5 1.0 %copy-start.3 = (f32[4,128,128]{2,1,0:T(8,128)S(1)}, f32[4,128,128]{2,1,0:T(8,128)}, u32[]{:S(2)}) copy-start(f32[4,128,128]{2,1,0:T(8,128)} %pair_ref.5) | copy-start | bytes 786436
  42.5 0.9 %copy-start.4 = (f32[384,6]{1,0:T(8,128)S(1)}, f32[384,6]{1,0:T(8,128)}, u32[]{:S(2)}) copy-start(f32[384,6]{1,0:T(8,128)} %copy.25.frame_weight_ref) | copy-start | bytes 27652
  43.4 1.0 %copy-start.6 = (f32[128,640]{1,0:T(8,128)S(1)}, f32[128,640]{1,0:T(8,128)}, u32[]{:S(2)}) copy-start(f32[128,640]{1,0:T(8,128)} %copy-done.5) | copy-start | bytes 983044
  44.4 0.9 %copy-start.8 = (f32[4,128,128]{2,1,0:T(8,128)S(1)}, f32[4,128,128]{2,1,0:T(8,128)}, u32[]{:S(2)}) copy-start(f32[4,128,128]{2,1,0:T(8,128)} %copy-done.7) | copy-start | bytes 786436
  45.3 0.8 %copy-start.12 = (bf16[128,128]{1,0:T(8,128)(2,1)S(1)}, bf16[128,128]{1,0:T(8,128)(2,1)}, u32[]{:S(2)}) copy-start(bf16[128,128]{1,0:T(8,128)(2,1)} %tri_out_ref.1) | copy-start | bytes 98308
  46.1 0.8 %copy-start.14 = (f32[64,128]{1,0:T(8,128)S(1)}, f32[64,128]{1,0:T(8,128)}, u32[]{:S(2)}) copy-start(f32[64,128]{1,0:T(8,128)} %copy-done.13) | copy-start | bytes 98308

commit v2 on v1

--- a/solution.py
+++ b/solution.py
@@ -151,10 +151,46 @@
     return onehot(((lane & 31) == entry) & (lane < 96))
 
 
+def copies(sems, *pairs):
+    started = [pltpu.make_async_copy(src, dst, sems.at[at]) for at, (src, dst) in enumerate(pairs)]
+    for copy in started:
+        copy.start()
+    return started
+
+
 def gate_kernel(
-    w, n, pair_ref, tri_ref, single_ref, quats_ref, translate_ref, mask_ref, chain_ref, send_ref, frame_ref, scr
+    w, n, pair_any, tri_any, single_any, quats_any, translate_any, mask_any, chain_any, send_ref, frame_ref,
+    pair_ref, tri_ref, single_ref, quats_ref, translate_ref, mask_ref, chain_ref, scr, sems,
 ):
     r, count, _ = pair_ref.shape
+    big = copies(sems, (tri_any.at[:, 0 : 4 * CH], tri_ref), *((pair_any.at[i], pair_ref.at[i]) for i in range(r)))
+    little = copies(
+        sems.at[r + 1 :],
+        (quats_any, quats_ref),
+        (translate_any, translate_ref),
+        (mask_any, mask_ref),
+        (chain_any, chain_ref),
+        (single_any, single_ref),
+    )
+    row, column = grid_of((2 * CH, 2 * CH))
+    d = row >> log2(2 * w)
+    side = (row >> log2(w)) & 1
+    take = onehot(column == side * CH + d * w + (row & (w - 1)))
+    big[0].wait()
+    gate_weight = jnp.concatenate([tri_ref[:, 0:CH], tri_ref[:, 2 * CH : 3 * CH]], axis=1)
+    value_weight = jnp.concatenate([tri_ref[:, CH : 2 * CH], tri_ref[:, 3 * CH : 4 * CH]], axis=1)
+    gate_weight = dot_nt(take, gate_weight).astype(bf16)
+    value_weight = dot_nt(take, value_weight).astype(bf16)
+    for copy in little:
+        copy.wait()
+    for i in range(r):
+        big[1 + i].wait()
+        normed = layer_norm(pair_ref[i]).astype(bf16)
+        gates = dot_nt(gate_weight, normed)
+        values = dot_nt(value_weight, normed)
+        side_values = jax.nn.sigmoid(gates) * values * mask_ref[i].astype(f32)
+        send_ref[:, i * count : (i + 1) * count] = side_values.astype(bf16)
+
     scr[...] = jnp.zeros_like(scr)
     quats = quats_ref[...]
     real = lax.rsqrt(1.0 + jnp.sum(quats * quats, axis=0, keepdims=True))
@@ -169,23 +205,7 @@
         frame = jnp.where((row == i) & (lane == MASK_AT), mask_ref[i].astype(f32), frame)
         frame = jnp.where((row == i) & (lane == CHAIN_AT), chain_ref[i].astype(f32), frame)
     frame_ref[...] = frame
-    state = jnp.concatenate([single_ref[...], jnp.zeros((IP - r, CS), f32)], axis=0)
-    fill_rows(send_ref, r * count, spread_rows(slots_of(state, frame), w, r))
-
-    row, column = grid_of((2 * CH, 2 * CH))
-    d = row >> log2(2 * w)
-    side = (row >> log2(w)) & 1
-    take = onehot(column == side * CH + d * w + (row & (w - 1)))
-    gate_weight = jnp.concatenate([tri_ref[:, 0:CH], tri_ref[:, 2 * CH : 3 * CH]], axis=1)
-    value_weight = jnp.concatenate([tri_ref[:, CH : 2 * CH], tri_ref[:, 3 * CH : 4 * CH]], axis=1)
-    gate_weight = dot_nt(take, gate_weight).astype(bf16)
-    value_weight = dot_nt(take, value_weight).astype(bf16)
-    for i in range(r):
-        normed = layer_norm(pair_ref[i]).astype(bf16)
-        gates = dot_nt(gate_weight, normed)
-        values = dot_nt(value_weight, normed)
-        side_values = jax.nn.sigmoid(gates) * values * mask_ref[i].astype(f32)
-        send_ref[:, i * count : (i + 1) * count] = side_values.astype(bf16)
+    fill_rows(send_ref, r * count, spread_rows(slots_of(pad_state(single_ref), frame), w, r))
 
 
 def product_kernel(w, n, r, recv_ref, send_ref):
@@ -222,20 +242,53 @@
 
 def head_masks():
     h, lane = grid_of((HP, 256))
-    scalar = jnp.where((lane >> log2(CHEAD)) == h, 1.0, 0.0)
-    scalar = jnp.where(h < H, scalar, 0.0)
+    query_scalar = jnp.where(((lane >> log2(CHEAD)) == h) & (h < H), 1.0, 0.0)
+    value_scalar = jnp.where((((lane - 64) >> log2(CHEAD)) == h) & (h < H), 1.0, 0.0)
     h, lane = grid_of((HP, 128))
     query = jnp.where(((lane >> log2(PQ)) == h) & (h < H), 1.0, 0.0)
     value = jnp.where(((lane >> log2(PV)) == h) & (h < H), 1.0, 0.0)
-    return scalar, query, value
-
-
-def logits_and_values(r, slots, state, frame, chain_ref, key_weight, query_weight, columns):
+    return query_scalar, value_scalar, query, value
+
+
+def own_side(r, state, frame, query_weight, columns):
+    both = jnp.concatenate([state, jnp.zeros_like(state)], axis=0).astype(bf16)
+    own = dot(both, query_weight)[0:IP]
+    width = H * CHEAD
+    points = H * PQ
+    fill = jnp.zeros((IP, 128 - points), f32)
+    own_local = [
+        jnp.concatenate([own[:, width + a * points : width + (a + 1) * points], fill], axis=1) for a in range(3)
+    ]
+    own_points = []
+    for a in range(3):
+        own_points.append(
+            frame[:, 3 * a : 3 * a + 1] * own_local[0]
+            + frame[:, 3 * a + 1 : 3 * a + 2] * own_local[1]
+            + frame[:, 3 * a + 2 : 3 * a + 3] * own_local[2]
+            + frame[:, 9 + a : 10 + a]
+        )
+    query_scalar, _, query_mask, _ = head_masks()
+    weight = columns[:, 0:1]
+    query_rows = []
+    lengths = []
+    for i in range(r):
+        scalar = own[i : i + 1, 0:256] * (third / math.sqrt(CHEAD)) * query_scalar
+        points = [p[i : i + 1] * query_mask for p in own_points]
+        query_rows.append(
+            jnp.concatenate([scalar] + [2.0 * weight * p for p in points] + [-weight * query_mask], axis=1)
+        )
+        length = points[0] * points[0] + points[1] * points[1] + points[2] * points[2]
+        lengths.append(-weight * jnp.sum(length, axis=1, keepdims=True))
+    return jnp.concatenate(query_rows, axis=0), jnp.concatenate(lengths, axis=0)
+
+
+def logits_and_values(r, slots, own, frame, key_weight, columns):
+    query_rows, lengths = own
     pieces = slots[:, CS:SLOT]
     entry = dot(pieces, piece_select(128, True))
     rows = dot_nt(piece_select(16), pieces)
     keys = dot(slots[:, 0:CS], key_weight)
-    local = [keys[:, 512 + 256 * a : 768 + 256 * a] for a in range(3)]
+    local = [keys[:, 384 + 256 * a : 640 + 256 * a] for a in range(3)]
     placed = []
     for a in range(3):
         placed.append(
@@ -244,55 +297,29 @@
             + entry[:, 3 * a + 2 : 3 * a + 3] * local[2]
             + entry[:, 9 + a : 10 + a]
         )
-    values = jnp.concatenate([keys[:, 256:512]] + [p[:, 0:128] for p in placed], axis=1)
+    values = jnp.concatenate([keys[:, 128:384]] + [p[:, 0:128] for p in placed], axis=1)
     key_points = [p[:, 128:256] for p in placed]
-    key_side = jnp.concatenate([keys[:, 0:256]] + key_points + [p * p for p in key_points], axis=1)
-
-    both = jnp.concatenate([state, jnp.zeros_like(state)], axis=0).astype(bf16)
-    own = dot(both, query_weight)[0:IP]
-    own_local = [own[:, 256 + 128 * a : 384 + 128 * a] for a in range(3)]
-    own_points = []
-    for a in range(3):
-        own_points.append(
-            frame[:, 3 * a : 3 * a + 1] * own_local[0]
-            + frame[:, 3 * a + 1 : 3 * a + 2] * own_local[1]
-            + frame[:, 3 * a + 2 : 3 * a + 3] * own_local[2]
-            + frame[:, 9 + a : 10 + a]
-        )
-    scalar_mask, query_mask, _ = head_masks()
-    weight = columns[:, 0:1]
-    query_rows = []
-    constants = []
+    length = key_points[0] * key_points[0] + key_points[1] * key_points[1] + key_points[2] * key_points[2]
+    key_side = jnp.concatenate([keys[:, 0:256]] + key_points + [length], axis=1)
+    far = mask_fill * (rows[MASK_AT : MASK_AT + 1, :] - 1.0)
+    added = []
     for i in range(r):
-        scalar = own[i : i + 1, 0:256] * (third / math.sqrt(CHEAD)) * scalar_mask
-        points = [p[i : i + 1] * query_mask for p in own_points]
-        query_rows.append(
-            jnp.concatenate(
-                [scalar] + [2.0 * weight * p for p in points] + [-weight * query_mask] * 3, axis=1
-            )
-        )
-        length = points[0] * points[0] + points[1] * points[1] + points[2] * points[2]
-        own_chain = chain_ref[i].astype(f32)
-        same = rows[CHAIN_AT : CHAIN_AT + 1, :] == own_chain
-        constants.append(
-            jnp.where(same, columns[:, 2:3], columns[:, 1:2])
-            + mask_fill * (rows[MASK_AT : MASK_AT + 1, :] - 1.0)
-            - weight * jnp.sum(length, axis=1, keepdims=True)
-        )
-    logits = dot_nt(jnp.concatenate(query_rows, axis=0), key_side, highest)
-    return logits + jnp.concatenate(constants, axis=0), values
-
-
-def attend(r, logits, values, pair_half, state, frame, out_weight, frame_weight):
+        same = rows[CHAIN_AT : CHAIN_AT + 1, :] == frame[i : i + 1, CHAIN_AT : CHAIN_AT + 1]
+        added.append(jnp.where(same, columns[:, 2:3], columns[:, 1:2]) + far + lengths[i * HP : (i + 1) * HP])
+    logits = dot_nt(query_rows, key_side, highest)
+    return logits + jnp.concatenate(added, axis=0), values
+
+
+def attend(r, logits, values, pair_half, state, frame, weights):
     top = jnp.max(logits, axis=1, keepdims=True)
     raised = jnp.exp(logits - top)
     attention = raised / jnp.sum(raised, axis=1, keepdims=True)
     summed = dot(attention, values, highest)
-    scalar_mask, _, value_mask = head_masks()
-    masks = jnp.concatenate([scalar_mask, value_mask, value_mask, value_mask], axis=1)
+    _, value_scalar, _, value_mask = head_masks()
+    masks = jnp.concatenate([value_scalar, value_mask, value_mask, value_mask], axis=1)
     summed = summed * jnp.concatenate([masks] * r, axis=0)
-    row, column = grid_of((IP, r * HP))
-    gathered = dot(jnp.where((column >> log2(HP)) == row, 1.0, 0.0), summed, highest)
+    gathered = jnp.sum(summed.reshape(r, HP, 640), axis=1)
+    gathered = jnp.concatenate([gathered, jnp.zeros((IP - r, 640), f32)], axis=0)
     relative = [
         gathered[:, 256 + 128 * a : 256 + 128 * a + H * PV] - frame[:, 9 + a : 10 + a] for a in range(3)
     ]
@@ -312,15 +339,16 @@
     row, column = grid_of((H * IP, r * HP))
     by_head = dot(onehot(column == (row & (IP - 1)) * HP + (row >> log2(IP))), out_pair)
     combined = jnp.concatenate(
-        [gathered[:, 0 : H * CHEAD]]
+        [gathered[:, 256 - H * CHEAD : 256]]
         + out_local
         + [out_norm]
         + [by_head[h * IP : (h + 1) * IP] for h in range(H)],
         axis=1,
     )
     combined = jnp.concatenate([combined, jnp.zeros_like(combined)], axis=0).astype(bf16)
+    out_weight, frame_weight = weights()
     state = layer_norm(state + dot(combined, out_weight)[0:IP])
-    update = dot(state, frame_weight, highest)
+    update = dot_nt(state, frame_weight, highest)
     quat = [update[:, a : a + 1] for a in range(3)]
     real = lax.rsqrt(1.0 + (quat[0] * quat[0] + quat[1] * quat[1] + quat[2] * quat[2]))
     step = quat_entries(quat[0] * real, quat[1] * real, quat[2] * real, real)
@@ -351,34 +379,100 @@
     return jnp.concatenate([single_ref[...], jnp.zeros((IP - r, CS), f32)], axis=0)
 
 
-def prepare_kernel(
-    w, n, recv_ref, pair_ref, gate_weight_ref, single_ref, frame_ref, chain_ref, key_ref, query_ref, columns_ref,
-    gate_ref, logits_ref, values_ref,
+def own_kernel(
+    pair_any, tri_any, qkv_any, single_any, frame_any, columns_any,
+    gate_ref, key_ref, query_ref, rows_ref, lengths_ref,
+    pair_ref, gate_weight_ref, qkv_ref, single_ref, frame_ref, columns_ref, sems,
 ):
     r, count, _ = pair_ref.shape
-    slots = natural_rows(recv_ref, r * count, w, r, n)
-    logits, values = logits_and_values(
-        r, slots, pad_state(single_ref), frame_ref[...], chain_ref, key_ref[...], query_ref[...], columns_ref[...]
-    )
-    logits_ref[...] = logits
-    values_ref[...] = values
+    for copy in copies(
+        sems,
+        (pair_any, pair_ref),
+        (tri_any.at[:, 4 * CH :], gate_weight_ref),
+        (qkv_any, qkv_ref),
+        (single_any, single_ref),
+        (frame_any, frame_ref),
+        (columns_any, columns_ref),
+    ):
+        copy.wait()
+    width = H * CHEAD
+    start = 3 * width
+    points = H * PQ
+
+    def padded(first, size, to):
+        block = qkv_ref[:, first : first + size].astype(f32)
+        return jnp.concatenate([block, jnp.zeros((CS, to - size), f32)], axis=1).astype(bf16)
+
+    queries = [qkv_ref[:, 0:width], qkv_ref[:, start : start + 3 * points]]
+    query_ref[...] = jnp.concatenate([q.astype(f32) for q in queries] + [jnp.zeros((CS, 48), f32)], axis=1).astype(bf16)
+    key_ref[:, 0 : 2 * width] = qkv_ref[:, width:start]
+    for a in range(3):
+        key_ref[:, 512 + 256 * a : 640 + 256 * a] = padded(start + (3 + a) * points, points, 128)
+        key_ref[:, 384 + 256 * a : 512 + 256 * a] = padded(start + 6 * points + a * H * PV, H * PV, 128)
+    rows, lengths = own_side(r, pad_state(single_ref), frame_ref[...], query_ref[...], columns_ref[...])
+    rows_ref[...] = rows
+    lengths_ref[...] = jnp.broadcast_to(lengths, lengths_ref.shape)
     for i in range(r):
         normed = layer_norm(pair_ref[i]).astype(bf16)
         gate_ref[i] = jax.nn.sigmoid(dot(normed, gate_weight_ref[...]))
 
 
+def prepare_kernel(
+    w, n, r, recv_any, frame_any, rows_any, lengths_any, key_any, columns_any, logits_ref, values_ref,
+    recv_ref, frame_ref, rows_ref, lengths_ref, key_ref, columns_ref, sems,
+):
+    lanes = recv_ref.shape[1]
+    for copy in copies(
+        sems,
+        (recv_any.at[:, r * n * r : r * n * r + lanes], recv_ref),
+        (frame_any, frame_ref),
+        (rows_any, rows_ref),
+        (lengths_any, lengths_ref),
+        (key_any, key_ref),
+        (columns_any, columns_ref),
+    ):
+        copy.wait()
+    slots = natural_rows(recv_ref, 0, w, r, n)
+    logits, values = logits_and_values(
+        r, slots, (rows_ref[...], lengths_ref[:, 0:1]), frame_ref[...], key_ref[...], columns_ref[...]
+    )
+    logits_ref[...] = logits
+    values_ref[...] = values
+
+
 def update_kernel(
-    w, n, recv_ref, pair_ref, gate_ref, logits_ref, values_ref, tri_out_ref, bias_weight_ref, single_ref, frame_ref,
-    out_weight_ref, frame_weight_ref, pair_out_ref, half_ref, bias_ref, state_ref, new_frame_ref, send_ref,
+    w, n, recv_any, tri_out_any, pair_any, gate_any, bias_weight_any, logits_any, values_any, single_any, frame_any,
+    out_weight_any, frame_weight_any, pair_out_any, half_ref, bias_ref, state_ref, new_frame_ref, send_ref,
+    recv_ref, tri_out_ref, pair_ref, gate_ref, bias_weight_ref, logits_ref, values_ref, single_ref, frame_ref,
+    out_weight_ref, frame_weight_ref, pair_out_ref, sems,
 ):
     r, count, _ = pair_ref.shape
+    bias_weight_ref[...] = jnp.zeros_like(bias_weight_ref)
+    loads = copies(
+        sems,
+        (recv_any, recv_ref),
+        (tri_out_any, tri_out_ref),
+        (pair_any, pair_ref),
+        (gate_any, gate_ref),
+        (bias_weight_any, bias_weight_ref.at[0:H]),
+        (logits_any, logits_ref),
+        (values_any, values_ref),
+        (single_any, single_ref),
+        (frame_any, frame_ref),
+        (out_weight_any, out_weight_ref),
+        (frame_weight_any, frame_weight_ref),
+    )
     half = r // 2
     row, column = grid_of((2 * CH, 2 * CH))
     c = row & (CH - 1)
     take = onehot(column == (c >> log2(w)) * 2 * w + (row >> log2(CH)) * w + (c & (w - 1)))
+    loads[0].wait()
     product = dot(take, recv_ref[...])
     biases = []
     halves = []
+    stores = []
+    for copy in loads[1:5]:
+        copy.wait()
     for high in range(2):
         normed = layer_norm(product[high * CH : (high + 1) * CH], axis=0).astype(bf16)
         update = dot_tn(normed, tri_out_ref[...])
@@ -386,60 +480,84 @@
             i = high * half + low
             pair_out = pair_ref[i] + gate_ref[i] * update[low * count : (low + 1) * count]
             pair_out_ref[i] = pair_out
+            store = pltpu.make_async_copy(pair_out_ref.at[i], pair_out_any.at[i], sems.at[11 + i])
+            store.start()
+            stores.append(store)
             normed_pair = layer_norm(pair_out)
             biases.append(dot_nt(bias_weight_ref[...], normed_pair, highest) * third)
             halves.append(normed_pair.astype(bf16))
             half_ref[i] = halves[-1]
     bias = jnp.concatenate(biases, axis=0)
     bias_ref[...] = bias
+
+    def weights():
+        loads[9].wait()
+        loads[10].wait()
+        return out_weight_ref[...], frame_weight_ref[...]
+
+    for copy in loads[5:9]:
+        copy.wait()
     state, frame = attend(
-        r, logits_ref[...] + bias, values_ref[...], halves, pad_state(single_ref), frame_ref[...],
-        out_weight_ref[...], frame_weight_ref[...],
+        r, logits_ref[...] + bias, values_ref[...], halves, pad_state(single_ref), frame_ref[...], weights
     )
     state_ref[...] = state
     new_frame_ref[...] = frame
     fill_rows(send_ref, 0, spread_rows(slots_of(state, frame), w, r))
+    for store in stores:
+        store.wait()
 
 
 def last_kernel(
-    w, n, recv_ref, half_ref, bias_ref, state_ref, frame_ref, chain_ref, key_ref, query_ref, columns_ref,
-    out_weight_ref, frame_weight_ref, single_out_ref, rotation_ref, translation_ref, scr,
+    w, n, recv_ref, half_ref, bias_ref, state_ref, frame_ref, columns_any, query_any, key_any,
+    out_weight_any, frame_weight_any, single_out_ref, rotation_ref, translation_ref,
+    columns_ref, query_ref, key_ref, out_weight_ref, frame_weight_ref, scr, sems,
 ):
     r = half_ref.shape[0]
+    loads = copies(
+        sems,
+        (query_any, query_ref),
+        (columns_any, columns_ref),
+        (key_any, key_ref),
+        (out_weight_any, out_weight_ref),
+        (frame_weight_any, frame_weight_ref),
+    )
     slots = natural_rows(recv_ref, 0, w, r, n)
     state, frame = state_ref[...], frame_ref[...]
-    logits, values = logits_and_values(
-        r, slots, state, frame, chain_ref, key_ref[...], query_ref[...], columns_ref[...]
-    )
-    state, frame = attend(
-        r, logits + bias_ref[...], values, [half_ref[i] for i in range(r)], state, frame,
-        out_weight_ref[...], frame_weight_ref[...],
-    )
+    loads[0].wait()
+    loads[1].wait()
+    own = own_side(r, state, frame, query_ref[...], columns_ref[...])
+    loads[2].wait()
+    logits, values = logits_and_values(r, slots, own, frame, key_ref[...], columns_ref[...])
+
+    def weights():
+        loads[3].wait()
+        loads[4].wait()
+        return out_weight_ref[...], frame_weight_ref[...]
+
+    halves = [half_ref[i] for i in range(r)]
+    state, frame = attend(r, logits + bias_ref[...], values, halves, state, frame, weights)
     single_out_ref[...] = state[0:r]
+    rotation_ref[...] = frame[0:r, 0:9]
     scr[...] = jnp.concatenate([frame, jnp.zeros((128 - IP, 128), f32)], axis=0).T
-    rotation_ref[...] = scr[0:9, 0:r]
     translation_ref[...] = scr[9:12, 0:r]
 
 
 VMEM = pl.BlockSpec(memory_space=pltpu.VMEM)
-SMEM = pl.BlockSpec(memory_space=pltpu.SMEM)
-
-
-def call(body, name, outs, args, small=(), scratch=(), limit=32, flops=0, moved=0):
+HBM = pl.BlockSpec(memory_space=pltpu.HBM)
+FREE = pl.BlockSpec(memory_space=pl.ANY)
+
+
+def call(body, name, outs, args, outside=(), outside_outs=(), free=(), scratch=(), limit=32, flops=0, moved=0):
     return pl.pallas_call(
         body,
         name=name,
         out_shape=[jax.ShapeDtypeStruct(s, d) for s, d in outs],
-        in_specs=[SMEM if at in small else VMEM for at in range(len(args))],
-        out_specs=[VMEM] * len(outs),
+        in_specs=[FREE if at in free else HBM if at in outside else VMEM for at in range(len(args))],
+        out_specs=[HBM if at in outside_outs else VMEM for at in range(len(outs))],
         scratch_shapes=list(scratch),
         compiler_params=pltpu.CompilerParams(vmem_limit_bytes=limit * 2**20),
         cost_estimate=pl.CostEstimate(flops=flops, bytes_accessed=moved, transcendentals=0),
     )(*args)
-
-
-def pad_lanes(block, width):
-    return jnp.pad(block, ((0, 0), (0, width - block.shape[1])))
 
 
 def local(
@@ -451,44 +569,63 @@
     w = CH // n
     rows = 2 * w
     lanes = r * SLOT // rows
-    scale = count // 128
-    limit = 24 if scale == 1 else 56
+    limit = 24 if count == 128 else 56
 
     def exchange(sent):
         width = sent.shape[1]
         got = lax.all_to_all(sent.reshape(n, rows, width), "row", 0, 0, tiled=True)
         return got.reshape(n * rows, width)
 
+    def like(array):
+        return pltpu.VMEM(array.shape, array.dtype)
+
+    dma = pltpu.SemaphoreType.DMA
     sent, frame = call(
         functools.partial(gate_kernel, w, n),
         "gate",
         [((n * rows, r * count + lanes), bf16), ((IP, 128), f32)],
         [pair, tri_weight, single, quats, translate, res_mask, chain_ids],
-        small=(5, 6),
-        scratch=[pltpu.VMEM((128, 128), f32)],
-        limit=limit,
+        outside=range(7),
+        scratch=[
+            like(pair),
+            pltpu.VMEM((CH, 4 * CH), bf16),
+            like(single),
+            like(quats),
+            like(translate),
+            pltpu.SMEM((r,), jnp.int32),
+            pltpu.SMEM((r,), jnp.int32),
+            pltpu.VMEM((128, 128), f32),
+            dma((r + 6,)),
+        ],
+        limit=60,
     )
     received = exchange(sent)
 
-    width = H * CHEAD
-    start = 3 * width
-    query_points = qkv_weight[:, start : start + 3 * H * PQ]
-    key_points = qkv_weight[:, start + 3 * H * PQ : start + 6 * H * PQ]
-    value_points = qkv_weight[:, start + 6 * H * PQ :]
-    key_weight = [pad_lanes(qkv_weight[:, width : 2 * width], 256), pad_lanes(qkv_weight[:, 2 * width : start], 256)]
-    query_weight = [pad_lanes(qkv_weight[:, :width], 256)]
-    for a in range(3):
-        key_weight.append(pad_lanes(value_points[:, a * H * PV : (a + 1) * H * PV], 128))
-        key_weight.append(pad_lanes(key_points[:, a * H * PQ : (a + 1) * H * PQ], 128))
-        query_weight.append(pad_lanes(query_points[:, a * H * PQ : (a + 1) * H * PQ], 128))
-    key_weight = jnp.concatenate(key_weight, axis=1)
-    query_weight = jnp.concatenate(query_weight, axis=1)
     point_weight = head_gamma * (math.sqrt(2.0 / (9.0 * PQ)) * 0.5 * third)
     columns = jnp.stack([point_weight, chain_bias[0], chain_bias[1]], axis=1)
     columns = jnp.pad(columns, ((0, HP - H), (0, 125)))
-    bias_rows = jnp.pad(bias_weight.T, ((0, HP - H), (0, 0)))
-    gate_weight = tri_weight[:, 4 * CH :]
-
+    gate, key_weight, query_weight, query_rows, lengths = call(
+        own_kernel,
+        "own",
+        [
+            ((r, count, CH), f32),
+            ((CS, 1152), bf16),
+            ((CS, 384), bf16),
+            ((r * HP, 768), f32),
+            ((r * HP, 128), f32),
+        ],
+        [pair, tri_weight, qkv_weight, single, frame, columns],
+        outside=range(6),
+        scratch=[
+            like(pair), pltpu.VMEM((CH, CH), bf16), like(qkv_weight), like(single), like(frame), like(columns), dma((6,))
+        ],
+        limit=60,
+        flops=2 * r * count * CH * CH,
+        moved=16 * 2**20,
+    )
+    received, gate, key_weight, query_weight, query_rows, lengths = lax.optimization_barrier(
+        (received, gate, key_weight, query_weight, query_rows, lengths)
+    )
     (formed,) = call(
         functools.partial(product_kernel, w, n, r),
         "product",
@@ -497,16 +634,27 @@
         limit=limit,
     )
     products = exchange(formed)
-    gate, logits, values = call(
-        functools.partial(prepare_kernel, w, n),
+    logits, values = call(
+        functools.partial(prepare_kernel, w, n, r),
         "prepare",
-        [((r, count, CH), f32), ((r * HP, count), f32), ((count, 640), f32)],
-        [received, pair, gate_weight, single, frame, chain_ids, key_weight, query_weight, columns],
-        small=(5,),
+        [((r * HP, count), f32), ((count, 640), f32)],
+        [received, frame, query_rows, lengths, key_weight, columns],
+        outside=range(6),
+        free=(0,),
+        scratch=[
+            pltpu.VMEM((n * rows, lanes), bf16),
+            like(frame),
+            like(query_rows),
+            like(lengths),
+            like(key_weight),
+            like(columns),
+            dma((6,)),
+        ],
         limit=limit,
         flops=2 * count * CS * 1280,
         moved=8 * 2**20,
     )
+    frame_weight = frame_weight.T
     pair_out, pair_half, bias, state, frame, sent = call(
         functools.partial(update_kernel, w, n),
         "update",
@@ -518,20 +666,46 @@
             ((IP, 128), f32),
             ((n * rows, lanes), bf16),
         ],
-        [products, pair, gate, logits, values, tri_out_weight, bias_rows, single, frame, out_weight, frame_weight],
+        [products, tri_out_weight, pair, gate, bias_weight.T, logits, values, single, frame, out_weight, frame_weight],
+        outside=range(11),
+        free=(0,),
+        outside_outs=(0,),
+        scratch=[
+            like(products),
+            like(tri_out_weight),
+            like(pair),
+            like(gate),
+            pltpu.VMEM((HP, CH), f32),
+            like(logits),
+            like(values),
+            like(single),
+            like(frame),
+            like(out_weight),
+            like(frame_weight),
+            like(pair),
+            dma((r + 11,)),
+        ],
         limit=limit,
     )
     received = exchange(sent)
     single_out, rotation, translation = call(
         functools.partial(last_kernel, w, n),
         "last",
-        [((r, CS), f32), ((9, r), f32), ((3, r), f32)],
-        [received, pair_half, bias, state, frame, chain_ids, key_weight, query_weight, columns, out_weight, frame_weight],
-        small=(5,),
-        scratch=[pltpu.VMEM((128, 128), f32)],
+        [((r, CS), f32), ((r, 9), f32), ((3, r), f32)],
+        [received, pair_half, bias, state, frame, columns, query_weight, key_weight, out_weight, frame_weight],
+        outside=range(5, 10),
+        scratch=[
+            like(columns),
+            like(query_weight),
+            like(key_weight),
+            like(out_weight),
+            like(frame_weight),
+            pltpu.VMEM((128, 128), f32),
+            dma((5,)),
+        ],
         limit=limit,
     )
-    return (pair_out, single_out, rotation, translation)
+    return (pair_out, single_out, rotation.T, translation)
 
 
 def solution(mesh):

time: 71.1 us -> 60.7 us (0.85)
  local copies, waits for them, and re-layouts: 17.4 us -> 8.08 us
  Pallas kernels: 14.8 us -> 18.9 us
  blocking collectives: 13.7 us -> 11 us
  other arithmetic: 1.97 us -> 0.67 us
    unnamed x61 -> x32, local copies, waits for them, and re-layouts: 15.3 us -> 6.63 us
    pallas_call x5 -> x6, Pallas kernels: 14.8 us -> 18.9 us  [call(): pl.pallas_call(body, name=name, out_shape=[jax.ShapeDtypeStruct(s, d) for...]
    all_to_all x1, blocking collectives: 13.7 us -> 11 us  [exchange(): got = lax.all_to_all(sent.reshape(n, rows, width), 'row', 0, 0, tiled=True)]
    slice x4 -> x0, local copies, waits for them, and re-layouts: 1.94 us -> none  [the longest x1 0.91 us: local(): query_points[:, a * H * PQ:(a + 1) * H * PQ]]
    concatenate x1 -> x0, other arithmetic: 1.26 us -> none  [local(): query_weight = jnp.concatenate(query_weight, axis=1)]
    another operation x2, local copies, waits for them, and re-layouts: 0.1 us -> 0.85 us  [local(): columns = jnp.stack([point_weight, chain_bias[0], chain_bias[1]], axis=1)]
  transfers between devices with their start and end apart: 2 -> 2, of which waited for: 2 -> 2; matrix products, arithmetic and copies ran while one was open for 7% -> 4% of each run, Pallas kernels for 3% -> 9%
where the time goes in v2:
time: 60.7 us; the launch traced here: 60 us
  Pallas kernels  18.9 us (31%)
  blocking collectives  11 us (18%)
  waiting for transfers between devices  10.6 us (17%)
  starting transfers between devices  9.94 us (16%)
  local copies, waits for them, and re-layouts  8.08 us (13%)
  between operations  0.77 us (1%)
  other arithmetic  0.67 us (1%)
    pallas_call x6, Pallas kernels, call(): pl.pallas_call(body, name=name, out_shape=[jax.ShapeDtypeStruct(s, d) for...  18.9 us
    all_to_all x1, blocking collectives, exchange(): got = lax.all_to_all(sent.reshape(n, rows, width), 'row', 0, 0, tiled=True)  11 us
    all_to_all x2, waiting for transfers between devices, exchange(): got = lax.all_to_all(sent.reshape(n, rows, width), 'row', 0, 0, tiled=True)  10.6 us
    all_to_all x2, starting transfers between devices, exchange(): got = lax.all_to_all(sent.reshape(n, rows, width), 'row', 0, 0, tiled=True)  9.94 us
    unnamed x32, local copies, waits for them, and re-layouts  6.63 us
  transfers between devices with their start and end apart: 2, of which 2 were waited for; matrix products, arithmetic and copies ran while one was open for 4% of the time, Pallas kernels for 9%

profile of v2, /device:TPU:0, one launch (start us, length us, event | category | flops | bytes accessed | tf_op | source)
XLA Modules:
  0.0 60.0 jit_solution(1133507786403879619)
XLA Ops:
  0.6 3.5 %gate.1 = (bf16[256,768]{1,0:T(8,128)(2,1)}, f32[8,128]{1,0:T(8,128)}) custom-call(f32[4,128,128]{2,1,0:T(8,128)} %pair_any.5, bf16[128,640]{1,0:T(8,128)(2,1)} %tri_any.3, f32[4,384]{1,0:T(4,128)} %single_any.5, f32[3,4]{1,0:T(4,128)} %quats_any.1, f32[3,4]{1,0:T(4,128)} %translate_any.1, s32[4]{0:T(128)} %mask_any.1, s32[4]{0:T(128)} %chain_any.1), custom_call_target="tpu_custom_call" | custom-call | tf_op jit(solution)/shard_map/gate/pallas_call | solution.py:551
  4.1 0.0 copy-start.10
  4.1 7.3 %all-to-all-start = ((bf16[32,8,768]{2,1,0:T(8,128)(2,1)}), bf16[32,8,768]{2,1,0:T(8,128)(2,1)S(1)}, u32[]{:S(2)}, u32[]{:S(2)}) async-start(bf16[32,8,768]{2,1,0:T(8,128)(2,1)} %bitcast.23), calls=%async_computation | async-start | bytes 786432 | tf_op jit(solution)/shard_map/all_to_all | solution.py:576
  11.5 0.7 %multiply_bitcast_fusion = f32[12,1]{0,1:T(1,128)S(1)} fusion(f32[12]{0:T(128)} %param.24), kind=kLoop, calls=%fused_computation.3 | loop fusion | flops 12 | bytes 96 | tf_op jit(solution)/shard_map/stack | solution.py:605
  12.1 0.8 %slice_bitcast_fusion.1 = (f32[12,1]{0,1:T(1,128)S(1)}, f32[12,1]{0,1:T(1,128)S(1)}) fusion(f32[2,12]{1,0:T(2,128)} %param.25), kind=kLoop, calls=%fused_computation.2 | loop fusion | bytes 192 | tf_op jit(solution)/shard_map/stack;squeeze | solution.py:605
  12.9 0.1 copy.21
  13.0 0.6 %pad.4.columns_any = f32[16,128]{1,0:T(8,128)} pad(f32[12,3]{1,0:T(8,128)S(1)} %copy.21, f32[]{:T(128)} %constant.4.clone.1), padding=0_4x0_125 | pad | bytes 8340 | tf_op jit(solution)/shard_map/jit(_pad)/pad | solution.py:606
  13.6 0.0 copy-start.7
  13.6 0.0 copy-start
  13.6 0.0 copy-start.3
  13.6 0.0 copy-start.8
  13.6 0.0 copy-start.9
  13.6 3.3 %own.1 = (f32[4,128,128]{2,1,0:T(8,128)}, bf16[384,1152]{1,0:T(8,128)(2,1)}, bf16[384,384]{1,0:T(8,128)(2,1)}, f32[64,768]{1,0:T(8,128)}, f32[64,128]{1,0:T(8,128)}) custom-call(f32[4,128,128]{2,1,0:T(8,128)} %pair_any.5, bf16[128,640]{1,0:T(8,128)(2,1)} %tri_any.3, bf16[384,1152]{1,0:T(8,128)(2,1)} %qkv_any.1, f32[4,384]{1,0:T(4,128)} %single_any.5, ...), custom_call_target="tpu_custom_call" | custom-call | flops 16777216 | bytes 16777216 | tf_op jit(solution)/shard_map/own/pallas_call | solution.py:551
  16.9 7.7 %all-to-all-done = bf16[32,8,768]{2,1,0:T(8,128)(2,1)S(1)} async-done(((bf16[32,8,768]{2,1,0:T(8,128)(2,1)}), bf16[32,8,768]{2,1,0:T(8,128)(2,1)S(1)}, u32[]{:S(2)}, u32[]{:S(2)}) %all-to-all-start) | async-done | bytes 393248 | tf_op jit(solution)/shard_map/all_to_all | solution.py:576
  24.6 1.7 %product.1 = bf16[256,256]{1,0:T(8,128)(2,1)} custom-call(bf16[256,768]{1,0:T(8,128)(2,1)S(1)} %bitcast.15), custom_call_target="tpu_custom_call" | custom-call | tf_op jit(solution)/shard_map/product/pallas_call | solution.py:551
  26.3 2.6 %all-to-all-start.1 = ((bf16[32,8,256]{2,1,0:T(8,128)(2,1)}), bf16[32,8,256]{2,1,0:T(8,128)(2,1)S(1)}, u32[]{:S(2)}, u32[]{:S(2)}) async-start(bf16[32,8,256]{2,1,0:T(8,128)(2,1)} %bitcast.5), calls=%async_computation.1 | async-start | bytes 262144 | tf_op jit(solution)/shard_map/all_to_all | solution.py:576
  28.9 0.0 copy-done.10
  28.9 0.0 copy-done.7
  29.0 0.0 copy-start.1
  29.0 1.2 %copy-done.1 = bf16[384,1152]{1,0:T(8,128)(2,1)S(1)} copy-done((bf16[384,1152]{1,0:T(8,128)(2,1)S(1)}, bf16[384,1152]{1,0:T(8,128)(2,1)}, u32[]{:S(2)}) %copy-start.1) | copy-done | bytes 884760
  30.1 0.0 copy-start.6
  30.1 0.9 %copy-done.6 = f32[64,768]{1,0:T(8,128)S(1)} copy-done((f32[64,768]{1,0:T(8,128)S(1)}, f32[64,768]{1,0:T(8,128)}, u32[]{:S(2)}) %copy-start.6) | copy-done | bytes 196632
  31.1 0.0 copy-start.14
  31.1 0.8 %copy-done.14 = f32[64,128]{1,0:T(8,128)S(1)} copy-done((f32[64,128]{1,0:T(8,128)S(1)}, f32[64,128]{1,0:T(8,128)}, u32[]{:S(2)}) %copy-start.14) | copy-done | bytes 32792
  31.8 1.8 %prepare.1 = (f32[64,128]{1,0:T(8,128)S(1)}, f32[128,640]{1,0:T(8,128)S(1)}) custom-call(bf16[256,768]{1,0:T(8,128)(2,1)S(1)} %bitcast.16, f32[8,128]{1,0:T(8,128)S(1)} %copy-done.10, f32[64,768]{1,0:T(8,128)S(1)} %copy-done.6, f32[64,128]{1,0:T(8,128)S(1)} %copy-done.14, bf16[384,1152]{1,0:T(8,128)(2,1)S(1)} %copy-done.1, f32[16,128]{1,0:T(8,128)S(1)} %copy-done.7), custom_call_target="tpu_custom_call" | custom-call | flops 125829120 | bytes 8388608 | tf_op jit(solution)/shard_map/prepare/pallas_call | solution.py:551
  33.6 0.0 copy-start.12
  33.6 0.6 copy-done.12
  34.2 0.0 copy-start.2
  34.2 0.0 copy-start.4
  34.2 3.0 %all-to-all-done.1 = bf16[32,8,256]{2,1,0:T(8,128)(2,1)S(1)} async-done(((bf16[32,8,256]{2,1,0:T(8,128)(2,1)}), bf16[32,8,256]{2,1,0:T(8,128)(2,1)S(1)}, u32[]{:S(2)}, u32[]{:S(2)}) %all-to-all-start.1) | async-done | bytes 131104 | tf_op jit(solution)/shard_map/all_to_all | solution.py:576
  37.2 0.0 copy-done
  37.2 0.0 copy-done.3
  37.2 0.0 copy-done.8
  37.2 0.0 copy-done.9
  37.2 0.0 copy-start.5
  37.2 0.9 %copy-done.5 = f32[4,128,128]{2,1,0:T(8,128)S(1)} copy-done((f32[4,128,128]{2,1,0:T(8,128)S(1)}, f32[4,128,128]{2,1,0:T(8,128)}, u32[]{:S(2)}) %copy-start.5) | copy-done | bytes 262168
  38.1 0.0 copy-start.11
  38.1 0.8 %copy-done.11 = bf16[128,128]{1,0:T(8,128)(2,1)S(1)} copy-done((bf16[128,128]{1,0:T(8,128)(2,1)S(1)}, bf16[128,128]{1,0:T(8,128)(2,1)}, u32[]{:S(2)}) %copy-start.11) | copy-done | bytes 32792
  38.9 0.0 copy-start.13
  38.9 0.8 %copy-done.13 = f32[64,128]{1,0:T(8,128)S(1)} copy-done((f32[64,128]{1,0:T(8,128)S(1)}, f32[64,128]{1,0:T(8,128)}, u32[]{:S(2)}) %copy-start.13) | copy-done | bytes 32792
  39.7 0.0 copy-start.15
  39.7 0.7 %copy-done.15 = f32[128,12]{0,1:T(8,128)S(1)} copy-done((f32[128,12]{0,1:T(8,128)S(1)}, f32[128,12]{0,1:T(8,128)}, u32[]{:S(2)}) %copy-start.15) | copy-done | bytes 6168
  40.4 4.3 %update.1 = (f32[4,128,128]{2,1,0:T(8,128)}, bf16[4,128,128]{2,1,0:T(8,128)(2,1)S(1)}, f32[64,128]{1,0:T(8,128)S(1)}, f32[8,384]{1,0:T(8,128)S(1)}, f32[8,128]{1,0:T(8,128)S(1)}, /*index=5*/bf16[256,256]{1,0:T(8,128)(2,1)S(1)}) custom-call(bf16[256,256]{1,0:T(8,128)(2,1)S(1)} %bitcast.17, bf16[128,128]{1,0:T(8,128)(2,1)S(1)} %copy-done.11, ...), custom_call_target="tpu_custom_call" | custom-call | tf_op jit(solution)/shard_map/update/pallas_call | solution.py:551
  44.7 11.0 %all_to_all.15 = bf16[32,8,256]{2,1,0:T(8,128)(2,1)S(1)} all-to-all(bf16[32,8,256]{2,1,0:T(8,128)(2,1)S(1)} %bitcast.19), channel_id=1, replica_groups=mesh['grp'=1,'row'=32] {'row'}, dimensions={0} | all-to-all | bytes 262144 | tf_op jit(solution)/shard_map/all_to_all | solution.py:576
  55.7 0.0 copy-done.2
  55.7 0.0 copy-done.4
  55.7 4.3 %last.1 = (f32[4,384]{1,0:T(4,128)}, f32[4,9]{1,0:T(4,128)}, f32[3,4]{1,0:T(4,128)}) custom-call(bf16[256,256]{1,0:T(8,128)(2,1)S(1)} %bitcast.18, bf16[4,128,128]{2,1,0:T(8,128)(2,1)S(1)} %get-tuple-element.44.half_ref, f32[64,128]{1,0:T(8,128)S(1)} %get-tuple-element.45.bias_ref, f32[8,384]{1,0:T(8,128)S(1)} %get-tuple-element.46.state_ref, ...), custom_call_target="tpu_custom_call" | custom-call | tf_op jit(solution)/shard_map/last/pallas_call | solution.py:551
  (1 shorter events, 0.0 us)
Async XLA Ops:
  4.1 24.8 %copy-start.10 = (f32[8,128]{1,0:T(8,128)S(1)}, f32[8,128]{1,0:T(8,128)}, u32[]{:S(2)}) copy-start(f32[8,128]{1,0:T(8,128)} %get-tuple-element.29.frame_any) | copy-start | bytes 12292
  4.1 20.5 %all-to-all-start = ((bf16[32,8,768]{2,1,0:T(8,128)(2,1)}), bf16[32,8,768]{2,1,0:T(8,128)(2,1)S(1)}, u32[]{:S(2)}, u32[]{:S(2)}) async-start(bf16[32,8,768]{2,1,0:T(8,128)(2,1)} %bitcast.23), calls=%async_computation | async-start | bytes 786432 | tf_op jit(solution)/shard_map/all_to_all | solution.py:576
  13.6 15.4 %copy-start.7 = (f32[16,128]{1,0:T(8,128)S(1)}, f32[16,128]{1,0:T(8,128)}, u32[]{:S(2)}) copy-start(f32[16,128]{1,0:T(8,128)} %pad.4.columns_any) | copy-start | bytes 24580
  13.6 23.6 %copy-start = (bf16[2112,384]{1,0:T(8,128)(2,1)S(1)}, bf16[2112,384]{1,0:T(8,128)(2,1)}, u32[]{:S(2)}) copy-start(bf16[2112,384]{1,0:T(8,128)(2,1)} %out_weight_any.3) | copy-start | bytes 4866052
  13.6 23.6 %copy-start.3 = (f32[4,128,128]{2,1,0:T(8,128)S(1)}, f32[4,128,128]{2,1,0:T(8,128)}, u32[]{:S(2)}) copy-start(f32[4,128,128]{2,1,0:T(8,128)} %pair_any.5) | copy-start | bytes 786436
  13.6 23.6 %copy-start.8 = (f32[4,384]{1,0:T(4,128)S(1)}, f32[4,384]{1,0:T(4,128)}, u32[]{:S(2)}) copy-start(f32[4,384]{1,0:T(4,128)} %single_any.5) | copy-start | bytes 18436
  13.6 23.6 %copy-start.9 = (f32[384,6]{0,1:T(8,128)S(1)}, f32[384,6]{0,1:T(8,128)}, u32[]{:S(2)}) copy-start(f32[384,6]{0,1:T(8,128)} %param.27) | copy-start | bytes 27652
  26.3 10.9 %all-to-all-start.1 = ((bf16[32,8,256]{2,1,0:T(8,128)(2,1)}), bf16[32,8,256]{2,1,0:T(8,128)(2,1)S(1)}, u32[]{:S(2)}, u32[]{:S(2)}) async-start(bf16[32,8,256]{2,1,0:T(8,128)(2,1)} %bitcast.5), calls=%async_computation.1 | async-start | bytes 262144 | tf_op jit(solution)/shard_map/all_to_all | solution.py:576
  29.0 1.2 %copy-start.1 = (bf16[384,1152]{1,0:T(8,128)(2,1)S(1)}, bf16[384,1152]{1,0:T(8,128)(2,1)}, u32[]{:S(2)}) copy-start(bf16[384,1152]{1,0:T(8,128)(2,1)} %get-tuple-element.39.key_any) | copy-start | bytes 2654212
  30.1 0.9 %copy-start.6 = (f32[64,768]{1,0:T(8,128)S(1)}, f32[64,768]{1,0:T(8,128)}, u32[]{:S(2)}) copy-start(f32[64,768]{1,0:T(8,128)} %get-tuple-element.37.rows_any) | copy-start | bytes 589828
  31.1 0.8 %copy-start.14 = (f32[64,128]{1,0:T(8,128)S(1)}, f32[64,128]{1,0:T(8,128)}, u32[]{:S(2)}) copy-start(f32[64,128]{1,0:T(8,128)} %get-tuple-element.38.lengths_any) | copy-start | bytes 98308
  33.6 0.6 copy-start.12
  34.2 21.5 %copy-start.2 = (bf16[384,1152]{1,0:T(8,128)(2,1)S(1)}, bf16[384,1152]{1,0:T(8,128)(2,1)}, u32[]{:S(2)}) copy-start(bf16[384,1152]{1,0:T(8,128)(2,1)} %get-tuple-element.39.key_any) | copy-start | bytes 2654212
  34.2 21.5 %copy-start.4 = (bf16[384,384]{1,0:T(8,128)(2,1)S(1)}, bf16[384,384]{1,0:T(8,128)(2,1)}, u32[]{:S(2)}) copy-start(bf16[384,384]{1,0:T(8,128)(2,1)} %get-tuple-element.48.query_any) | copy-start | bytes 884740
  37.2 1.0 %copy-start.5 = (f32[4,128,128]{2,1,0:T(8,128)S(1)}, f32[4,128,128]{2,1,0:T(8,128)}, u32[]{:S(2)}) copy-start(f32[4,128,128]{2,1,0:T(8,128)} %get-tuple-element.36.gate_any) | copy-start | bytes 786436
  38.1 0.8 %copy-start.11 = (bf16[128,128]{1,0:T(8,128)(2,1)S(1)}, bf16[128,128]{1,0:T(8,128)(2,1)}, u32[]{:S(2)}) copy-start(bf16[128,128]{1,0:T(8,128)(2,1)} %tri_out_any.1) | copy-start | bytes 98308
  38.9 0.8 %copy-start.13 = (f32[64,128]{1,0:T(8,128)S(1)}, f32[64,128]{1,0:T(8,128)}, u32[]{:S(2)}) copy-start(f32[64,128]{1,0:T(8,128)} %copy-done.12) | copy-start | bytes 98308
  39.7 0.7 %copy-start.15 = (f32[128,12]{0,1:T(8,128)S(1)}, f32[128,12]{0,1:T(8,128)}, u32[]{:S(2)}) copy-start(f32[128,12]{0,1:T(8,128)} %param.23) | copy-start | bytes 18436

commit v3 on v2

--- a/solution.py
+++ b/solution.py
@@ -379,12 +379,22 @@
     return jnp.concatenate([single_ref[...], jnp.zeros((IP - r, CS), f32)], axis=0)
 
 
+PACK_ROWS = 216
+TRI_OUT, BIAS, COLUMNS, FRAME_WEIGHT, STATE, FRAME = 0, 128, 144, 160, 184, 208
+
+
+def wide(pack_ref, first):
+    return jnp.concatenate([pack_ref[first + IP * part : first + IP * (part + 1)] for part in range(3)], axis=1)
+
+
 def own_kernel(
-    pair_any, tri_any, qkv_any, single_any, frame_any, columns_any,
-    gate_ref, key_ref, query_ref, rows_ref, lengths_ref,
-    pair_ref, gate_weight_ref, qkv_ref, single_ref, frame_ref, columns_ref, sems,
+    pair_any, tri_any, qkv_any, single_any, frame_any, columns_any, tri_out_any, bias_weight_any, frame_weight_any,
+    gate_ref, key_ref, query_ref, rows_ref, pack_ref, pair_copy_any,
+    pair_ref, gate_weight_ref, qkv_ref, single_ref, tri_out_ref, bias_weight_ref, frame_weight_ref, sems,
 ):
     r, count, _ = pair_ref.shape
+    frame_ref = pack_ref.at[FRAME : FRAME + IP]
+    columns_ref = pack_ref.at[COLUMNS : COLUMNS + HP]
     for copy in copies(
         sems,
         (pair_any, pair_ref),
@@ -393,8 +403,23 @@
         (single_any, single_ref),
         (frame_any, frame_ref),
         (columns_any, columns_ref),
+        (tri_out_any, tri_out_ref),
+        (bias_weight_any, bias_weight_ref),
+        (frame_weight_any, frame_weight_ref),
     ):
         copy.wait()
+    back = pltpu.make_async_copy(pair_ref, pair_copy_any, sems.at[9])
+    back.start()
+    pack_ref[TRI_OUT : TRI_OUT + CH, :] = tri_out_ref[...].astype(f32)
+    bias_weight = bias_weight_ref[...]
+    pack_ref[BIAS : BIAS + HP, :] = jnp.concatenate([bias_weight, jnp.zeros((HP - H, CH), f32)], axis=0)
+    state = pad_state(single_ref)
+    frame_weight = frame_weight_ref[...]
+    frame_weight = jnp.concatenate([frame_weight, jnp.zeros((IP - 6, CS), f32)], axis=0)
+    for part in range(3):
+        lanes = slice(128 * part, 128 * (part + 1))
+        pack_ref[FRAME_WEIGHT + IP * part : FRAME_WEIGHT + IP * (part + 1), :] = frame_weight[:, lanes]
+        pack_ref[STATE + IP * part : STATE + IP * (part + 1), :] = state[:, lanes]
     width = H * CHEAD
     start = 3 * width
     points = H * PQ
@@ -409,96 +434,63 @@
     for a in range(3):
         key_ref[:, 512 + 256 * a : 640 + 256 * a] = padded(start + (3 + a) * points, points, 128)
         key_ref[:, 384 + 256 * a : 512 + 256 * a] = padded(start + 6 * points + a * H * PV, H * PV, 128)
-    rows, lengths = own_side(r, pad_state(single_ref), frame_ref[...], query_ref[...], columns_ref[...])
-    rows_ref[...] = rows
-    lengths_ref[...] = jnp.broadcast_to(lengths, lengths_ref.shape)
+    rows, lengths = own_side(r, state, frame_ref[...], query_ref[...], columns_ref[...])
+    rows_ref[:, 0:768] = rows
+    rows_ref[:, 768:896] = jnp.broadcast_to(lengths, (r * HP, 128))
     for i in range(r):
         normed = layer_norm(pair_ref[i]).astype(bf16)
-        gate_ref[i] = jax.nn.sigmoid(dot(normed, gate_weight_ref[...]))
-
-
-def prepare_kernel(
-    w, n, r, recv_any, frame_any, rows_any, lengths_any, key_any, columns_any, logits_ref, values_ref,
-    recv_ref, frame_ref, rows_ref, lengths_ref, key_ref, columns_ref, sems,
-):
-    lanes = recv_ref.shape[1]
-    for copy in copies(
-        sems,
-        (recv_any.at[:, r * n * r : r * n * r + lanes], recv_ref),
-        (frame_any, frame_ref),
-        (rows_any, rows_ref),
-        (lengths_any, lengths_ref),
-        (key_any, key_ref),
-        (columns_any, columns_ref),
-    ):
-        copy.wait()
-    slots = natural_rows(recv_ref, 0, w, r, n)
+        gate_ref[i] = jax.nn.sigmoid(dot(normed, gate_weight_ref[...])).astype(bf16)
+    back.wait()
+
+
+def prepare_kernel(w, n, r, recv_ref, rows_ref, key_ref, pack_ref, logits_ref, values_ref):
+    slots = natural_rows(recv_ref, r * n * r, w, r, n)
     logits, values = logits_and_values(
-        r, slots, (rows_ref[...], lengths_ref[:, 0:1]), frame_ref[...], key_ref[...], columns_ref[...]
+        r, slots, (rows_ref[:, 0:768], rows_ref[:, 768:769]), pack_ref[FRAME : FRAME + IP], key_ref[...],
+        pack_ref[COLUMNS : COLUMNS + HP],
     )
     logits_ref[...] = logits
     values_ref[...] = values
 
 
 def update_kernel(
-    w, n, recv_any, tri_out_any, pair_any, gate_any, bias_weight_any, logits_any, values_any, single_any, frame_any,
-    out_weight_any, frame_weight_any, pair_out_any, half_ref, bias_ref, state_ref, new_frame_ref, send_ref,
-    recv_ref, tri_out_ref, pair_ref, gate_ref, bias_weight_ref, logits_ref, values_ref, single_ref, frame_ref,
-    out_weight_ref, frame_weight_ref, pair_out_ref, sems,
+    w, n, recv_ref, pair_any, gate_ref, logits_ref, values_ref, pack_ref, out_weight_ref,
+    pair_out_any, half_ref, bias_ref, state_ref, new_frame_ref, send_ref, pair_ref, sems,
 ):
     r, count, _ = pair_ref.shape
-    bias_weight_ref[...] = jnp.zeros_like(bias_weight_ref)
-    loads = copies(
-        sems,
-        (recv_any, recv_ref),
-        (tri_out_any, tri_out_ref),
-        (pair_any, pair_ref),
-        (gate_any, gate_ref),
-        (bias_weight_any, bias_weight_ref.at[0:H]),
-        (logits_any, logits_ref),
-        (values_any, values_ref),
-        (single_any, single_ref),
-        (frame_any, frame_ref),
-        (out_weight_any, out_weight_ref),
-        (frame_weight_any, frame_weight_ref),
-    )
+    load = pltpu.make_async_copy(pair_any, pair_ref, sems.at[r])
+    load.start()
     half = r // 2
     row, column = grid_of((2 * CH, 2 * CH))
     c = row & (CH - 1)
     take = onehot(column == (c >> log2(w)) * 2 * w + (row >> log2(CH)) * w + (c & (w - 1)))
-    loads[0].wait()
     product = dot(take, recv_ref[...])
+    tri_out = pack_ref[TRI_OUT : TRI_OUT + CH, :].astype(bf16)
+    updates = []
+    for high in range(2):
+        normed = layer_norm(product[high * CH : (high + 1) * CH], axis=0).astype(bf16)
+        updates.append(dot_tn(normed, tri_out))
+    load.wait()
     biases = []
     halves = []
     stores = []
-    for copy in loads[1:5]:
-        copy.wait()
-    for high in range(2):
-        normed = layer_norm(product[high * CH : (high + 1) * CH], axis=0).astype(bf16)
-        update = dot_tn(normed, tri_out_ref[...])
-        for low in range(half):
-            i = high * half + low
-            pair_out = pair_ref[i] + gate_ref[i] * update[low * count : (low + 1) * count]
-            pair_out_ref[i] = pair_out
-            store = pltpu.make_async_copy(pair_out_ref.at[i], pair_out_any.at[i], sems.at[11 + i])
-            store.start()
-            stores.append(store)
-            normed_pair = layer_norm(pair_out)
-            biases.append(dot_nt(bias_weight_ref[...], normed_pair, highest) * third)
-            halves.append(normed_pair.astype(bf16))
-            half_ref[i] = halves[-1]
+    for i in range(r):
+        low = i % half
+        update = updates[i // half][low * count : (low + 1) * count]
+        pair_out = pair_ref[i] + gate_ref[i].astype(f32) * update
+        pair_ref[i] = pair_out
+        store = pltpu.make_async_copy(pair_ref.at[i], pair_out_any.at[i], sems.at[i])
+        store.start()
+        stores.append(store)
+        normed_pair = layer_norm(pair_out)
+        biases.append(dot_nt(pack_ref[BIAS : BIAS + HP, :], normed_pair, highest) * third)
+        halves.append(normed_pair.astype(bf16))
+        half_ref[i] = halves[-1]
     bias = jnp.concatenate(biases, axis=0)
     bias_ref[...] = bias
-
-    def weights():
-        loads[9].wait()
-        loads[10].wait()
-        return out_weight_ref[...], frame_weight_ref[...]
-
-    for copy in loads[5:9]:
-        copy.wait()
     state, frame = attend(
-        r, logits_ref[...] + bias, values_ref[...], halves, pad_state(single_ref), frame_ref[...], weights
+        r, logits_ref[...] + bias, values_ref[...], halves, wide(pack_ref, STATE), pack_ref[FRAME : FRAME + IP],
+        lambda: (out_weight_ref[...], wide(pack_ref, FRAME_WEIGHT)),
     )
     state_ref[...] = state
     new_frame_ref[...] = frame
@@ -508,34 +500,20 @@
 
 
 def last_kernel(
-    w, n, recv_ref, half_ref, bias_ref, state_ref, frame_ref, columns_any, query_any, key_any,
-    out_weight_any, frame_weight_any, single_out_ref, rotation_ref, translation_ref,
-    columns_ref, query_ref, key_ref, out_weight_ref, frame_weight_ref, scr, sems,
+    w, n, recv_ref, half_ref, bias_ref, state_ref, frame_ref, pack_ref, query_ref, key_ref, out_weight_ref,
+    single_out_ref, rotation_ref, translation_ref, scr,
 ):
     r = half_ref.shape[0]
-    loads = copies(
-        sems,
-        (query_any, query_ref),
-        (columns_any, columns_ref),
-        (key_any, key_ref),
-        (out_weight_any, out_weight_ref),
-        (frame_weight_any, frame_weight_ref),
-    )
     slots = natural_rows(recv_ref, 0, w, r, n)
     state, frame = state_ref[...], frame_ref[...]
-    loads[0].wait()
-    loads[1].wait()
-    own = own_side(r, state, frame, query_ref[...], columns_ref[...])
-    loads[2].wait()
-    logits, values = logits_and_values(r, slots, own, frame, key_ref[...], columns_ref[...])
-
-    def weights():
-        loads[3].wait()
-        loads[4].wait()
-        return out_weight_ref[...], frame_weight_ref[...]
-
+    columns = pack_ref[COLUMNS : COLUMNS + HP]
+    own = own_side(r, state, frame, query_ref[...], columns)
+    logits, values = logits_and_values(r, slots, own, frame, key_ref[...], columns)
     halves = [half_ref[i] for i in range(r)]
-    state, frame = attend(r, logits + bias_ref[...], values, halves, state, frame, weights)
+    state, frame = attend(
+        r, logits + bias_ref[...], values, halves, state, frame,
+        lambda: (out_weight_ref[...], wide(pack_ref, FRAME_WEIGHT)),
+    )
     single_out_ref[...] = state[0:r]
     rotation_ref[...] = frame[0:r, 0:9]
     scr[...] = jnp.concatenate([frame, jnp.zeros((128 - IP, 128), f32)], axis=0).T
@@ -544,17 +522,17 @@
 
 VMEM = pl.BlockSpec(memory_space=pltpu.VMEM)
 HBM = pl.BlockSpec(memory_space=pltpu.HBM)
-FREE = pl.BlockSpec(memory_space=pl.ANY)
-
-
-def call(body, name, outs, args, outside=(), outside_outs=(), free=(), scratch=(), limit=32, flops=0, moved=0):
+
+
+def call(body, name, outs, args, outside=(), outside_outs=(), scratch=(), limit=32, alias=None, flops=0, moved=0):
     return pl.pallas_call(
         body,
         name=name,
         out_shape=[jax.ShapeDtypeStruct(s, d) for s, d in outs],
-        in_specs=[FREE if at in free else HBM if at in outside else VMEM for at in range(len(args))],
+        in_specs=[HBM if at in outside else VMEM for at in range(len(args))],
         out_specs=[HBM if at in outside_outs else VMEM for at in range(len(outs))],
         scratch_shapes=list(scratch),
+        input_output_aliases=alias or {},
         compiler_params=pltpu.CompilerParams(vmem_limit_bytes=limit * 2**20),
         cost_estimate=pl.CostEstimate(flops=flops, bytes_accessed=moved, transcendentals=0),
     )(*args)
@@ -604,27 +582,36 @@
     point_weight = head_gamma * (math.sqrt(2.0 / (9.0 * PQ)) * 0.5 * third)
     columns = jnp.stack([point_weight, chain_bias[0], chain_bias[1]], axis=1)
     columns = jnp.pad(columns, ((0, HP - H), (0, 125)))
-    gate, key_weight, query_weight, query_rows, lengths = call(
+    gate, key_weight, query_weight, query_rows, pack, pair_copy = call(
         own_kernel,
         "own",
         [
-            ((r, count, CH), f32),
+            ((r, count, CH), bf16),
             ((CS, 1152), bf16),
             ((CS, 384), bf16),
-            ((r * HP, 768), f32),
-            ((r * HP, 128), f32),
+            ((r * HP, 896), f32),
+            ((PACK_ROWS, 128), f32),
+            (pair.shape, f32),
         ],
-        [pair, tri_weight, qkv_weight, single, frame, columns],
-        outside=range(6),
+        [pair, tri_weight, qkv_weight, single, frame, columns, tri_out_weight, bias_weight.T, frame_weight.T],
+        outside=range(9),
+        outside_outs=(5,),
         scratch=[
-            like(pair), pltpu.VMEM((CH, CH), bf16), like(qkv_weight), like(single), like(frame), like(columns), dma((6,))
+            like(pair),
+            pltpu.VMEM((CH, CH), bf16),
+            like(qkv_weight),
+            like(single),
+            like(tri_out_weight),
+            pltpu.VMEM((H, CH), f32),
+            pltpu.VMEM((6, CS), f32),
+            dma((10,)),
         ],
         limit=60,
         flops=2 * r * count * CH * CH,
         moved=16 * 2**20,
     )
-    received, gate, key_weight, query_weight, query_rows, lengths = lax.optimization_barrier(
-        (received, gate, key_weight, query_weight, query_rows, lengths)
+    received, gate, key_weight, query_weight, query_rows, pack, pair_copy = lax.optimization_barrier(
+        (received, gate, key_weight, query_weight, query_rows, pack, pair_copy)
     )
     (formed,) = call(
         functools.partial(product_kernel, w, n, r),
@@ -638,23 +625,11 @@
         functools.partial(prepare_kernel, w, n, r),
         "prepare",
         [((r * HP, count), f32), ((count, 640), f32)],
-        [received, frame, query_rows, lengths, key_weight, columns],
-        outside=range(6),
-        free=(0,),
-        scratch=[
-            pltpu.VMEM((n * rows, lanes), bf16),
-            like(frame),
-            like(query_rows),
-            like(lengths),
-            like(key_weight),
-            like(columns),
-            dma((6,)),
-        ],
+        [received, query_rows, key_weight, pack],
         limit=limit,
-        flops=2 * count * CS * 1280,
+        flops=2 * count * CS * 1152,
         moved=8 * 2**20,
     )
-    frame_weight = frame_weight.T
     pair_out, pair_half, bias, state, frame, sent = call(
         functools.partial(update_kernel, w, n),
         "update",
@@ -666,25 +641,11 @@
             ((IP, 128), f32),
             ((n * rows, lanes), bf16),
         ],
-        [products, tri_out_weight, pair, gate, bias_weight.T, logits, values, single, frame, out_weight, frame_weight],
-        outside=range(11),
-        free=(0,),
+        [products, pair_copy, gate, logits, values, pack, out_weight],
+        outside=(1,),
         outside_outs=(0,),
-        scratch=[
-            like(products),
-            like(tri_out_weight),
-            like(pair),
-            like(gate),
-            pltpu.VMEM((HP, CH), f32),
-            like(logits),
-            like(values),
-            like(single),
-            like(frame),
-            like(out_weight),
-            like(frame_weight),
-            like(pair),
-            dma((r + 11,)),
-        ],
+        alias={1: 0},
+        scratch=[like(pair), dma((r + 1,))],
         limit=limit,
     )
     received = exchange(sent)
@@ -692,17 +653,8 @@
         functools.partial(last_kernel, w, n),
         "last",
         [((r, CS), f32), ((r, 9), f32), ((3, r), f32)],
-        [received, pair_half, bias, state, frame, columns, query_weight, key_weight, out_weight, frame_weight],
-        outside=range(5, 10),
-        scratch=[
-            like(columns),
-            like(query_weight),
-            like(key_weight),
-            like(out_weight),
-            like(frame_weight),
-            pltpu.VMEM((128, 128), f32),
-            dma((5,)),
-        ],
+        [received, pair_half, bias, state, frame, pack, query_weight, key_weight, out_weight],
+        scratch=[pltpu.VMEM((128, 128), f32)],
         limit=limit,
     )
     return (pair_out, single_out, rotation.T, translation)

time: 60.7 us -> 55.2 us (0.909)
  local copies, waits for them, and re-layouts: 8.08 us -> 4.48 us
  Pallas kernels: 18.9 us -> 17.3 us
  waiting for transfers between devices: 10.6 us -> 11.6 us
  blocking collectives: 11 us -> 10.1 us
    unnamed x32 -> x16, local copies, waits for them, and re-layouts: 6.63 us -> 3.02 us
    pallas_call x6, Pallas kernels: 18.9 us -> 17.3 us  [call(): pl.pallas_call(body, name=name, out_shape=[jax.ShapeDtypeStruct(s, d) for...]
    all_to_all x1, blocking collectives: 11 us -> 10.1 us  [exchange(): got = lax.all_to_all(sent.reshape(n, rows, width), 'row', 0, 0, tiled=True)]
    all_to_all x2, waiting for transfers between devices: 10.6 us -> 11.6 us  [exchange(): got = lax.all_to_all(sent.reshape(n, rows, width), 'row', 0, 0, tiled=True)]
  transfers between devices with their start and end apart: 2 -> 2, of which waited for: 2 -> 2; matrix products, arithmetic and copies ran while one was open for 4% -> 4% of each run, Pallas kernels for 9% -> 8%
where the time goes in v3:
time: 55.2 us; the launch traced here: 54.8 us
  Pallas kernels  17.3 us (31%)
  waiting for transfers between devices  11.6 us (21%)
  blocking collectives  10.1 us (18%)
  starting transfers between devices  9.94 us (18%)
  local copies, waits for them, and re-layouts  4.48 us (8%)
  between operations  0.73 us (1%)
  other arithmetic  0.67 us (1%)
    pallas_call x6, Pallas kernels, call(): pl.pallas_call(body, name=name, out_shape=[jax.ShapeDtypeStruct(s, d) for...  17.3 us
    all_to_all x2, waiting for transfers between devices, exchange(): got = lax.all_to_all(sent.reshape(n, rows, width), 'row', 0, 0, tiled=True)  11.6 us
    all_to_all x1, blocking collectives, exchange(): got = lax.all_to_all(sent.reshape(n, rows, width), 'row', 0, 0, tiled=True)  10.1 us
    all_to_all x2, starting transfers between devices, exchange(): got = lax.all_to_all(sent.reshape(n, rows, width), 'row', 0, 0, tiled=True)  9.94 us
    unnamed x16, local copies, waits for them, and re-layouts  3.02 us
  transfers between devices with their start and end apart: 2, of which 2 were waited for; matrix products, arithmetic and copies ran while one was open for 4% of the time, Pallas kernels for 8%

profile of v3, /device:TPU:0, one launch (start us, length us, event | category | flops | bytes accessed | tf_op | source)
XLA Modules:
  0.0 54.8 jit_solution(9164923646942920533)
XLA Ops:
  0.6 3.5 %gate.1 = (bf16[256,768]{1,0:T(8,128)(2,1)}, f32[8,128]{1,0:T(8,128)}) custom-call(f32[4,128,128]{2,1,0:T(8,128)} %pair_any.3, bf16[128,640]{1,0:T(8,128)(2,1)} %tri_any.3, f32[4,384]{1,0:T(4,128)} %single_any.3, f32[3,4]{1,0:T(4,128)} %quats_any.1, f32[3,4]{1,0:T(4,128)} %translate_any.1, s32[4]{0:T(128)} %mask_any.1, s32[4]{0:T(128)} %chain_any.1), custom_call_target="tpu_custom_call" | custom-call | tf_op jit(solution)/shard_map/gate/pallas_call | solution.py:528
  4.2 7.3 %all-to-all-start = ((bf16[32,8,768]{2,1,0:T(8,128)(2,1)}), bf16[32,8,768]{2,1,0:T(8,128)(2,1)S(1)}, u32[]{:S(2)}, u32[]{:S(2)}) async-start(bf16[32,8,768]{2,1,0:T(8,128)(2,1)} %bitcast.20), calls=%async_computation | async-start | bytes 786432 | tf_op jit(solution)/shard_map/all_to_all | solution.py:554
  11.5 0.7 %multiply_bitcast_fusion = f32[12,1]{0,1:T(1,128)S(1)} fusion(f32[12]{0:T(128)} %param.24), kind=kLoop, calls=%fused_computation.3 | loop fusion | flops 12 | bytes 96 | tf_op jit(solution)/shard_map/stack | solution.py:583
  12.1 0.8 %slice_bitcast_fusion.1 = (f32[12,1]{0,1:T(1,128)S(1)}, f32[12,1]{0,1:T(1,128)S(1)}) fusion(f32[2,12]{1,0:T(2,128)} %param.25), kind=kLoop, calls=%fused_computation.2 | loop fusion | bytes 192 | tf_op jit(solution)/shard_map/stack;squeeze | solution.py:583
  12.9 0.1 copy.22
  13.0 0.6 %pad.4.columns_any = f32[16,128]{1,0:T(8,128)} pad(f32[12,3]{1,0:T(8,128)S(1)} %copy.22, f32[]{:T(128)} %constant.4.clone.1), padding=0_4x0_125 | pad | bytes 8340 | tf_op jit(solution)/shard_map/jit(_pad)/pad | solution.py:584
  13.6 0.0 copy-start
  13.6 3.4 %own.1 = (bf16[4,128,128]{2,1,0:T(8,128)(2,1)}, bf16[384,1152]{1,0:T(8,128)(2,1)}, bf16[384,384]{1,0:T(8,128)(2,1)}, f32[64,896]{1,0:T(8,128)}, f32[216,128]{1,0:T(8,128)}, /*index=5*/f32[4,128,128]{2,1,0:T(8,128)}) custom-call(f32[4,128,128]{2,1,0:T(8,128)} %pair_any.3, bf16[128,640]{1,0:T(8,128)(2,1)} %tri_any.3, bf16[384,1152]{1,0:T(8,128)(2,1)} %qkv_any.1, ...), custom_call_target="tpu_custom_call" | custom-call | flops 16777216 | bytes 16777216 | tf_op jit(solution)/shard_map/own/pallas_call | solution.py:528
  17.0 0.0 copy-start.4
  17.0 0.0 copy-start.7
  17.0 7.6 %all-to-all-done = bf16[32,8,768]{2,1,0:T(8,128)(2,1)S(1)} async-done(((bf16[32,8,768]{2,1,0:T(8,128)(2,1)}), bf16[32,8,768]{2,1,0:T(8,128)(2,1)S(1)}, u32[]{:S(2)}, u32[]{:S(2)}) %all-to-all-start) | async-done | bytes 393248 | tf_op jit(solution)/shard_map/all_to_all | solution.py:554
  24.6 1.7 %product.1 = bf16[256,256]{1,0:T(8,128)(2,1)} custom-call(bf16[256,768]{1,0:T(8,128)(2,1)S(1)} %bitcast.15), custom_call_target="tpu_custom_call" | custom-call | tf_op jit(solution)/shard_map/product/pallas_call | solution.py:528
  26.3 2.6 %all-to-all-start.1 = ((bf16[32,8,256]{2,1,0:T(8,128)(2,1)}), bf16[32,8,256]{2,1,0:T(8,128)(2,1)S(1)}, u32[]{:S(2)}, u32[]{:S(2)}) async-start(bf16[32,8,256]{2,1,0:T(8,128)(2,1)} %bitcast.7), calls=%async_computation.1 | async-start | bytes 262144 | tf_op jit(solution)/shard_map/all_to_all | solution.py:554
  28.9 0.0 copy-start.1
  29.0 1.2 %copy-done.1 = bf16[384,1152]{1,0:T(8,128)(2,1)S(1)} copy-done((bf16[384,1152]{1,0:T(8,128)(2,1)S(1)}, bf16[384,1152]{1,0:T(8,128)(2,1)}, u32[]{:S(2)}) %copy-start.1) | copy-done | bytes 884760
  30.1 0.0 copy-start.3
  30.1 0.9 %copy-done.3 = f32[216,128]{1,0:T(8,128)S(1)} copy-done((f32[216,128]{1,0:T(8,128)S(1)}, f32[216,128]{1,0:T(8,128)}, u32[]{:S(2)}) %copy-start.3) | copy-done | bytes 110616
  31.0 0.0 copy-start.6
  31.0 0.9 %copy-done.6 = f32[64,896]{1,0:T(8,128)S(1)} copy-done((f32[64,896]{1,0:T(8,128)S(1)}, f32[64,896]{1,0:T(8,128)}, u32[]{:S(2)}) %copy-start.6) | copy-done | bytes 229400
  32.0 1.2 %prepare.1 = (f32[64,128]{1,0:T(8,128)S(1)}, f32[128,640]{1,0:T(8,128)S(1)}) custom-call(bf16[256,768]{1,0:T(8,128)(2,1)S(1)} %bitcast.16, f32[64,896]{1,0:T(8,128)S(1)} %copy-done.6, bf16[384,1152]{1,0:T(8,128)(2,1)S(1)} %copy-done.1, f32[216,128]{1,0:T(8,128)S(1)} %copy-done.3), custom_call_target="tpu_custom_call" | custom-call | flops 113246208 | bytes 8388608 | tf_op jit(solution)/shard_map/prepare/pallas_call | solution.py:528
  33.2 0.0 copy-start.2
  33.2 0.0 copy-start.5
  33.2 4.0 %all-to-all-done.1 = bf16[32,8,256]{2,1,0:T(8,128)(2,1)S(1)} async-done(((bf16[32,8,256]{2,1,0:T(8,128)(2,1)}), bf16[32,8,256]{2,1,0:T(8,128)(2,1)S(1)}, u32[]{:S(2)}, u32[]{:S(2)}) %all-to-all-start.1) | async-done | bytes 131104 | tf_op jit(solution)/shard_map/all_to_all | solution.py:554
  37.2 0.0 copy-done
  37.2 0.0 copy-done.4
  37.2 0.0 copy-done.7
  37.2 4.1 %update.1 = (f32[4,128,128]{2,1,0:T(8,128)}, bf16[4,128,128]{2,1,0:T(8,128)(2,1)S(1)}, f32[64,128]{1,0:T(8,128)S(1)}, f32[8,384]{1,0:T(8,128)S(1)}, f32[8,128]{1,0:T(8,128)S(1)}, /*index=5*/bf16[256,256]{1,0:T(8,128)(2,1)S(1)}) custom-call(bf16[256,256]{1,0:T(8,128)(2,1)S(1)} %bitcast.17, ...), custom_call_target="tpu_custom_call", output_to_operand_aliasing={{0}: (1, {})} | custom-call | tf_op jit(solution)/shard_map/update/pallas_call | solution.py:528
  41.3 10.1 %all_to_all.15 = bf16[32,8,256]{2,1,0:T(8,128)(2,1)S(1)} all-to-all(bf16[32,8,256]{2,1,0:T(8,128)(2,1)S(1)} %bitcast.19), channel_id=1, replica_groups=mesh['grp'=1,'row'=32] {'row'}, dimensions={0} | all-to-all | bytes 262144 | tf_op jit(solution)/shard_map/all_to_all | solution.py:554
  51.4 0.0 copy-done.2
  51.4 0.0 copy-done.5
  51.4 3.4 %last.1 = (f32[4,384]{1,0:T(4,128)}, f32[4,9]{1,0:T(4,128)}, f32[3,4]{1,0:T(4,128)}) custom-call(bf16[256,256]{1,0:T(8,128)(2,1)S(1)} %bitcast.18, bf16[4,128,128]{2,1,0:T(8,128)(2,1)S(1)} %get-tuple-element.48.half_ref, f32[64,128]{1,0:T(8,128)S(1)} %get-tuple-element.49.bias_ref, f32[8,384]{1,0:T(8,128)S(1)} %get-tuple-element.50.state_ref, ...), custom_call_target="tpu_custom_call" | custom-call | tf_op jit(solution)/shard_map/last/pallas_call | solution.py:528
  (1 shorter events, 0.0 us)
Async XLA Ops:
  4.2 20.5 %all-to-all-start = ((bf16[32,8,768]{2,1,0:T(8,128)(2,1)}), bf16[32,8,768]{2,1,0:T(8,128)(2,1)S(1)}, u32[]{:S(2)}, u32[]{:S(2)}) async-start(bf16[32,8,768]{2,1,0:T(8,128)(2,1)} %bitcast.20), calls=%async_computation | async-start | bytes 786432 | tf_op jit(solution)/shard_map/all_to_all | solution.py:554
  13.6 23.6 %copy-start = (bf16[2112,384]{1,0:T(8,128)(2,1)S(1)}, bf16[2112,384]{1,0:T(8,128)(2,1)}, u32[]{:S(2)}) copy-start(bf16[2112,384]{1,0:T(8,128)(2,1)} %out_weight_ref.3) | copy-start | bytes 4866052
  17.0 20.2 %copy-start.4 = (f32[216,128]{1,0:T(8,128)S(1)}, f32[216,128]{1,0:T(8,128)}, u32[]{:S(2)}) copy-start(f32[216,128]{1,0:T(8,128)} %get-tuple-element.43.pack_ref) | copy-start | bytes 331780
  17.0 20.2 %copy-start.7 = (bf16[4,128,128]{2,1,0:T(8,128)(2,1)S(1)}, bf16[4,128,128]{2,1,0:T(8,128)(2,1)}, u32[]{:S(2)}) copy-start(bf16[4,128,128]{2,1,0:T(8,128)(2,1)} %get-tuple-element.40.gate_ref) | copy-start | bytes 393220
  26.3 10.9 %all-to-all-start.1 = ((bf16[32,8,256]{2,1,0:T(8,128)(2,1)}), bf16[32,8,256]{2,1,0:T(8,128)(2,1)S(1)}, u32[]{:S(2)}, u32[]{:S(2)}) async-start(bf16[32,8,256]{2,1,0:T(8,128)(2,1)} %bitcast.7), calls=%async_computation.1 | async-start | bytes 262144 | tf_op jit(solution)/shard_map/all_to_all | solution.py:554
  28.9 1.2 %copy-start.1 = (bf16[384,1152]{1,0:T(8,128)(2,1)S(1)}, bf16[384,1152]{1,0:T(8,128)(2,1)}, u32[]{:S(2)}) copy-start(bf16[384,1152]{1,0:T(8,128)(2,1)} %get-tuple-element.42.key_ref) | copy-start | bytes 2654212
  30.1 0.9 %copy-start.3 = (f32[216,128]{1,0:T(8,128)S(1)}, f32[216,128]{1,0:T(8,128)}, u32[]{:S(2)}) copy-start(f32[216,128]{1,0:T(8,128)} %get-tuple-element.43.pack_ref) | copy-start | bytes 331780
  31.0 0.9 %copy-start.6 = (f32[64,896]{1,0:T(8,128)S(1)}, f32[64,896]{1,0:T(8,128)}, u32[]{:S(2)}) copy-start(f32[64,896]{1,0:T(8,128)} %get-tuple-element.41.rows_ref) | copy-start | bytes 688132
  33.2 18.2 %copy-start.2 = (bf16[384,1152]{1,0:T(8,128)(2,1)S(1)}, bf16[384,1152]{1,0:T(8,128)(2,1)}, u32[]{:S(2)}) copy-start(bf16[384,1152]{1,0:T(8,128)(2,1)} %get-tuple-element.42.key_ref) | copy-start | bytes 2654212
  33.2 18.2 %copy-start.5 = (bf16[384,384]{1,0:T(8,128)(2,1)S(1)}, bf16[384,384]{1,0:T(8,128)(2,1)}, u32[]{:S(2)}) copy-start(bf16[384,384]{1,0:T(8,128)(2,1)} %get-tuple-element.52.query_ref) | copy-start | bytes 884740

commit v4 on v3

--- a/solution.py
+++ b/solution.py
@@ -11,12 +11,12 @@
 CH = 128
 CS = 384
 H = 12
-HP = 16
 CHEAD = 16
 PQ = 4
 PV = 8
 SLOT = 512
 IP = 8
+ROWS = H * IP
 MASK_AT = 12
 CHAIN_AT = 13
 
@@ -88,6 +88,11 @@
 def spread_rows(slots, w, r):
     rows = 2 * w
     lanes = r * SLOT // rows
+    if rows == 8 and r == 4:
+        low, high = slots[0:IP, 0:lanes].astype(f32), slots[0:IP, lanes:].astype(f32)
+        row, _ = grid_of((IP, lanes))
+        one = jnp.where(row < r, low, pltpu.roll(high, r, 0))
+        return jnp.concatenate([one, one], axis=0).astype(bf16)
     x, i = grid_of((16, 16))
     q = x & (rows - 1)
     if lanes <= SLOT:
@@ -163,33 +168,31 @@
     pair_ref, tri_ref, single_ref, quats_ref, translate_ref, mask_ref, chain_ref, scr, sems,
 ):
     r, count, _ = pair_ref.shape
-    big = copies(sems, (tri_any.at[:, 0 : 4 * CH], tri_ref), *((pair_any.at[i], pair_ref.at[i]) for i in range(r)))
-    little = copies(
-        sems.at[r + 1 :],
+    loads = copies(
+        sems,
         (quats_any, quats_ref),
         (translate_any, translate_ref),
         (mask_any, mask_ref),
         (chain_any, chain_ref),
         (single_any, single_ref),
+        (tri_any.at[:, 0 : 4 * CH], tri_ref),
+        (pair_any, pair_ref),
     )
     row, column = grid_of((2 * CH, 2 * CH))
     d = row >> log2(2 * w)
     side = (row >> log2(w)) & 1
     take = onehot(column == side * CH + d * w + (row & (w - 1)))
-    big[0].wait()
+    for load in loads:
+        load.wait()
     gate_weight = jnp.concatenate([tri_ref[:, 0:CH], tri_ref[:, 2 * CH : 3 * CH]], axis=1)
     value_weight = jnp.concatenate([tri_ref[:, CH : 2 * CH], tri_ref[:, 3 * CH : 4 * CH]], axis=1)
     gate_weight = dot_nt(take, gate_weight).astype(bf16)
     value_weight = dot_nt(take, value_weight).astype(bf16)
-    for copy in little:
-        copy.wait()
-    for i in range(r):
-        big[1 + i].wait()
-        normed = layer_norm(pair_ref[i]).astype(bf16)
-        gates = dot_nt(gate_weight, normed)
-        values = dot_nt(value_weight, normed)
-        side_values = jax.nn.sigmoid(gates) * values * mask_ref[i].astype(f32)
-        send_ref[:, i * count : (i + 1) * count] = side_values.astype(bf16)
+    normed = layer_norm(pair_ref[...].reshape(r * count, CH)).astype(bf16)
+    gates = dot_nt(gate_weight, normed)
+    values = dot_nt(value_weight, normed)
+    mask = jnp.concatenate([jnp.full((1, count), mask_ref[i].astype(f32)) for i in range(r)], axis=1)
+    send_ref[:, 0 : r * count] = (jax.nn.sigmoid(gates) * values * mask).astype(bf16)
 
     scr[...] = jnp.zeros_like(scr)
     quats = quats_ref[...]
@@ -208,8 +211,9 @@
     fill_rows(send_ref, r * count, spread_rows(slots_of(pad_state(single_ref), frame), w, r))
 
 
-def product_kernel(w, n, r, recv_ref, send_ref):
+def product_kernel(w, n, r, recv_ref, send_ref, slots_ref):
     count = n * r
+    slots_ref[...] = recv_ref[:, r * count :]
     rows = 2 * w
     pieces = natural_rows(recv_ref, r * count, w, r, n, CS, SLOT)
     mask = dot_nt(piece_select(16), pieces)[MASK_AT : MASK_AT + 1, :]
@@ -240,55 +244,67 @@
     send_ref[...] = dot(swap_rows(n * rows, n), jnp.concatenate(blocks, axis=0)).astype(bf16)
 
 
-def head_masks():
-    h, lane = grid_of((HP, 256))
-    query_scalar = jnp.where(((lane >> log2(CHEAD)) == h) & (h < H), 1.0, 0.0)
-    value_scalar = jnp.where((((lane - 64) >> log2(CHEAD)) == h) & (h < H), 1.0, 0.0)
-    h, lane = grid_of((HP, 128))
-    query = jnp.where(((lane >> log2(PQ)) == h) & (h < H), 1.0, 0.0)
-    value = jnp.where(((lane >> log2(PV)) == h) & (h < H), 1.0, 0.0)
-    return query_scalar, value_scalar, query, value
-
-
-def own_side(r, state, frame, query_weight, columns):
+def tiles(x):
+    return [x[h * IP : (h + 1) * IP] for h in range(H)]
+
+
+def own_side(state, frame, qkv_ref, point_weight):
     both = jnp.concatenate([state, jnp.zeros_like(state)], axis=0).astype(bf16)
-    own = dot(both, query_weight)[0:IP]
+    own = dot(both, jnp.concatenate([qkv_ref[:, 0:256], qkv_ref[:, 512:768]], axis=1))[0:IP]
     width = H * CHEAD
-    points = H * PQ
-    fill = jnp.zeros((IP, 128 - points), f32)
-    own_local = [
-        jnp.concatenate([own[:, width + a * points : width + (a + 1) * points], fill], axis=1) for a in range(3)
-    ]
-    own_points = []
+    count = H * PQ
+    start = 3 * width - 256
+    fill = jnp.zeros((IP, 128 - count), f32)
+    own_local = [jnp.concatenate([own[:, start + a * count : start + (a + 1) * count], fill], axis=1) for a in range(3)]
+    scalars = jnp.concatenate([jnp.zeros((IP, 256 - width), f32), own[:, 0:width]], axis=1)
+    points = []
     for a in range(3):
-        own_points.append(
+        points.append(
             frame[:, 3 * a : 3 * a + 1] * own_local[0]
             + frame[:, 3 * a + 1 : 3 * a + 2] * own_local[1]
             + frame[:, 3 * a + 2 : 3 * a + 3] * own_local[2]
             + frame[:, 9 + a : 10 + a]
         )
-    query_scalar, _, query_mask, _ = head_masks()
-    weight = columns[:, 0:1]
-    query_rows = []
+    weight = jnp.broadcast_to(point_weight, (IP, 128))
+    length = weight * (points[0] * points[0] + points[1] * points[1] + points[2] * points[2])
+    everything = jnp.concatenate(
+        [scalars * (third / math.sqrt(CHEAD))] + [2.0 * weight * p for p in points] + [-weight], axis=1
+    )
+    _, lane = grid_of((IP, 768))
+    head = jnp.where(lane < 256, (lane - (256 - width)) >> log2(CHEAD), (lane & 127) >> log2(PQ))
+    _, lane = grid_of((IP, 128))
+    rows = []
     lengths = []
-    for i in range(r):
-        scalar = own[i : i + 1, 0:256] * (third / math.sqrt(CHEAD)) * query_scalar
-        points = [p[i : i + 1] * query_mask for p in own_points]
-        query_rows.append(
-            jnp.concatenate([scalar] + [2.0 * weight * p for p in points] + [-weight * query_mask], axis=1)
-        )
-        length = points[0] * points[0] + points[1] * points[1] + points[2] * points[2]
-        lengths.append(-weight * jnp.sum(length, axis=1, keepdims=True))
-    return jnp.concatenate(query_rows, axis=0), jnp.concatenate(lengths, axis=0)
-
-
-def logits_and_values(r, slots, own, frame, key_weight, columns):
+    for h in range(H):
+        rows.append(jnp.where(head == h, everything, 0.0))
+        lengths.append(-jnp.sum(jnp.where((lane >> log2(PQ)) == h, length, 0.0), axis=1, keepdims=True))
+    return jnp.concatenate(rows, axis=0), jnp.concatenate(lengths, axis=0)
+
+
+def logits_and_values(slots, own, frame, qkv, columns):
     query_rows, lengths = own
     pieces = slots[:, CS:SLOT]
     entry = dot(pieces, piece_select(128, True))
     rows = dot_nt(piece_select(16), pieces)
-    keys = dot(slots[:, 0:CS], key_weight)
-    local = [keys[:, 384 + 256 * a : 640 + 256 * a] for a in range(3)]
+    keys = dot(slots[:, 0:CS], qkv)
+    points = H * PQ
+    first = 3 * H * CHEAD + 3 * points
+    _, lane = grid_of((keys.shape[0], 128))
+
+    def block(start, size):
+        at, offset = start // 128 * 128, start % 128
+        one = keys[:, at : at + 128]
+        if offset == 0:
+            return one
+        one = pltpu.roll(one, 128 - offset, 1)
+        if offset + size <= 128:
+            return one
+        return jnp.where(lane < 128 - offset, one, pltpu.roll(keys[:, at + 128 : at + 256], 128 - offset, 1))
+
+    local = []
+    for a in range(3):
+        value_points = block(first + 3 * points + a * H * PV, H * PV)
+        local.append(jnp.concatenate([value_points, block(first + a * points, points)], axis=1))
     placed = []
     for a in range(3):
         placed.append(
@@ -297,29 +313,31 @@
             + entry[:, 3 * a + 2 : 3 * a + 3] * local[2]
             + entry[:, 9 + a : 10 + a]
         )
-    values = jnp.concatenate([keys[:, 128:384]] + [p[:, 0:128] for p in placed], axis=1)
+    values = jnp.concatenate([keys[:, 384:640]] + [p[:, 0:128] for p in placed], axis=1)
     key_points = [p[:, 128:256] for p in placed]
     length = key_points[0] * key_points[0] + key_points[1] * key_points[1] + key_points[2] * key_points[2]
-    key_side = jnp.concatenate([keys[:, 0:256]] + key_points + [length], axis=1)
+    key_side = jnp.concatenate([keys[:, 128:384]] + key_points + [length], axis=1)
     far = mask_fill * (rows[MASK_AT : MASK_AT + 1, :] - 1.0)
-    added = []
-    for i in range(r):
-        same = rows[CHAIN_AT : CHAIN_AT + 1, :] == frame[i : i + 1, CHAIN_AT : CHAIN_AT + 1]
-        added.append(jnp.where(same, columns[:, 2:3], columns[:, 1:2]) + far + lengths[i * HP : (i + 1) * HP])
-    logits = dot_nt(query_rows, key_side, highest)
-    return logits + jnp.concatenate(added, axis=0), values
-
-
-def attend(r, logits, values, pair_half, state, frame, weights):
+    chain = jnp.broadcast_to(rows[CHAIN_AT : CHAIN_AT + 1, :], (IP, rows.shape[1]))
+    chain = jnp.concatenate([chain - frame[:, CHAIN_AT : CHAIN_AT + 1]] * H, axis=0)
+    added = jnp.where(chain == 0.0, columns[:, ROWS + 1 : ROWS + 2], columns[:, ROWS : ROWS + 1]) + far + lengths
+    return dot_nt(query_rows, key_side, highest) + added, values
+
+
+def attend(r, logits, values, halves, state, frame, weights):
     top = jnp.max(logits, axis=1, keepdims=True)
     raised = jnp.exp(logits - top)
     attention = raised / jnp.sum(raised, axis=1, keepdims=True)
+    row, _ = grid_of(attention.shape)
+    parts = [jnp.where((row & (IP - 1)) == i, attention, 0.0).astype(bf16) for i in range(r)]
+    out_pair = dot(jnp.concatenate(parts, axis=1), halves)
     summed = dot(attention, values, highest)
-    _, value_scalar, _, value_mask = head_masks()
-    masks = jnp.concatenate([value_scalar, value_mask, value_mask, value_mask], axis=1)
-    summed = summed * jnp.concatenate([masks] * r, axis=0)
-    gathered = jnp.sum(summed.reshape(r, HP, 640), axis=1)
-    gathered = jnp.concatenate([gathered, jnp.zeros((IP - r, 640), f32)], axis=0)
+    _, lane = grid_of((IP, 640))
+    head = jnp.where(lane < 256, lane >> log2(CHEAD), (lane & 127) >> log2(PV))
+    gathered = None
+    for h, tile in enumerate(tiles(summed)):
+        one = jnp.where(head == h, tile, 0.0)
+        gathered = one if gathered is None else gathered + one
     relative = [
         gathered[:, 256 + 128 * a : 256 + 128 * a + H * PV] - frame[:, 9 + a : 10 + a] for a in range(3)
     ]
@@ -332,24 +350,14 @@
     out_norm = jnp.sqrt(
         out_local[0] * out_local[0] + out_local[1] * out_local[1] + out_local[2] * out_local[2] + 1e-08
     )
-    half = attention.astype(bf16)
-    out_pair = jnp.concatenate(
-        [dot(half[i * HP : (i + 1) * HP], pair_half[i]) for i in range(r)], axis=0
-    ).astype(bf16)
-    row, column = grid_of((H * IP, r * HP))
-    by_head = dot(onehot(column == (row & (IP - 1)) * HP + (row >> log2(IP))), out_pair)
     combined = jnp.concatenate(
-        [gathered[:, 256 - H * CHEAD : 256]]
-        + out_local
-        + [out_norm]
-        + [by_head[h * IP : (h + 1) * IP] for h in range(H)],
-        axis=1,
+        [gathered[:, 0 : H * CHEAD]] + out_local + [out_norm] + tiles(out_pair), axis=1
     )
     combined = jnp.concatenate([combined, jnp.zeros_like(combined)], axis=0).astype(bf16)
     out_weight, frame_weight = weights()
     state = layer_norm(state + dot(combined, out_weight)[0:IP])
-    update = dot_nt(state, frame_weight, highest)
-    quat = [update[:, a : a + 1] for a in range(3)]
+    update = [jnp.sum(state * frame_weight[e : e + 1], axis=1, keepdims=True) for e in range(6)]
+    quat = update[0:3]
     real = lax.rsqrt(1.0 + (quat[0] * quat[0] + quat[1] * quat[1] + quat[2] * quat[2]))
     step = quat_entries(quat[0] * real, quat[1] * real, quat[2] * real, real)
     old = [frame[:, e : e + 1] for e in range(9)]
@@ -364,9 +372,9 @@
     for target in range(3):
         columns.append(
             frame[:, 9 + target : 10 + target]
-            + old[target * 3] * update[:, 3:4]
-            + old[target * 3 + 1] * update[:, 4:5]
-            + old[target * 3 + 2] * update[:, 5:6]
+            + old[target * 3] * update[3]
+            + old[target * 3 + 1] * update[4]
+            + old[target * 3 + 2] * update[5]
         )
     _, lane = grid_of((IP, 128))
     for at, column in enumerate(columns):
@@ -379,8 +387,8 @@
     return jnp.concatenate([single_ref[...], jnp.zeros((IP - r, CS), f32)], axis=0)
 
 
-PACK_ROWS = 216
-TRI_OUT, BIAS, COLUMNS, FRAME_WEIGHT, STATE, FRAME = 0, 128, 144, 160, 184, 208
+PACK_ROWS = 192
+BIAS, POINT_WEIGHT, FRAME_WEIGHT, STATE, FRAME = 0, 128, 136, 160, 184
 
 
 def wide(pack_ref, first):
@@ -389,12 +397,11 @@
 
 def own_kernel(
     pair_any, tri_any, qkv_any, single_any, frame_any, columns_any, tri_out_any, bias_weight_any, frame_weight_any,
-    gate_ref, key_ref, query_ref, rows_ref, pack_ref, pair_copy_any,
-    pair_ref, gate_weight_ref, qkv_ref, single_ref, tri_out_ref, bias_weight_ref, frame_weight_ref, sems,
+    gate_ref, rows_ref, pack_ref, pair_copy_any,
+    pair_ref, gate_weight_ref, qkv_ref, single_ref, columns_ref, tri_out_ref, bias_weight_ref, frame_weight_ref, sems,
 ):
     r, count, _ = pair_ref.shape
     frame_ref = pack_ref.at[FRAME : FRAME + IP]
-    columns_ref = pack_ref.at[COLUMNS : COLUMNS + HP]
     for copy in copies(
         sems,
         (pair_any, pair_ref),
@@ -410,9 +417,13 @@
         copy.wait()
     back = pltpu.make_async_copy(pair_ref, pair_copy_any, sems.at[9])
     back.start()
-    pack_ref[TRI_OUT : TRI_OUT + CH, :] = tri_out_ref[...].astype(f32)
+    gate_ref[r * count :, :] = tri_out_ref[...]
     bias_weight = bias_weight_ref[...]
-    pack_ref[BIAS : BIAS + HP, :] = jnp.concatenate([bias_weight, jnp.zeros((HP - H, CH), f32)], axis=0)
+    spread = [jnp.broadcast_to(bias_weight[h : h + 1], (IP, CH)) for h in range(H)]
+    bias_weight = jnp.concatenate(spread + [jnp.zeros((128 - ROWS, CH), f32)], axis=0).T
+    _, lane = grid_of((CH, 128))
+    pack_ref[BIAS : BIAS + CH, :] = jnp.where(lane < ROWS, bias_weight, columns_ref[0:CH, :])
+    pack_ref[POINT_WEIGHT : POINT_WEIGHT + IP, :] = columns_ref[CH : CH + IP, :]
     state = pad_state(single_ref)
     frame_weight = frame_weight_ref[...]
     frame_weight = jnp.concatenate([frame_weight, jnp.zeros((IP - 6, CS), f32)], axis=0)
@@ -420,34 +431,20 @@
         lanes = slice(128 * part, 128 * (part + 1))
         pack_ref[FRAME_WEIGHT + IP * part : FRAME_WEIGHT + IP * (part + 1), :] = frame_weight[:, lanes]
         pack_ref[STATE + IP * part : STATE + IP * (part + 1), :] = state[:, lanes]
-    width = H * CHEAD
-    start = 3 * width
-    points = H * PQ
-
-    def padded(first, size, to):
-        block = qkv_ref[:, first : first + size].astype(f32)
-        return jnp.concatenate([block, jnp.zeros((CS, to - size), f32)], axis=1).astype(bf16)
-
-    queries = [qkv_ref[:, 0:width], qkv_ref[:, start : start + 3 * points]]
-    query_ref[...] = jnp.concatenate([q.astype(f32) for q in queries] + [jnp.zeros((CS, 48), f32)], axis=1).astype(bf16)
-    key_ref[:, 0 : 2 * width] = qkv_ref[:, width:start]
-    for a in range(3):
-        key_ref[:, 512 + 256 * a : 640 + 256 * a] = padded(start + (3 + a) * points, points, 128)
-        key_ref[:, 384 + 256 * a : 512 + 256 * a] = padded(start + 6 * points + a * H * PV, H * PV, 128)
-    rows, lengths = own_side(r, state, frame_ref[...], query_ref[...], columns_ref[...])
+    rows, lengths = own_side(state, frame_ref[...], qkv_ref, pack_ref[POINT_WEIGHT : POINT_WEIGHT + 1])
     rows_ref[:, 0:768] = rows
-    rows_ref[:, 768:896] = jnp.broadcast_to(lengths, (r * HP, 128))
+    rows_ref[:, 768:896] = jnp.broadcast_to(lengths, (ROWS, 128))
     for i in range(r):
         normed = layer_norm(pair_ref[i]).astype(bf16)
-        gate_ref[i] = jax.nn.sigmoid(dot(normed, gate_weight_ref[...])).astype(bf16)
+        gate_ref[i * count : (i + 1) * count] = jax.nn.sigmoid(dot(normed, gate_weight_ref[...])).astype(bf16)
     back.wait()
 
 
-def prepare_kernel(w, n, r, recv_ref, rows_ref, key_ref, pack_ref, logits_ref, values_ref):
-    slots = natural_rows(recv_ref, r * n * r, w, r, n)
+def prepare_kernel(w, n, r, recv_ref, rows_ref, qkv_ref, pack_ref, logits_ref, values_ref):
+    slots = natural_rows(recv_ref, 0, w, r, n)
     logits, values = logits_and_values(
-        r, slots, (rows_ref[:, 0:768], rows_ref[:, 768:769]), pack_ref[FRAME : FRAME + IP], key_ref[...],
-        pack_ref[COLUMNS : COLUMNS + HP],
+        slots, (rows_ref[:, 0:768], rows_ref[:, 768:769]), pack_ref[FRAME : FRAME + IP], qkv_ref[...],
+        pack_ref[BIAS : BIAS + ROWS],
     )
     logits_ref[...] = logits
     values_ref[...] = values
@@ -458,35 +455,34 @@
     pair_out_any, half_ref, bias_ref, state_ref, new_frame_ref, send_ref, pair_ref, sems,
 ):
     r, count, _ = pair_ref.shape
-    load = pltpu.make_async_copy(pair_any, pair_ref, sems.at[r])
+    load = pltpu.make_async_copy(pair_any, pair_ref, sems.at[0])
     load.start()
-    half = r // 2
     row, column = grid_of((2 * CH, 2 * CH))
     c = row & (CH - 1)
     take = onehot(column == (c >> log2(w)) * 2 * w + (row >> log2(CH)) * w + (c & (w - 1)))
     product = dot(take, recv_ref[...])
-    tri_out = pack_ref[TRI_OUT : TRI_OUT + CH, :].astype(bf16)
+    tri_out = gate_ref[r * count :, :]
     updates = []
     for high in range(2):
         normed = layer_norm(product[high * CH : (high + 1) * CH], axis=0).astype(bf16)
         updates.append(dot_tn(normed, tri_out))
+    update = jnp.concatenate(updates, axis=0)
+    bias_weight = pack_ref[BIAS : BIAS + CH, :]
+    _, lane = grid_of((CH, 128))
+    bias_weight = jnp.concatenate(
+        [jnp.where(((lane & (IP - 1)) == i) & (lane < ROWS), bias_weight, 0.0) for i in range(r)], axis=0
+    )
     load.wait()
-    biases = []
-    halves = []
-    stores = []
-    for i in range(r):
-        low = i % half
-        update = updates[i // half][low * count : (low + 1) * count]
-        pair_out = pair_ref[i] + gate_ref[i].astype(f32) * update
-        pair_ref[i] = pair_out
-        store = pltpu.make_async_copy(pair_ref.at[i], pair_out_any.at[i], sems.at[i])
-        store.start()
-        stores.append(store)
-        normed_pair = layer_norm(pair_out)
-        biases.append(dot_nt(pack_ref[BIAS : BIAS + HP, :], normed_pair, highest) * third)
-        halves.append(normed_pair.astype(bf16))
-        half_ref[i] = halves[-1]
-    bias = jnp.concatenate(biases, axis=0)
+    pair = pair_ref[...].reshape(r * count, CH)
+    pair_out = pair + gate_ref[0 : r * count, :].astype(f32) * update
+    pair_ref[...] = pair_out.reshape(r, count, CH)
+    store = pltpu.make_async_copy(pair_ref, pair_out_any, sems.at[1])
+    store.start()
+    normed_pair = layer_norm(pair_out)
+    halves = normed_pair.astype(bf16)
+    half_ref[...] = halves
+    side_by_side = jnp.concatenate([normed_pair[i * count : (i + 1) * count] for i in range(r)], axis=1)
+    bias = (dot(side_by_side, bias_weight, highest) * third).T[0:ROWS]
     bias_ref[...] = bias
     state, frame = attend(
         r, logits_ref[...] + bias, values_ref[...], halves, wide(pack_ref, STATE), pack_ref[FRAME : FRAME + IP],
@@ -495,23 +491,19 @@
     state_ref[...] = state
     new_frame_ref[...] = frame
     fill_rows(send_ref, 0, spread_rows(slots_of(state, frame), w, r))
-    for store in stores:
-        store.wait()
+    store.wait()
 
 
 def last_kernel(
-    w, n, recv_ref, half_ref, bias_ref, state_ref, frame_ref, pack_ref, query_ref, key_ref, out_weight_ref,
+    w, n, r, recv_ref, half_ref, bias_ref, state_ref, frame_ref, pack_ref, qkv_ref, out_weight_ref,
     single_out_ref, rotation_ref, translation_ref, scr,
 ):
-    r = half_ref.shape[0]
     slots = natural_rows(recv_ref, 0, w, r, n)
     state, frame = state_ref[...], frame_ref[...]
-    columns = pack_ref[COLUMNS : COLUMNS + HP]
-    own = own_side(r, state, frame, query_ref[...], columns)
-    logits, values = logits_and_values(r, slots, own, frame, key_ref[...], columns)
-    halves = [half_ref[i] for i in range(r)]
+    own = own_side(state, frame, qkv_ref, pack_ref[POINT_WEIGHT : POINT_WEIGHT + 1])
+    logits, values = logits_and_values(slots, own, frame, qkv_ref[...], pack_ref[BIAS : BIAS + ROWS])
     state, frame = attend(
-        r, logits + bias_ref[...], values, halves, state, frame,
+        r, logits + bias_ref[...], values, half_ref[...], state, frame,
         lambda: (out_weight_ref[...], wide(pack_ref, FRAME_WEIGHT)),
     )
     single_out_ref[...] = state[0:r]
@@ -573,34 +565,33 @@
             pltpu.SMEM((r,), jnp.int32),
             pltpu.SMEM((r,), jnp.int32),
             pltpu.VMEM((128, 128), f32),
-            dma((r + 6,)),
+            dma((7,)),
         ],
         limit=60,
     )
     received = exchange(sent)
 
     point_weight = head_gamma * (math.sqrt(2.0 / (9.0 * PQ)) * 0.5 * third)
-    columns = jnp.stack([point_weight, chain_bias[0], chain_bias[1]], axis=1)
-    columns = jnp.pad(columns, ((0, HP - H), (0, 125)))
-    gate, key_weight, query_weight, query_rows, pack, pair_copy = call(
+    columns = jnp.pad(jnp.repeat(chain_bias.T, IP, axis=0), ((0, CH - ROWS + IP), (ROWS, 126 - ROWS)))
+    columns = columns.at[CH, 0 : H * PQ].set(jnp.repeat(point_weight, PQ))
+    gate, query_rows, pack, pair_copy = call(
         own_kernel,
         "own",
         [
-            ((r, count, CH), bf16),
-            ((CS, 1152), bf16),
-            ((CS, 384), bf16),
-            ((r * HP, 896), f32),
+            ((r * count + CH, CH), bf16),
+            ((ROWS, 896), f32),
             ((PACK_ROWS, 128), f32),
             (pair.shape, f32),
         ],
         [pair, tri_weight, qkv_weight, single, frame, columns, tri_out_weight, bias_weight.T, frame_weight.T],
         outside=range(9),
-        outside_outs=(5,),
+        outside_outs=(3,),
         scratch=[
             like(pair),
             pltpu.VMEM((CH, CH), bf16),
             like(qkv_weight),
             like(single),
+            like(columns),
             like(tri_out_weight),
             pltpu.VMEM((H, CH), f32),
             pltpu.VMEM((6, CS), f32),
@@ -610,13 +601,13 @@
         flops=2 * r * count * CH * CH,
         moved=16 * 2**20,
     )
-    received, gate, key_weight, query_weight, query_rows, pack, pair_copy = lax.optimization_barrier(
-        (received, gate, key_weight, query_weight, query_rows, pack, pair_copy)
-    )
-    (formed,) = call(
+    received, gate, query_rows, pack, pair_copy = lax.optimization_barrier(
+        (received, gate, query_rows, pack, pair_copy)
+    )
+    formed, slots = call(
         functools.partial(product_kernel, w, n, r),
         "product",
-        [((n * rows, (r // 2) * count), bf16)],
+        [((n * rows, (r // 2) * count), bf16), ((n * rows, lanes), bf16)],
         [received],
         limit=limit,
     )
@@ -624,8 +615,8 @@
     logits, values = call(
         functools.partial(prepare_kernel, w, n, r),
         "prepare",
-        [((r * HP, count), f32), ((count, 640), f32)],
-        [received, query_rows, key_weight, pack],
+        [((ROWS, count), f32), ((count, 640), f32)],
+        [slots, query_rows, qkv_weight, pack],
         limit=limit,
         flops=2 * count * CS * 1152,
         moved=8 * 2**20,
@@ -635,8 +626,8 @@
         "update",
         [
             ((r, count, CH), f32),
-            ((r, count, CH), bf16),
-            ((r * HP, count), f32),
+            ((r * count, CH), bf16),
+            ((ROWS, count), f32),
             ((IP, CS), f32),
             ((IP, 128), f32),
             ((n * rows, lanes), bf16),
@@ -645,15 +636,15 @@
         outside=(1,),
         outside_outs=(0,),
         alias={1: 0},
-        scratch=[like(pair), dma((r + 1,))],
+        scratch=[like(pair), dma((2,))],
         limit=limit,
     )
     received = exchange(sent)
     single_out, rotation, translation = call(
-        functools.partial(last_kernel, w, n),
+        functools.partial(last_kernel, w, n, r),
         "last",
         [((r, CS), f32), ((r, 9), f32), ((3, r), f32)],
-        [received, pair_half, bias, state, frame, pack, query_weight, key_weight, out_weight],
+        [received, pair_half, bias, state, frame, pack, qkv_weight, out_weight],
         scratch=[pltpu.VMEM((128, 128), f32)],
         limit=limit,
     )

time: 55.2 us -> 52.7 us (0.955)
  Pallas kernels: 17.3 us -> 14.6 us
    pallas_call x6, Pallas kernels: 17.3 us -> 14.6 us  [call(): pl.pallas_call(body, name=name, out_shape=[jax.ShapeDtypeStruct(s, d) for...]
    another operation x2 -> x1, local copies, waits for them, and re-layouts: 0.85 us -> 0.08 us  [local(): columns = jnp.stack([point_weight, chain_bias[0], chain_bias[1]], axis=1)]
    transpose x0 -> x1, local copies, waits for them, and re-layouts: none -> 0.77 us  [local(): columns = jnp.pad(jnp.repeat(chain_bias.T, IP, axis=0), ((0, CH - ROWS +...]
    another operation x2 -> x0, other arithmetic: 0.67 us -> none  [local(): columns = jnp.stack([point_weight, chain_bias[0], chain_bias[1]], axis=1)]
    mul x0 -> x1, other arithmetic: none -> 0.66 us  [local(): point_weight = head_gamma * (math.sqrt(2.0 / (9.0 * PQ)) * 0.5 * third)]
    unnamed x16 -> x18, local copies, waits for them, and re-layouts: 3.02 us -> 3.4 us
  transfers between devices with their start and end apart: 2 -> 2, of which waited for: 2 -> 2; matrix products, arithmetic and copies ran while one was open for 4% -> 3% of each run, Pallas kernels for 8% -> 8%
where the time goes in v4:
time: 52.7 us; the launch traced here: 52.3 us
  Pallas kernels  14.6 us (28%)
  waiting for transfers between devices  11.9 us (23%)
  blocking collectives  9.99 us (19%)
  starting transfers between devices  9.93 us (19%)
  local copies, waits for them, and re-layouts  4.54 us (9%)
  between operations  0.76 us (1%)
  other arithmetic  0.66 us (1%)
    pallas_call x6, Pallas kernels, call(): pl.pallas_call(body, name=name, out_shape=[jax.ShapeDtypeStruct(s, d) for...  14.6 us
    all_to_all x2, waiting for transfers between devices, exchange(): got = lax.all_to_all(sent.reshape(n, rows, width), 'row', 0, 0, tiled=True)  11.9 us
    all_to_all x1, blocking collectives, exchange(): got = lax.all_to_all(sent.reshape(n, rows, width), 'row', 0, 0, tiled=True)  9.99 us
    all_to_all x2, starting transfers between devices, exchange(): got = lax.all_to_all(sent.reshape(n, rows, width), 'row', 0, 0, tiled=True)  9.93 us
    unnamed x18, local copies, waits for them, and re-layouts  3.4 us
  transfers between devices with their start and end apart: 2, of which 2 were waited for; matrix products, arithmetic and copies ran while one was open for 3% of the time, Pallas kernels for 8%

profile of v4, /device:TPU:0, one launch (start us, length us, event | category | flops | bytes accessed | tf_op | source)
XLA Modules:
  0.0 52.3 jit_solution(16302683147820118634)
XLA Ops:
  0.6 2.4 %gate.1 = (bf16[256,768]{1,0:T(8,128)(2,1)}, f32[8,128]{1,0:T(8,128)}) custom-call(f32[4,128,128]{2,1,0:T(8,128)} %pair_any.3, bf16[128,640]{1,0:T(8,128)(2,1)} %tri_any.3, f32[4,384]{1,0:T(4,128)} %single_any.3, f32[3,4]{1,0:T(4,128)} %quats_any.1, f32[3,4]{1,0:T(4,128)} %translate_any.1, s32[4]{0:T(128)} %mask_any.1, s32[4]{0:T(128)} %chain_any.1), custom_call_target="tpu_custom_call" | custom-call | tf_op jit(solution)/shard_map/gate/pallas_call | solution.py:520
  3.0 0.0 copy-start
  3.1 7.3 %all-to-all-start = ((bf16[32,8,768]{2,1,0:T(8,128)(2,1)}), bf16[32,8,768]{2,1,0:T(8,128)(2,1)S(1)}, u32[]{:S(2)}, u32[]{:S(2)}) async-start(bf16[32,8,768]{2,1,0:T(8,128)(2,1)} %bitcast.16), calls=%async_computation | async-start | bytes 786432 | tf_op jit(solution)/shard_map/all_to_all | solution.py:546
  10.4 0.7 %broadcast_multiply_fusion = f32[12]{0:T(128)S(1)} fusion(f32[12]{0:T(128)} %param.26), kind=kLoop, calls=%fused_computation.1 | loop fusion | flops 12 | bytes 96 | tf_op jit(solution)/shard_map/mul | solution.py:574
  11.0 0.1 broadcast_in_dim.7
  11.1 0.1 reshape.64
  11.2 0.8 %copy.20 = f32[12,2]{1,0:T(8,128)S(1)} copy(f32[12,2]{0,1:T(2,128)} %bitcast.19) | data formatting | bytes 192 | tf_op jit(solution)/shard_map/transpose | solution.py:575
  12.0 0.1 pad.7
  12.0 0.1 scatter.4.columns_any
  12.2 0.0 copy-start.8
  12.2 0.6 %copy-done.8 = f32[136,128]{1,0:T(8,128)} copy-done((f32[136,128]{1,0:T(8,128)}, f32[136,128]{1,0:T(8,128)S(1)}, u32[]{:S(2)}) %copy-start.8) | copy-done | bytes 69656
  12.8 0.0 copy-start.1
  12.8 3.0 %own.1 = (bf16[640,128]{1,0:T(8,128)(2,1)}, f32[96,896]{1,0:T(8,128)}, f32[192,128]{1,0:T(8,128)}, f32[4,128,128]{2,1,0:T(8,128)}) custom-call(f32[4,128,128]{2,1,0:T(8,128)} %pair_any.3, bf16[128,640]{1,0:T(8,128)(2,1)} %tri_any.3, bf16[384,1152]{1,0:T(8,128)(2,1)} %qkv_ref.3, f32[4,384]{1,0:T(4,128)} %single_any.3, f32[8,128]{1,0:T(8,128)} %get-tuple-element.41.frame_any, ...), custom_call_target="tpu_custom_call" | custom-call | flops 16777216 | bytes 16777216 | tf_op jit(solution)/shard_map/own/pallas_call | solution.py:520
  15.8 0.0 copy-start.3
  15.8 0.0 copy-start.5
  15.8 7.7 %all-to-all-done = bf16[32,8,768]{2,1,0:T(8,128)(2,1)S(1)} async-done(((bf16[32,8,768]{2,1,0:T(8,128)(2,1)}), bf16[32,8,768]{2,1,0:T(8,128)(2,1)S(1)}, u32[]{:S(2)}, u32[]{:S(2)}) %all-to-all-start) | async-done | bytes 393248 | tf_op jit(solution)/shard_map/all_to_all | solution.py:546
  23.5 1.7 %product.1 = (bf16[256,256]{1,0:T(8,128)(2,1)}, bf16[256,256]{1,0:T(8,128)(2,1)S(1)}) custom-call(bf16[256,768]{1,0:T(8,128)(2,1)S(1)} %bitcast.12), custom_call_target="tpu_custom_call" | custom-call | tf_op jit(solution)/shard_map/product/pallas_call | solution.py:520
  25.2 0.0 copy-start.6
  25.2 2.6 %all-to-all-start.1 = ((bf16[32,8,256]{2,1,0:T(8,128)(2,1)}), bf16[32,8,256]{2,1,0:T(8,128)(2,1)S(1)}, u32[]{:S(2)}, u32[]{:S(2)}) async-start(bf16[32,8,256]{2,1,0:T(8,128)(2,1)} %bitcast.6), calls=%async_computation.1 | async-start | bytes 262144 | tf_op jit(solution)/shard_map/all_to_all | solution.py:546
  27.9 0.0 copy-done.6
  27.9 0.0 copy-done
  27.9 0.0 copy-start.2
  27.9 0.9 %copy-done.2 = f32[192,128]{1,0:T(8,128)S(1)} copy-done((f32[192,128]{1,0:T(8,128)S(1)}, f32[192,128]{1,0:T(8,128)}, u32[]{:S(2)}) %copy-start.2) | copy-done | bytes 98328
  28.8 0.0 copy-start.4
  28.8 1.0 %copy-done.4 = f32[96,896]{1,0:T(8,128)S(1)} copy-done((f32[96,896]{1,0:T(8,128)S(1)}, f32[96,896]{1,0:T(8,128)}, u32[]{:S(2)}) %copy-start.4) | copy-done | bytes 344088
  29.8 0.0 copy-start.7
  29.8 0.9 %copy-done.7 = bf16[256,256]{1,0:T(8,128)(2,1)S(1)} copy-done((bf16[256,256]{1,0:T(8,128)(2,1)S(1)}, bf16[256,256]{1,0:T(8,128)(2,1)}, u32[]{:S(2)}) %copy-start.7) | copy-done | bytes 131096
  30.7 1.3 %prepare.1 = (f32[96,128]{1,0:T(8,128)S(1)}, f32[128,640]{1,0:T(8,128)S(1)}) custom-call(bf16[256,256]{1,0:T(8,128)(2,1)S(1)} %copy-done.7, f32[96,896]{1,0:T(8,128)S(1)} %copy-done.4, bf16[384,1152]{1,0:T(8,128)(2,1)S(1)} %copy-done, f32[192,128]{1,0:T(8,128)S(1)} %copy-done.2), custom_call_target="tpu_custom_call" | custom-call | flops 113246208 | bytes 8388608 | tf_op jit(solution)/shard_map/prepare/pallas_call | solution.py:520
  31.9 4.2 %all-to-all-done.1 = bf16[32,8,256]{2,1,0:T(8,128)(2,1)S(1)} async-done(((bf16[32,8,256]{2,1,0:T(8,128)(2,1)}), bf16[32,8,256]{2,1,0:T(8,128)(2,1)S(1)}, u32[]{:S(2)}, u32[]{:S(2)}) %all-to-all-start.1) | async-done | bytes 131104 | tf_op jit(solution)/shard_map/all_to_all | solution.py:546
  36.1 0.0 copy-done.1
  36.1 0.0 copy-done.3
  36.1 0.0 copy-done.5
  36.1 3.1 %update.1 = (f32[4,128,128]{2,1,0:T(8,128)}, bf16[512,128]{1,0:T(8,128)(2,1)S(1)}, f32[96,128]{1,0:T(8,128)S(1)}, f32[8,384]{1,0:T(8,128)S(1)}, f32[8,128]{1,0:T(8,128)S(1)}, /*index=5*/bf16[256,256]{1,0:T(8,128)(2,1)S(1)}) custom-call(bf16[256,256]{1,0:T(8,128)(2,1)S(1)} %bitcast.14, ...), custom_call_target="tpu_custom_call", output_to_operand_aliasing={{0}: (1, {})} | custom-call | tf_op jit(solution)/shard_map/update/pallas_call | solution.py:520
  39.2 10.0 %all_to_all.15 = bf16[32,8,256]{2,1,0:T(8,128)(2,1)S(1)} all-to-all(bf16[32,8,256]{2,1,0:T(8,128)(2,1)S(1)} %bitcast.15), channel_id=1, replica_groups=mesh['grp'=1,'row'=32] {'row'}, dimensions={0} | all-to-all | bytes 262144 | tf_op jit(solution)/shard_map/all_to_all | solution.py:546
  49.2 3.1 %last.1 = (f32[4,384]{1,0:T(4,128)}, f32[4,9]{1,0:T(4,128)}, f32[3,4]{1,0:T(4,128)}) custom-call(bf16[256,256]{1,0:T(8,128)(2,1)S(1)} %bitcast.13, bf16[512,128]{1,0:T(8,128)(2,1)S(1)} %get-tuple-element.57.half_ref, f32[96,128]{1,0:T(8,128)S(1)} %get-tuple-element.58.bias_ref, f32[8,384]{1,0:T(8,128)S(1)} %get-tuple-element.59.state_ref, ...), custom_call_target="tpu_custom_call" | custom-call | tf_op jit(solution)/shard_map/last/pallas_call | solution.py:520
  (1 shorter events, 0.0 us)
Async XLA Ops:
  3.0 24.8 %copy-start = (bf16[384,1152]{1,0:T(8,128)(2,1)S(1)}, bf16[384,1152]{1,0:T(8,128)(2,1)}, u32[]{:S(2)}) copy-start(bf16[384,1152]{1,0:T(8,128)(2,1)} %qkv_ref.3) | copy-start | bytes 2654212
  3.1 20.5 %all-to-all-start = ((bf16[32,8,768]{2,1,0:T(8,128)(2,1)}), bf16[32,8,768]{2,1,0:T(8,128)(2,1)S(1)}, u32[]{:S(2)}, u32[]{:S(2)}) async-start(bf16[32,8,768]{2,1,0:T(8,128)(2,1)} %bitcast.16), calls=%async_computation | async-start | bytes 786432 | tf_op jit(solution)/shard_map/all_to_all | solution.py:546
  12.2 0.6 %copy-start.8 = (f32[136,128]{1,0:T(8,128)}, f32[136,128]{1,0:T(8,128)S(1)}, u32[]{:S(2)}) copy-start(f32[136,128]{1,0:T(8,128)S(1)} %scatter.4.columns_any) | copy-start | bytes 208900
  12.8 23.3 %copy-start.1 = (bf16[2112,384]{1,0:T(8,128)(2,1)S(1)}, bf16[2112,384]{1,0:T(8,128)(2,1)}, u32[]{:S(2)}) copy-start(bf16[2112,384]{1,0:T(8,128)(2,1)} %out_weight_ref.3) | copy-start | bytes 4866052
  15.8 20.3 %copy-start.3 = (f32[192,128]{1,0:T(8,128)S(1)}, f32[192,128]{1,0:T(8,128)}, u32[]{:S(2)}) copy-start(f32[192,128]{1,0:T(8,128)} %get-tuple-element.52.pack_ref) | copy-start | bytes 294916
  15.8 20.3 %copy-start.5 = (bf16[640,128]{1,0:T(8,128)(2,1)S(1)}, bf16[640,128]{1,0:T(8,128)(2,1)}, u32[]{:S(2)}) copy-start(bf16[640,128]{1,0:T(8,128)(2,1)} %get-tuple-element.49.gate_ref) | copy-start | bytes 491524
  25.2 2.6 %copy-start.6 = (bf16[256,256]{1,0:T(8,128)(2,1)}, bf16[256,256]{1,0:T(8,128)(2,1)S(1)}, u32[]{:S(2)}) copy-start(bf16[256,256]{1,0:T(8,128)(2,1)S(1)} %get-tuple-element.50.recv_ref) | copy-start | bytes 393220
  25.2 10.9 %all-to-all-start.1 = ((bf16[32,8,256]{2,1,0:T(8,128)(2,1)}), bf16[32,8,256]{2,1,0:T(8,128)(2,1)S(1)}, u32[]{:S(2)}, u32[]{:S(2)}) async-start(bf16[32,8,256]{2,1,0:T(8,128)(2,1)} %bitcast.6), calls=%async_computation.1 | async-start | bytes 262144 | tf_op jit(solution)/shard_map/all_to_all | solution.py:546
  27.9 0.9 %copy-start.2 = (f32[192,128]{1,0:T(8,128)S(1)}, f32[192,128]{1,0:T(8,128)}, u32[]{:S(2)}) copy-start(f32[192,128]{1,0:T(8,128)} %get-tuple-element.52.pack_ref) | copy-start | bytes 294916
  28.8 1.0 %copy-start.4 = (f32[96,896]{1,0:T(8,128)S(1)}, f32[96,896]{1,0:T(8,128)}, u32[]{:S(2)}) copy-start(f32[96,896]{1,0:T(8,128)} %get-tuple-element.51.rows_ref) | copy-start | bytes 1032196
  29.8 0.9 %copy-start.7 = (bf16[256,256]{1,0:T(8,128)(2,1)S(1)}, bf16[256,256]{1,0:T(8,128)(2,1)}, u32[]{:S(2)}) copy-start(bf16[256,256]{1,0:T(8,128)(2,1)} %copy-done.6) | copy-start | bytes 393220

commit v5 on v4

--- a/solution.py
+++ b/solution.py
@@ -62,6 +62,21 @@
 
 def dot_tn(a, b):
     return lax.dot_general(a, b, (((0,), (0,)), ((), ())), preferred_element_type=f32)
+
+
+def halves_of(x):
+    high = x.astype(bf16)
+    return high, (x - high.astype(f32)).astype(bf16)
+
+
+def dot_close(a, b):
+    a_high, a_low = halves_of(a)
+    b_high, b_low = halves_of(b)
+    return dot(jnp.concatenate([a_high, a_low, a_high], axis=1), jnp.concatenate([b_high, b_high, b_low], axis=0))
+
+
+def sigmoid(x):
+    return 0.5 * jnp.tanh(0.5 * x) + 0.5
 
 
 def log2(number):
@@ -192,7 +207,7 @@
     gates = dot_nt(gate_weight, normed)
     values = dot_nt(value_weight, normed)
     mask = jnp.concatenate([jnp.full((1, count), mask_ref[i].astype(f32)) for i in range(r)], axis=1)
-    send_ref[:, 0 : r * count] = (jax.nn.sigmoid(gates) * values * mask).astype(bf16)
+    send_ref[:, 0 : r * count] = (sigmoid(gates) * values * mask).astype(bf16)
 
     scr[...] = jnp.zeros_like(scr)
     quats = quats_ref[...]
@@ -331,7 +346,7 @@
     row, _ = grid_of(attention.shape)
     parts = [jnp.where((row & (IP - 1)) == i, attention, 0.0).astype(bf16) for i in range(r)]
     out_pair = dot(jnp.concatenate(parts, axis=1), halves)
-    summed = dot(attention, values, highest)
+    summed = dot_close(attention, values)
     _, lane = grid_of((IP, 640))
     head = jnp.where(lane < 256, lane >> log2(CHEAD), (lane & 127) >> log2(PV))
     gathered = None
@@ -350,12 +365,16 @@
     out_norm = jnp.sqrt(
         out_local[0] * out_local[0] + out_local[1] * out_local[1] + out_local[2] * out_local[2] + 1e-08
     )
-    combined = jnp.concatenate(
-        [gathered[:, 0 : H * CHEAD]] + out_local + [out_norm] + tiles(out_pair), axis=1
-    )
-    combined = jnp.concatenate([combined, jnp.zeros_like(combined)], axis=0).astype(bf16)
-    out_weight, frame_weight = weights()
-    state = layer_norm(state + dot(combined, out_weight)[0:IP])
+    out_ref, frame_weight = weights()
+
+    def projected(blocks, first):
+        rows = jnp.concatenate(blocks, axis=1)
+        rows = jnp.concatenate([rows, jnp.zeros_like(rows)], axis=0).astype(bf16)
+        return dot(rows, out_ref[first : first + rows.shape[1], :])[0:IP]
+
+    from_pair = projected(tiles(out_pair), H * (CHEAD + 4 * PV))
+    from_points = projected([gathered[:, 0 : H * CHEAD]] + out_local + [out_norm], 0)
+    state = layer_norm(state + (from_points + from_pair))
     update = [jnp.sum(state * frame_weight[e : e + 1], axis=1, keepdims=True) for e in range(6)]
     quat = update[0:3]
     real = lax.rsqrt(1.0 + (quat[0] * quat[0] + quat[1] * quat[1] + quat[2] * quat[2]))
@@ -482,11 +501,11 @@
     halves = normed_pair.astype(bf16)
     half_ref[...] = halves
     side_by_side = jnp.concatenate([normed_pair[i * count : (i + 1) * count] for i in range(r)], axis=1)
-    bias = (dot(side_by_side, bias_weight, highest) * third).T[0:ROWS]
+    bias = (dot_close(side_by_side, bias_weight) * third).T[0:ROWS]
     bias_ref[...] = bias
     state, frame = attend(
         r, logits_ref[...] + bias, values_ref[...], halves, wide(pack_ref, STATE), pack_ref[FRAME : FRAME + IP],
-        lambda: (out_weight_ref[...], wide(pack_ref, FRAME_WEIGHT)),
+        lambda: (out_weight_ref, wide(pack_ref, FRAME_WEIGHT)),
     )
     state_ref[...] = state
     new_frame_ref[...] = frame
@@ -504,7 +523,7 @@
     logits, values = logits_and_values(slots, own, frame, qkv_ref[...], pack_ref[BIAS : BIAS + ROWS])
     state, frame = attend(
         r, logits + bias_ref[...], values, half_ref[...], state, frame,
-        lambda: (out_weight_ref[...], wide(pack_ref, FRAME_WEIGHT)),
+        lambda: (out_weight_ref, wide(pack_ref, FRAME_WEIGHT)),
     )
     single_out_ref[...] = state[0:r]
     rotation_ref[...] = frame[0:r, 0:9]

time: 52.7 us -> 52 us (0.987)
  Pallas kernels: 14.6 us -> 13.8 us
    pallas_call x6, Pallas kernels: 14.6 us -> 13.8 us  [call(): pl.pallas_call(body, name=name, out_shape=[jax.ShapeDtypeStruct(s, d) for...]
  transfers between devices with their start and end apart: 2 -> 2, of which waited for: 2 -> 2; matrix products, arithmetic and copies ran while one was open for 3% -> 4% of each run, Pallas kernels for 8% -> 8%
where the time goes in v5:
time: 52 us; the launch traced here: 51.5 us
  Pallas kernels  13.8 us (27%)
  waiting for transfers between devices  11.9 us (23%)
  blocking collectives  10 us (19%)
  starting transfers between devices  9.93 us (19%)
  local copies, waits for them, and re-layouts  4.54 us (9%)
  between operations  0.76 us (1%)
  other arithmetic  0.66 us (1%)
    pallas_call x6, Pallas kernels, call(): pl.pallas_call(body, name=name, out_shape=[jax.ShapeDtypeStruct(s, d) for...  13.8 us
    all_to_all x2, waiting for transfers between devices, exchange(): got = lax.all_to_all(sent.reshape(n, rows, width), 'row', 0, 0, tiled=True)  11.9 us
    all_to_all x1, blocking collectives, exchange(): got = lax.all_to_all(sent.reshape(n, rows, width), 'row', 0, 0, tiled=True)  10 us
    all_to_all x2, starting transfers between devices, exchange(): got = lax.all_to_all(sent.reshape(n, rows, width), 'row', 0, 0, tiled=True)  9.93 us
    unnamed x18, local copies, waits for them, and re-layouts  3.4 us
  transfers between devices with their start and end apart: 2, of which 2 were waited for; matrix products, arithmetic and copies ran while one was open for 4% of the time, Pallas kernels for 8%

profile of v5, /device:TPU:0, one launch (start us, length us, event | category | flops | bytes accessed | tf_op | source)
XLA Modules:
  0.0 51.5 jit_solution(12550950739077522924)
XLA Ops:
  0.6 2.4 %gate.1 = (bf16[256,768]{1,0:T(8,128)(2,1)}, f32[8,128]{1,0:T(8,128)}) custom-call(f32[4,128,128]{2,1,0:T(8,128)} %pair_any.3, bf16[128,640]{1,0:T(8,128)(2,1)} %tri_any.3, f32[4,384]{1,0:T(4,128)} %single_any.3, f32[3,4]{1,0:T(4,128)} %quats_any.1, f32[3,4]{1,0:T(4,128)} %translate_any.1, s32[4]{0:T(128)} %mask_any.1, s32[4]{0:T(128)} %chain_any.1), custom_call_target="tpu_custom_call" | custom-call | tf_op jit(solution)/shard_map/gate/pallas_call | solution.py:539
  3.0 0.0 copy-start
  3.0 7.3 %all-to-all-start = ((bf16[32,8,768]{2,1,0:T(8,128)(2,1)}), bf16[32,8,768]{2,1,0:T(8,128)(2,1)S(1)}, u32[]{:S(2)}, u32[]{:S(2)}) async-start(bf16[32,8,768]{2,1,0:T(8,128)(2,1)} %bitcast.16), calls=%async_computation | async-start | bytes 786432 | tf_op jit(solution)/shard_map/all_to_all | solution.py:565
  10.4 0.7 %broadcast_multiply_fusion = f32[12]{0:T(128)S(1)} fusion(f32[12]{0:T(128)} %param.26), kind=kLoop, calls=%fused_computation.1 | loop fusion | flops 12 | bytes 96 | tf_op jit(solution)/shard_map/mul | solution.py:593
  11.0 0.1 broadcast_in_dim.7
  11.1 0.1 reshape.64
  11.2 0.8 %copy.20 = f32[12,2]{1,0:T(8,128)S(1)} copy(f32[12,2]{0,1:T(2,128)} %bitcast.19) | data formatting | bytes 192 | tf_op jit(solution)/shard_map/transpose | solution.py:594
  12.0 0.1 pad.7
  12.0 0.1 scatter.4.columns_any
  12.2 0.0 copy-start.8
  12.2 0.6 %copy-done.8 = f32[136,128]{1,0:T(8,128)} copy-done((f32[136,128]{1,0:T(8,128)}, f32[136,128]{1,0:T(8,128)S(1)}, u32[]{:S(2)}) %copy-start.8) | copy-done | bytes 69656
  12.8 0.0 copy-start.1
  12.8 3.0 %own.1 = (bf16[640,128]{1,0:T(8,128)(2,1)}, f32[96,896]{1,0:T(8,128)}, f32[192,128]{1,0:T(8,128)}, f32[4,128,128]{2,1,0:T(8,128)}) custom-call(f32[4,128,128]{2,1,0:T(8,128)} %pair_any.3, bf16[128,640]{1,0:T(8,128)(2,1)} %tri_any.3, bf16[384,1152]{1,0:T(8,128)(2,1)} %qkv_ref.3, f32[4,384]{1,0:T(4,128)} %single_any.3, f32[8,128]{1,0:T(8,128)} %get-tuple-element.41.frame_any, ...), custom_call_target="tpu_custom_call" | custom-call | flops 16777216 | bytes 16777216 | tf_op jit(solution)/shard_map/own/pallas_call | solution.py:539
  15.8 0.0 copy-start.3
  15.8 0.0 copy-start.5
  15.8 7.7 %all-to-all-done = bf16[32,8,768]{2,1,0:T(8,128)(2,1)S(1)} async-done(((bf16[32,8,768]{2,1,0:T(8,128)(2,1)}), bf16[32,8,768]{2,1,0:T(8,128)(2,1)S(1)}, u32[]{:S(2)}, u32[]{:S(2)}) %all-to-all-start) | async-done | bytes 393248 | tf_op jit(solution)/shard_map/all_to_all | solution.py:565
  23.5 1.7 %product.1 = (bf16[256,256]{1,0:T(8,128)(2,1)}, bf16[256,256]{1,0:T(8,128)(2,1)S(1)}) custom-call(bf16[256,768]{1,0:T(8,128)(2,1)S(1)} %bitcast.12), custom_call_target="tpu_custom_call" | custom-call | tf_op jit(solution)/shard_map/product/pallas_call | solution.py:539
  25.2 0.0 copy-start.6
  25.2 2.6 %all-to-all-start.1 = ((bf16[32,8,256]{2,1,0:T(8,128)(2,1)}), bf16[32,8,256]{2,1,0:T(8,128)(2,1)S(1)}, u32[]{:S(2)}, u32[]{:S(2)}) async-start(bf16[32,8,256]{2,1,0:T(8,128)(2,1)} %bitcast.6), calls=%async_computation.1 | async-start | bytes 262144 | tf_op jit(solution)/shard_map/all_to_all | solution.py:565
  27.9 0.0 copy-done.6
  27.9 0.0 copy-done
  27.9 0.0 copy-start.2
  27.9 0.9 %copy-done.2 = f32[192,128]{1,0:T(8,128)S(1)} copy-done((f32[192,128]{1,0:T(8,128)S(1)}, f32[192,128]{1,0:T(8,128)}, u32[]{:S(2)}) %copy-start.2) | copy-done | bytes 98328
  28.8 0.0 copy-start.4
  28.8 1.0 %copy-done.4 = f32[96,896]{1,0:T(8,128)S(1)} copy-done((f32[96,896]{1,0:T(8,128)S(1)}, f32[96,896]{1,0:T(8,128)}, u32[]{:S(2)}) %copy-start.4) | copy-done | bytes 344088
  29.8 0.0 copy-start.7
  29.8 0.9 %copy-done.7 = bf16[256,256]{1,0:T(8,128)(2,1)S(1)} copy-done((bf16[256,256]{1,0:T(8,128)(2,1)S(1)}, bf16[256,256]{1,0:T(8,128)(2,1)}, u32[]{:S(2)}) %copy-start.7) | copy-done | bytes 131096
  30.7 1.3 %prepare.1 = (f32[96,128]{1,0:T(8,128)S(1)}, f32[128,640]{1,0:T(8,128)S(1)}) custom-call(bf16[256,256]{1,0:T(8,128)(2,1)S(1)} %copy-done.7, f32[96,896]{1,0:T(8,128)S(1)} %copy-done.4, bf16[384,1152]{1,0:T(8,128)(2,1)S(1)} %copy-done, f32[192,128]{1,0:T(8,128)S(1)} %copy-done.2), custom_call_target="tpu_custom_call" | custom-call | flops 113246208 | bytes 8388608 | tf_op jit(solution)/shard_map/prepare/pallas_call | solution.py:539
  31.9 4.2 %all-to-all-done.1 = bf16[32,8,256]{2,1,0:T(8,128)(2,1)S(1)} async-done(((bf16[32,8,256]{2,1,0:T(8,128)(2,1)}), bf16[32,8,256]{2,1,0:T(8,128)(2,1)S(1)}, u32[]{:S(2)}, u32[]{:S(2)}) %all-to-all-start.1) | async-done | bytes 131104 | tf_op jit(solution)/shard_map/all_to_all | solution.py:565
  36.1 0.0 copy-done.1
  36.1 0.0 copy-done.3
  36.1 0.0 copy-done.5
  36.1 2.6 %update.1 = (f32[4,128,128]{2,1,0:T(8,128)}, bf16[512,128]{1,0:T(8,128)(2,1)S(1)}, f32[96,128]{1,0:T(8,128)S(1)}, f32[8,384]{1,0:T(8,128)S(1)}, f32[8,128]{1,0:T(8,128)S(1)}, /*index=5*/bf16[256,256]{1,0:T(8,128)(2,1)S(1)}) custom-call(bf16[256,256]{1,0:T(8,128)(2,1)S(1)} %bitcast.14, ...), custom_call_target="tpu_custom_call", output_to_operand_aliasing={{0}: (1, {})} | custom-call | tf_op jit(solution)/shard_map/update/pallas_call | solution.py:539
  38.7 10.0 %all_to_all.15 = bf16[32,8,256]{2,1,0:T(8,128)(2,1)S(1)} all-to-all(bf16[32,8,256]{2,1,0:T(8,128)(2,1)S(1)} %bitcast.15), channel_id=1, replica_groups=mesh['grp'=1,'row'=32] {'row'}, dimensions={0} | all-to-all | bytes 262144 | tf_op jit(solution)/shard_map/all_to_all | solution.py:565
  48.7 2.8 %last.1 = (f32[4,384]{1,0:T(4,128)}, f32[4,9]{1,0:T(4,128)}, f32[3,4]{1,0:T(4,128)}) custom-call(bf16[256,256]{1,0:T(8,128)(2,1)S(1)} %bitcast.13, bf16[512,128]{1,0:T(8,128)(2,1)S(1)} %get-tuple-element.57.half_ref, f32[96,128]{1,0:T(8,128)S(1)} %get-tuple-element.58.bias_ref, f32[8,384]{1,0:T(8,128)S(1)} %get-tuple-element.59.state_ref, ...), custom_call_target="tpu_custom_call" | custom-call | tf_op jit(solution)/shard_map/last/pallas_call | solution.py:539
  (1 shorter events, 0.0 us)
Async XLA Ops:
  3.0 24.8 %copy-start = (bf16[384,1152]{1,0:T(8,128)(2,1)S(1)}, bf16[384,1152]{1,0:T(8,128)(2,1)}, u32[]{:S(2)}) copy-start(bf16[384,1152]{1,0:T(8,128)(2,1)} %qkv_ref.3) | copy-start | bytes 2654212
  3.0 20.5 %all-to-all-start = ((bf16[32,8,768]{2,1,0:T(8,128)(2,1)}), bf16[32,8,768]{2,1,0:T(8,128)(2,1)S(1)}, u32[]{:S(2)}, u32[]{:S(2)}) async-start(bf16[32,8,768]{2,1,0:T(8,128)(2,1)} %bitcast.16), calls=%async_computation | async-start | bytes 786432 | tf_op jit(solution)/shard_map/all_to_all | solution.py:565
  12.2 0.6 %copy-start.8 = (f32[136,128]{1,0:T(8,128)}, f32[136,128]{1,0:T(8,128)S(1)}, u32[]{:S(2)}) copy-start(f32[136,128]{1,0:T(8,128)S(1)} %scatter.4.columns_any) | copy-start | bytes 208900
  12.8 23.3 %copy-start.1 = (bf16[2112,384]{1,0:T(8,128)(2,1)S(1)}, bf16[2112,384]{1,0:T(8,128)(2,1)}, u32[]{:S(2)}) copy-start(bf16[2112,384]{1,0:T(8,128)(2,1)} %out_weight_ref.3) | copy-start | bytes 4866052
  15.8 20.3 %copy-start.3 = (f32[192,128]{1,0:T(8,128)S(1)}, f32[192,128]{1,0:T(8,128)}, u32[]{:S(2)}) copy-start(f32[192,128]{1,0:T(8,128)} %get-tuple-element.52.pack_ref) | copy-start | bytes 294916
  15.8 20.3 %copy-start.5 = (bf16[640,128]{1,0:T(8,128)(2,1)S(1)}, bf16[640,128]{1,0:T(8,128)(2,1)}, u32[]{:S(2)}) copy-start(bf16[640,128]{1,0:T(8,128)(2,1)} %get-tuple-element.49.gate_ref) | copy-start | bytes 491524
  25.2 2.6 %copy-start.6 = (bf16[256,256]{1,0:T(8,128)(2,1)}, bf16[256,256]{1,0:T(8,128)(2,1)S(1)}, u32[]{:S(2)}) copy-start(bf16[256,256]{1,0:T(8,128)(2,1)S(1)} %get-tuple-element.50.recv_ref) | copy-start | bytes 393220
  25.2 10.9 %all-to-all-start.1 = ((bf16[32,8,256]{2,1,0:T(8,128)(2,1)}), bf16[32,8,256]{2,1,0:T(8,128)(2,1)S(1)}, u32[]{:S(2)}, u32[]{:S(2)}) async-start(bf16[32,8,256]{2,1,0:T(8,128)(2,1)} %bitcast.6), calls=%async_computation.1 | async-start | bytes 262144 | tf_op jit(solution)/shard_map/all_to_all | solution.py:565
  27.9 0.9 %copy-start.2 = (f32[192,128]{1,0:T(8,128)S(1)}, f32[192,128]{1,0:T(8,128)}, u32[]{:S(2)}) copy-start(f32[192,128]{1,0:T(8,128)} %get-tuple-element.52.pack_ref) | copy-start | bytes 294916
  28.8 1.0 %copy-start.4 = (f32[96,896]{1,0:T(8,128)S(1)}, f32[96,896]{1,0:T(8,128)}, u32[]{:S(2)}) copy-start(f32[96,896]{1,0:T(8,128)} %get-tuple-element.51.rows_ref) | copy-start | bytes 1032196
  29.8 0.9 %copy-start.7 = (bf16[256,256]{1,0:T(8,128)(2,1)S(1)}, bf16[256,256]{1,0:T(8,128)(2,1)}, u32[]{:S(2)}) copy-start(bf16[256,256]{1,0:T(8,128)(2,1)} %copy-done.6) | copy-start | bytes 393220

commit v6 on v5

--- a/solution.py
+++ b/solution.py
@@ -135,13 +135,13 @@
             if low < high:
                 values = x_ref[:, first + low - t * lanes : first + high - t * lanes]
                 pieces.append(dot(onehot((j == s * r + q - t * r) & ((q >> log2(r)) == t)), values))
-        return (pieces[0] if len(pieces) == 1 else jnp.concatenate(pieces, axis=1)).astype(bf16)
+        return pieces[0] if len(pieces) == 1 else jnp.concatenate(pieces, axis=1)
     total = None
     for t in range(lanes // SLOT):
         values = x_ref[:, first + t * SLOT + start : first + t * SLOT + stop]
         one = dot(onehot(j == s * r + t * rows + q), values)
         total = one if total is None else total + one
-    return total.astype(bf16)
+    return total
 
 
 def frame_pieces(frame):
@@ -153,8 +153,47 @@
 
 
 def slots_of(state, frame):
-    both = jnp.concatenate([state, frame_pieces(frame)], axis=1)
+    _, lane = grid_of((IP, 128))
+    tail = state[:, 256:CS]
+    mask = jnp.where(lane == 127, frame[:, MASK_AT : MASK_AT + 1], 0.0)
+    moved = jnp.where((lane >= 112) & (lane < 120), pltpu.roll(tail, 120, 1), mask)
+    last = jnp.where(lane < 96, frame_pieces(frame), moved)
+    both = jnp.concatenate([state[:, 0:256], jnp.where(lane < 120, tail, mask), last], axis=1)
     return jnp.concatenate([both, jnp.zeros_like(both)], axis=0).astype(bf16)
+
+
+def state_of(slots):
+    _, lane = grid_of((slots.shape[0], 128))
+    tail = jnp.where(lane < 120, slots[:, 256:384], pltpu.roll(slots[:, 384:512], 8, 1))
+    return jnp.concatenate([slots[:, 0:256], tail], axis=1).astype(bf16)
+
+
+def half_rows(slots, w, r):
+    rows = 2 * w
+    x, i = grid_of((16, 16))
+    parity = (x >> log2(rows)) & 1
+    blocks = []
+    for at in range(2 * r // rows):
+        b = (x & (rows - 1)) * (2 * r // rows) + at
+        total = None
+        for quarter in range(4):
+            take = onehot((i == (b & (r - 1))) & (parity + 2 * (b >> log2(r)) == quarter))
+            one = dot(take, slots[:, quarter * 128 : (quarter + 1) * 128])
+            total = one if total is None else total + one
+        blocks.append(total)
+    return (blocks[0] if len(blocks) == 1 else jnp.concatenate(blocks, axis=1)).astype(bf16)
+
+
+def quarter_of(x, first, second, w, r, n):
+    rows = 2 * w
+    j, row = grid_of((n * r, n * rows))
+    total = None
+    for at in range(2 * r // rows):
+        b = (row & (rows - 1)) * (2 * r // rows) + at
+        take = onehot((j == (row >> log2(rows)) * r + (b & (r - 1))) & ((b >> log2(r)) == second))
+        one = dot(take, x[:, first + at * 128 : first + (at + 1) * 128])
+        total = one if total is None else total + one
+    return total
 
 
 def fill_rows(out_ref, first, tile):
@@ -223,15 +262,16 @@
         frame = jnp.where((row == i) & (lane == MASK_AT), mask_ref[i].astype(f32), frame)
         frame = jnp.where((row == i) & (lane == CHAIN_AT), chain_ref[i].astype(f32), frame)
     frame_ref[...] = frame
-    fill_rows(send_ref, r * count, spread_rows(slots_of(pad_state(single_ref), frame), w, r))
+    fill_rows(send_ref, r * count, half_rows(slots_of(pad_state(single_ref), frame), w, r))
 
 
 def product_kernel(w, n, r, recv_ref, send_ref, slots_ref):
     count = n * r
     slots_ref[...] = recv_ref[:, r * count :]
     rows = 2 * w
-    pieces = natural_rows(recv_ref, r * count, w, r, n, CS, SLOT)
-    mask = dot_nt(piece_select(16), pieces)[MASK_AT : MASK_AT + 1, :]
+    pieces = quarter_of(recv_ref, r * count, 1, w, r, n).astype(bf16)
+    _, lane = grid_of((16, 128))
+    mask = dot_nt(onehot(lane == 127), pieces)[0:1, :]
     mask = jnp.concatenate([mask] * r, axis=1)
     order = swap_rows(n * rows, rows)
     sides = (dot(order, recv_ref[:, 0 : r * count]) * mask).astype(bf16)
@@ -298,10 +338,10 @@
 
 def logits_and_values(slots, own, frame, qkv, columns):
     query_rows, lengths = own
-    pieces = slots[:, CS:SLOT]
+    pieces = slots[:, CS:SLOT].astype(bf16)
     entry = dot(pieces, piece_select(128, True))
     rows = dot_nt(piece_select(16), pieces)
-    keys = dot(slots[:, 0:CS], qkv)
+    keys = dot(state_of(slots), qkv)
     points = H * PQ
     first = 3 * H * CHEAD + 3 * points
     _, lane = grid_of((keys.shape[0], 128))
@@ -459,8 +499,11 @@
     back.wait()
 
 
-def prepare_kernel(w, n, r, recv_ref, rows_ref, qkv_ref, pack_ref, logits_ref, values_ref):
-    slots = natural_rows(recv_ref, 0, w, r, n)
+def prepare_kernel(w, n, r, mine_ref, other_ref, rows_ref, qkv_ref, pack_ref, logits_ref, values_ref):
+    odd = pack_ref[POINT_WEIGHT + 1 : POINT_WEIGHT + 2, 0:1] > 0.5
+    mine, other = mine_ref[...].astype(f32), other_ref[...].astype(f32)
+    halves = [jnp.where(odd, other, mine).astype(bf16), jnp.where(odd, mine, other).astype(bf16)]
+    slots = jnp.concatenate([quarter_of(halves[q & 1], 0, q >> 1, w, r, n) for q in range(4)], axis=1)
     logits, values = logits_and_values(
         slots, (rows_ref[:, 0:768], rows_ref[:, 768:769]), pack_ref[FRAME : FRAME + IP], qkv_ref[...],
         pack_ref[BIAS : BIAS + ROWS],
@@ -572,7 +615,7 @@
     sent, frame = call(
         functools.partial(gate_kernel, w, n),
         "gate",
-        [((n * rows, r * count + lanes), bf16), ((IP, 128), f32)],
+        [((n * rows, r * count + lanes // 2), bf16), ((IP, 128), f32)],
         [pair, tri_weight, single, quats, translate, res_mask, chain_ids],
         outside=range(7),
         scratch=[
@@ -593,6 +636,7 @@
     point_weight = head_gamma * (math.sqrt(2.0 / (9.0 * PQ)) * 0.5 * third)
     columns = jnp.pad(jnp.repeat(chain_bias.T, IP, axis=0), ((0, CH - ROWS + IP), (ROWS, 126 - ROWS)))
     columns = columns.at[CH, 0 : H * PQ].set(jnp.repeat(point_weight, PQ))
+    columns = columns.at[CH + 1, 0].set((lax.axis_index("row") & 1).astype(f32))
     gate, query_rows, pack, pair_copy = call(
         own_kernel,
         "own",
@@ -626,16 +670,17 @@
     formed, slots = call(
         functools.partial(product_kernel, w, n, r),
         "product",
-        [((n * rows, (r // 2) * count), bf16), ((n * rows, lanes), bf16)],
+        [((n * rows, (r // 2) * count), bf16), ((n * rows, lanes // 2), bf16)],
         [received],
         limit=limit,
     )
     products = exchange(formed)
+    other = lax.ppermute(slots, "row", [(i, i ^ 1) for i in range(n)])
     logits, values = call(
         functools.partial(prepare_kernel, w, n, r),
         "prepare",
         [((ROWS, count), f32), ((count, 640), f32)],
-        [slots, query_rows, qkv_weight, pack],
+        [slots, other, query_rows, qkv_weight, pack],
         limit=limit,
         flops=2 * count * CS * 1152,
         moved=8 * 2**20,

time: 52 us -> 50.9 us (0.979)
  local copies, waits for them, and re-layouts: 4.54 us -> 3.74 us
  waiting for transfers between devices: 11.9 us -> 11.2 us
    all_to_all x2, waiting for transfers between devices: 11.9 us -> 10.1 us  [exchange(): got = lax.all_to_all(sent.reshape(n, rows, width), 'row', 0, 0, tiled=True)]
    ppermute x0 -> x1, waiting for transfers between devices: none -> 1.14 us  [local(): other = lax.ppermute(slots, 'row', [(i, i ^ 1) for i in range(n)])]
    unnamed x18 -> x14, local copies, waits for them, and re-layouts: 3.4 us -> 2.52 us
  transfers between devices with their start and end apart: 2 -> 3, of which waited for: 2 -> 3; matrix products, arithmetic and copies ran while one was open for 4% -> 4% of each run, Pallas kernels for 8% -> 9%
where the time goes in v6:
time: 50.9 us; the launch traced here: 50.5 us
  Pallas kernels  13.9 us (27%)
  waiting for transfers between devices  11.2 us (22%)
  blocking collectives  10.2 us (20%)
  starting transfers between devices  10 us (20%)
  local copies, waits for them, and re-layouts  3.74 us (7%)
  between operations  0.74 us (1%)
  other arithmetic  0.66 us (1%)
    pallas_call x6, Pallas kernels, call(): pl.pallas_call(body, name=name, out_shape=[jax.ShapeDtypeStruct(s, d) for...  13.9 us
    all_to_all x1, blocking collectives, exchange(): got = lax.all_to_all(sent.reshape(n, rows, width), 'row', 0, 0, tiled=True)  10.2 us
    all_to_all x2, waiting for transfers between devices, exchange(): got = lax.all_to_all(sent.reshape(n, rows, width), 'row', 0, 0, tiled=True)  10.1 us
    all_to_all x2, starting transfers between devices, exchange(): got = lax.all_to_all(sent.reshape(n, rows, width), 'row', 0, 0, tiled=True)  9.86 us
    unnamed x14, local copies, waits for them, and re-layouts  2.52 us
    ppermute x1, waiting for transfers between devices, local(): other = lax.ppermute(slots, 'row', [(i, i ^ 1) for i in range(n)])  1.14 us
  transfers between devices with their start and end apart: 3, of which 3 were waited for; matrix products, arithmetic and copies ran while one was open for 4% of the time, Pallas kernels for 9%

profile of v6, /device:TPU:0, one launch (start us, length us, event | category | flops | bytes accessed | tf_op | source)
XLA Modules:
  0.0 50.5 jit_solution(396455620555672579)
XLA Ops:
  0.6 0.0 copy-start
  0.6 2.5 %gate.1 = (bf16[256,640]{1,0:T(8,128)(2,1)}, f32[8,128]{1,0:T(8,128)}) custom-call(f32[4,128,128]{2,1,0:T(8,128)} %pair_any.3, bf16[128,640]{1,0:T(8,128)(2,1)} %tri_any.3, f32[4,384]{1,0:T(4,128)} %single_any.3, f32[3,4]{1,0:T(4,128)} %quats_any.1, f32[3,4]{1,0:T(4,128)} %translate_any.1, s32[4]{0:T(128)} %mask_any.1, s32[4]{0:T(128)} %chain_any.1), custom_call_target="tpu_custom_call" | custom-call | tf_op jit(solution)/shard_map/gate/pallas_call | solution.py:582
  3.1 7.3 %all-to-all-start = ((bf16[32,8,640]{2,1,0:T(8,128)(2,1)}), bf16[32,8,640]{2,1,0:T(8,128)(2,1)S(1)}, u32[]{:S(2)}, u32[]{:S(2)}) async-start(bf16[32,8,640]{2,1,0:T(8,128)(2,1)} %bitcast.17), calls=%async_computation | async-start | bytes 655360 | tf_op jit(solution)/shard_map/all_to_all | solution.py:608
  10.4 0.7 %broadcast_multiply_fusion = f32[12]{0:T(128)S(1)} fusion(f32[12]{0:T(128)} %param.28), kind=kLoop, calls=%fused_computation.1 | loop fusion | flops 12 | bytes 96 | tf_op jit(solution)/shard_map/mul | solution.py:636
  11.1 0.1 broadcast_in_dim.7
  11.2 0.1 reshape.95
  11.2 0.8 %copy.20 = f32[12,2]{1,0:T(8,128)S(1)} copy(f32[12,2]{0,1:T(2,128)} %bitcast.20) | data formatting | bytes 192 | tf_op jit(solution)/shard_map/transpose | solution.py:637
  12.0 0.1 pad.11
  12.1 0.1 scatter.6
  12.2 0.1 scatter.9.columns_any
  12.3 0.0 copy-start.6
  12.3 0.6 %copy-done.6 = f32[136,128]{1,0:T(8,128)} copy-done((f32[136,128]{1,0:T(8,128)}, f32[136,128]{1,0:T(8,128)S(1)}, u32[]{:S(2)}) %copy-start.6) | copy-done | bytes 69656
  13.0 0.0 copy-start.1
  13.0 3.0 %own.1 = (bf16[640,128]{1,0:T(8,128)(2,1)}, f32[96,896]{1,0:T(8,128)}, f32[192,128]{1,0:T(8,128)}, f32[4,128,128]{2,1,0:T(8,128)}) custom-call(f32[4,128,128]{2,1,0:T(8,128)} %pair_any.3, bf16[128,640]{1,0:T(8,128)(2,1)} %tri_any.3, bf16[384,1152]{1,0:T(8,128)(2,1)} %qkv_ref.3, f32[4,384]{1,0:T(4,128)} %single_any.3, f32[8,128]{1,0:T(8,128)} %get-tuple-element.53.frame_any, ...), custom_call_target="tpu_custom_call" | custom-call | flops 16777216 | bytes 16777216 | tf_op jit(solution)/shard_map/own/pallas_call | solution.py:582
  16.0 0.0 copy-start.3
  16.0 0.0 copy-start.5
  16.0 6.4 %all-to-all-done = bf16[32,8,640]{2,1,0:T(8,128)(2,1)S(1)} async-done(((bf16[32,8,640]{2,1,0:T(8,128)(2,1)}), bf16[32,8,640]{2,1,0:T(8,128)(2,1)S(1)}, u32[]{:S(2)}, u32[]{:S(2)}) %all-to-all-start) | async-done | bytes 327712 | tf_op jit(solution)/shard_map/all_to_all | solution.py:608
  22.4 1.7 %product.1 = (bf16[256,256]{1,0:T(8,128)(2,1)}, bf16[256,128]{1,0:T(8,128)(2,1)S(1)}) custom-call(bf16[256,640]{1,0:T(8,128)(2,1)S(1)} %bitcast.13), custom_call_target="tpu_custom_call" | custom-call | tf_op jit(solution)/shard_map/product/pallas_call | solution.py:582
  24.1 2.6 %all-to-all-start.1 = ((bf16[32,8,256]{2,1,0:T(8,128)(2,1)}), bf16[32,8,256]{2,1,0:T(8,128)(2,1)S(1)}, u32[]{:S(2)}, u32[]{:S(2)}) async-start(bf16[32,8,256]{2,1,0:T(8,128)(2,1)} %bitcast.7), calls=%async_computation.1 | async-start | bytes 262144 | tf_op jit(solution)/shard_map/all_to_all | solution.py:608
  26.6 0.2 collective-permute-start
  26.8 1.1 %collective-permute-done.other_ref = bf16[256,128]{1,0:T(8,128)(2,1)S(1)} collective-permute-done((bf16[256,128]{1,0:T(8,128)(2,1)S(1)}, bf16[256,128]{1,0:T(8,128)(2,1)S(1)}, u32[]{:S(2)}, u32[]{:S(2)}) %collective-permute-start) | collective-permute-done | bytes 65568 | tf_op jit(solution)/shard_map/ppermute | solution.py:678
  28.0 0.0 copy-done
  28.0 0.0 copy-start.2
  28.0 0.9 %copy-done.2 = f32[192,128]{1,0:T(8,128)S(1)} copy-done((f32[192,128]{1,0:T(8,128)S(1)}, f32[192,128]{1,0:T(8,128)}, u32[]{:S(2)}) %copy-start.2) | copy-done | bytes 98328
  28.9 0.0 copy-start.4
  28.9 1.0 %copy-done.4 = f32[96,896]{1,0:T(8,128)S(1)} copy-done((f32[96,896]{1,0:T(8,128)S(1)}, f32[96,896]{1,0:T(8,128)}, u32[]{:S(2)}) %copy-start.4) | copy-done | bytes 344088
  29.8 1.3 %prepare.1 = (f32[96,128]{1,0:T(8,128)S(1)}, f32[128,640]{1,0:T(8,128)S(1)}) custom-call(bf16[256,128]{1,0:T(8,128)(2,1)S(1)} %get-tuple-element.62.mine_ref, bf16[256,128]{1,0:T(8,128)(2,1)S(1)} %collective-permute-done.other_ref, f32[96,896]{1,0:T(8,128)S(1)} %copy-done.4, bf16[384,1152]{1,0:T(8,128)(2,1)S(1)} %copy-done, f32[192,128]{1,0:T(8,128)S(1)} %copy-done.2), custom_call_target="tpu_custom_call" | custom-call | flops 113246208 | bytes 8388608 | tf_op jit(solution)/shard_map/prepare/pallas_call | solution.py:582
  31.2 3.7 %all-to-all-done.1 = bf16[32,8,256]{2,1,0:T(8,128)(2,1)S(1)} async-done(((bf16[32,8,256]{2,1,0:T(8,128)(2,1)}), bf16[32,8,256]{2,1,0:T(8,128)(2,1)S(1)}, u32[]{:S(2)}, u32[]{:S(2)}) %all-to-all-start.1) | async-done | bytes 131104 | tf_op jit(solution)/shard_map/all_to_all | solution.py:608
  34.9 0.0 copy-done.1
  34.9 0.0 copy-done.3
  34.9 0.0 copy-done.5
  34.9 2.6 %update.1 = (f32[4,128,128]{2,1,0:T(8,128)}, bf16[512,128]{1,0:T(8,128)(2,1)S(1)}, f32[96,128]{1,0:T(8,128)S(1)}, f32[8,384]{1,0:T(8,128)S(1)}, f32[8,128]{1,0:T(8,128)S(1)}, /*index=5*/bf16[256,256]{1,0:T(8,128)(2,1)S(1)}) custom-call(bf16[256,256]{1,0:T(8,128)(2,1)S(1)} %bitcast.15, ...), custom_call_target="tpu_custom_call", output_to_operand_aliasing={{0}: (1, {})} | custom-call | tf_op jit(solution)/shard_map/update/pallas_call | solution.py:582
  37.5 10.2 %all_to_all.15 = bf16[32,8,256]{2,1,0:T(8,128)(2,1)S(1)} all-to-all(bf16[32,8,256]{2,1,0:T(8,128)(2,1)S(1)} %bitcast.16), channel_id=1, replica_groups=mesh['grp'=1,'row'=32] {'row'}, dimensions={0} | all-to-all | bytes 262144 | tf_op jit(solution)/shard_map/all_to_all | solution.py:608
  47.7 2.8 %last.1 = (f32[4,384]{1,0:T(4,128)}, f32[4,9]{1,0:T(4,128)}, f32[3,4]{1,0:T(4,128)}) custom-call(bf16[256,256]{1,0:T(8,128)(2,1)S(1)} %bitcast.14, bf16[512,128]{1,0:T(8,128)(2,1)S(1)} %get-tuple-element.69.half_ref, f32[96,128]{1,0:T(8,128)S(1)} %get-tuple-element.70.bias_ref, f32[8,384]{1,0:T(8,128)S(1)} %get-tuple-element.71.state_ref, ...), custom_call_target="tpu_custom_call" | custom-call | tf_op jit(solution)/shard_map/last/pallas_call | solution.py:582
  (1 shorter events, 0.0 us)
Async XLA Ops:
  0.6 27.3 %copy-start = (bf16[384,1152]{1,0:T(8,128)(2,1)S(1)}, bf16[384,1152]{1,0:T(8,128)(2,1)}, u32[]{:S(2)}) copy-start(bf16[384,1152]{1,0:T(8,128)(2,1)} %qkv_ref.3) | copy-start | bytes 2654212
  3.1 19.3 %all-to-all-start = ((bf16[32,8,640]{2,1,0:T(8,128)(2,1)}), bf16[32,8,640]{2,1,0:T(8,128)(2,1)S(1)}, u32[]{:S(2)}, u32[]{:S(2)}) async-start(bf16[32,8,640]{2,1,0:T(8,128)(2,1)} %bitcast.17), calls=%async_computation | async-start | bytes 655360 | tf_op jit(solution)/shard_map/all_to_all | solution.py:608
  12.3 0.6 %copy-start.6 = (f32[136,128]{1,0:T(8,128)}, f32[136,128]{1,0:T(8,128)S(1)}, u32[]{:S(2)}) copy-start(f32[136,128]{1,0:T(8,128)S(1)} %scatter.9.columns_any) | copy-start | bytes 208900
  13.0 21.9 %copy-start.1 = (bf16[2112,384]{1,0:T(8,128)(2,1)S(1)}, bf16[2112,384]{1,0:T(8,128)(2,1)}, u32[]{:S(2)}) copy-start(bf16[2112,384]{1,0:T(8,128)(2,1)} %out_weight_ref.3) | copy-start | bytes 4866052
  16.0 18.9 %copy-start.3 = (f32[192,128]{1,0:T(8,128)S(1)}, f32[192,128]{1,0:T(8,128)}, u32[]{:S(2)}) copy-start(f32[192,128]{1,0:T(8,128)} %get-tuple-element.64.pack_ref) | copy-start | bytes 294916
  16.0 18.9 %copy-start.5 = (bf16[640,128]{1,0:T(8,128)(2,1)S(1)}, bf16[640,128]{1,0:T(8,128)(2,1)}, u32[]{:S(2)}) copy-start(bf16[640,128]{1,0:T(8,128)(2,1)} %get-tuple-element.61.gate_ref) | copy-start | bytes 491524
  24.1 10.8 %all-to-all-start.1 = ((bf16[32,8,256]{2,1,0:T(8,128)(2,1)}), bf16[32,8,256]{2,1,0:T(8,128)(2,1)S(1)}, u32[]{:S(2)}, u32[]{:S(2)}) async-start(bf16[32,8,256]{2,1,0:T(8,128)(2,1)} %bitcast.7), calls=%async_computation.1 | async-start | bytes 262144 | tf_op jit(solution)/shard_map/all_to_all | solution.py:608
  26.6 1.3 %collective-permute-start = (bf16[256,128]{1,0:T(8,128)(2,1)S(1)}, bf16[256,128]{1,0:T(8,128)(2,1)S(1)}, u32[]{:S(2)}, u32[]{:S(2)}) collective-permute-start(bf16[256,128]{1,0:T(8,128)(2,1)S(1)} %get-tuple-element.62.mine_ref), channel_id=1, source_target_pairs={{0,1},{1,0},{2,3},{3,2},{4,5},{5,4},{6,7},{7,6},{8,9},{9,8},{10,11... | collective-permute-start | bytes 196616 | tf_op jit(solution)/shard_map/ppermute | solution.py:678
  28.0 0.9 %copy-start.2 = (f32[192,128]{1,0:T(8,128)S(1)}, f32[192,128]{1,0:T(8,128)}, u32[]{:S(2)}) copy-start(f32[192,128]{1,0:T(8,128)} %get-tuple-element.64.pack_ref) | copy-start | bytes 294916
  28.9 1.0 %copy-start.4 = (f32[96,896]{1,0:T(8,128)S(1)}, f32[96,896]{1,0:T(8,128)}, u32[]{:S(2)}) copy-start(f32[96,896]{1,0:T(8,128)} %get-tuple-element.63.rows_ref) | copy-start | bytes 1032196

commit v7 on v6

--- a/solution.py
+++ b/solution.py
@@ -265,7 +265,7 @@
     fill_rows(send_ref, r * count, half_rows(slots_of(pad_state(single_ref), frame), w, r))
 
 
-def product_kernel(w, n, r, recv_ref, send_ref, slots_ref):
+def product_kernel(w, n, r, recv_ref, send_ref, slots_ref, right_ref):
     count = n * r
     slots_ref[...] = recv_ref[:, r * count :]
     rows = 2 * w
@@ -274,19 +274,39 @@
     mask = dot_nt(onehot(lane == 127), pieces)[0:1, :]
     mask = jnp.concatenate([mask] * r, axis=1)
     order = swap_rows(n * rows, rows)
-    sides = (dot(order, recv_ref[:, 0 : r * count]) * mask).astype(bf16)
+    sides = dot(order, recv_ref[:, 0 : r * count]) * mask
     row, column = grid_of((count, count))
     to_natural = onehot(row == (column & (n - 1)) * r + (column >> log2(n)))
 
     def stacked(block):
-        part = sides[block * n : (block + 1) * n]
+        part = sides[block * n : (block + 1) * n].astype(bf16)
         return jnp.concatenate([part[:, i * count : (i + 1) * count] for i in range(r)], axis=0)
+
+    if by_channel(w, count):
+        for c in range(w):
+            for i in range(r):
+                part = sides[(w + c) * n : (w + c + 1) * n, i * count : (i + 1) * count]
+                right_ref[c, pl.ds(i, n, stride=r), :] = part
+
+    def natural(c):
+        if by_channel(w, count):
+            return right_ref[c, 0:128].astype(bf16)
+        return dot(to_natural, stacked(w + c)).astype(bf16)
 
     half = r // 2
     products = []
     for c in range(w):
-        right = dot(to_natural, stacked(w + c)).astype(bf16)
-        products.append(dot_nt(stacked(c), right).astype(bf16))
+        products.append(dot_nt(stacked(c), natural(c)))
+    if by_channel(w, count):
+        for high in range(2):
+            for low in range(half):
+                for c in range(w):
+                    first = (high * half + low) * n
+                    right_ref[low, pl.ds(high * w + c, n, stride=rows), :] = products[c][first : first + n]
+        for low in range(half):
+            send_ref[:, low * count : (low + 1) * count] = right_ref[low].astype(bf16)
+        return
+    products = [product.astype(bf16) for product in products]
     blocks = []
     for high in range(2):
         for c in range(w):
@@ -382,11 +402,11 @@
 def attend(r, logits, values, halves, state, frame, weights):
     top = jnp.max(logits, axis=1, keepdims=True)
     raised = jnp.exp(logits - top)
-    attention = raised / jnp.sum(raised, axis=1, keepdims=True)
-    row, _ = grid_of(attention.shape)
-    parts = [jnp.where((row & (IP - 1)) == i, attention, 0.0).astype(bf16) for i in range(r)]
-    out_pair = dot(jnp.concatenate(parts, axis=1), halves)
-    summed = dot_close(attention, values)
+    share = 1.0 / jnp.sum(raised, axis=1, keepdims=True)
+    row, _ = grid_of(raised.shape)
+    parts = [jnp.where((row & (IP - 1)) == i, raised, 0.0).astype(bf16) for i in range(r)]
+    out_pair = dot(jnp.concatenate(parts, axis=1), halves) * share
+    summed = dot_close(raised, values) * share
     _, lane = grid_of((IP, 640))
     head = jnp.where(lane < 256, lane >> log2(CHEAD), (lane & 127) >> log2(PV))
     gathered = None
@@ -454,8 +474,12 @@
     return jnp.concatenate([pack_ref[first + IP * part : first + IP * (part + 1)] for part in range(3)], axis=1)
 
 
+def by_channel(w, count):
+    return w == 4 and count == 128
+
+
 def own_kernel(
-    pair_any, tri_any, qkv_any, single_any, frame_any, columns_any, tri_out_any, bias_weight_any, frame_weight_any,
+    w, pair_any, tri_any, qkv_any, single_any, frame_any, columns_any, tri_out_any, bias_weight_any, frame_weight_any,
     gate_ref, rows_ref, pack_ref, pair_copy_any,
     pair_ref, gate_weight_ref, qkv_ref, single_ref, columns_ref, tri_out_ref, bias_weight_ref, frame_weight_ref, sems,
 ):
@@ -476,7 +500,13 @@
         copy.wait()
     back = pltpu.make_async_copy(pair_ref, pair_copy_any, sems.at[9])
     back.start()
-    gate_ref[r * count :, :] = tri_out_ref[...]
+    if by_channel(w, count):
+        row, column = grid_of((CH, CH))
+        n = CH // w
+        take = onehot(column == (row & (n - 1)) * w + (row >> log2(n)))
+        gate_ref[r * count :, :] = dot(take, tri_out_ref[...]).astype(bf16)
+    else:
+        gate_ref[r * count :, :] = tri_out_ref[...]
     bias_weight = bias_weight_ref[...]
     spread = [jnp.broadcast_to(bias_weight[h : h + 1], (IP, CH)) for h in range(H)]
     bias_weight = jnp.concatenate(spread + [jnp.zeros((128 - ROWS, CH), f32)], axis=0).T
@@ -514,16 +544,27 @@
 
 def update_kernel(
     w, n, recv_ref, pair_any, gate_ref, logits_ref, values_ref, pack_ref, out_weight_ref,
-    pair_out_any, half_ref, bias_ref, state_ref, new_frame_ref, send_ref, pair_ref, sems,
+    pair_out_any, half_ref, bias_ref, state_ref, new_frame_ref, send_ref, pair_ref, wide_ref, sems,
 ):
     r, count, _ = pair_ref.shape
     load = pltpu.make_async_copy(pair_any, pair_ref, sems.at[0])
     load.start()
+    tri_out = gate_ref[r * count :, :]
     row, column = grid_of((2 * CH, 2 * CH))
     c = row & (CH - 1)
     take = onehot(column == (c >> log2(w)) * 2 * w + (row >> log2(CH)) * w + (c & (w - 1)))
-    product = dot(take, recv_ref[...])
-    tri_out = gate_ref[r * count :, :]
+    if by_channel(w, count):
+        for low in range(2):
+            wide_ref[low] = recv_ref[:, low * count : (low + 1) * count].astype(f32)
+        product = jnp.concatenate(
+            [
+                jnp.concatenate([wide_ref[low, pl.ds(q, n, stride=2 * w), :] for q in range(2 * w)], axis=0)
+                for low in range(2)
+            ],
+            axis=1,
+        )
+    else:
+        product = dot(take, recv_ref[...])
     updates = []
     for high in range(2):
         normed = layer_norm(product[high * CH : (high + 1) * CH], axis=0).astype(bf16)
@@ -638,7 +679,7 @@
     columns = columns.at[CH, 0 : H * PQ].set(jnp.repeat(point_weight, PQ))
     columns = columns.at[CH + 1, 0].set((lax.axis_index("row") & 1).astype(f32))
     gate, query_rows, pack, pair_copy = call(
-        own_kernel,
+        functools.partial(own_kernel, w),
         "own",
         [
             ((r * count + CH, CH), bf16),
@@ -672,6 +713,7 @@
         "product",
         [((n * rows, (r // 2) * count), bf16), ((n * rows, lanes // 2), bf16)],
         [received],
+        scratch=[pltpu.VMEM((w, 256, 128), f32)],
         limit=limit,
     )
     products = exchange(formed)
@@ -700,7 +742,7 @@
         outside=(1,),
         outside_outs=(0,),
         alias={1: 0},
-        scratch=[like(pair), dma((2,))],
+        scratch=[like(pair), pltpu.VMEM((2, 2 * CH, 128), f32), dma((2,))],
         limit=limit,
     )
     received = exchange(sent)

time: 50.9 us -> 50.4 us (level)
  Pallas kernels: 13.9 us -> 13.3 us
    pallas_call x6, Pallas kernels: 13.9 us -> 13.3 us  [call(): pl.pallas_call(body, name=name, out_shape=[jax.ShapeDtypeStruct(s, d) for...]
where the time goes in v7:
time: 50.4 us; the launch traced here: 50 us
  Pallas kernels  13.3 us (26%)
  waiting for transfers between devices  11.2 us (22%)
  blocking collectives  10.2 us (20%)
  starting transfers between devices  10 us (20%)
  local copies, waits for them, and re-layouts  3.74 us (7%)
  between operations  0.74 us (1%)
  other arithmetic  0.66 us (1%)
    pallas_call x6, Pallas kernels, call(): pl.pallas_call(body, name=name, out_shape=[jax.ShapeDtypeStruct(s, d) for...  13.3 us
    all_to_all x1, blocking collectives, exchange(): got = lax.all_to_all(sent.reshape(n, rows, width), 'row', 0, 0, tiled=True)  10.2 us
    all_to_all x2, waiting for transfers between devices, exchange(): got = lax.all_to_all(sent.reshape(n, rows, width), 'row', 0, 0, tiled=True)  10.1 us
    all_to_all x2, starting transfers between devices, exchange(): got = lax.all_to_all(sent.reshape(n, rows, width), 'row', 0, 0, tiled=True)  9.86 us
    unnamed x14, local copies, waits for them, and re-layouts  2.52 us
    ppermute x1, waiting for transfers between devices, local(): other = lax.ppermute(slots, 'row', [(i, i ^ 1) for i in range(n)])  1.14 us
  transfers between devices with their start and end apart: 3, of which 3 were waited for; matrix products, arithmetic and copies ran while one was open for 4% of the time, Pallas kernels for 9%

profile of v7, /device:TPU:0, one launch (start us, length us, event | category | flops | bytes accessed | tf_op | source)
XLA Modules:
  0.0 50.0 jit_solution(5834290402265126979)
XLA Ops:
  0.6 0.0 copy-start
  0.6 2.5 %gate.1 = (bf16[256,640]{1,0:T(8,128)(2,1)}, f32[8,128]{1,0:T(8,128)}) custom-call(f32[4,128,128]{2,1,0:T(8,128)} %pair_any.3, bf16[128,640]{1,0:T(8,128)(2,1)} %tri_any.3, f32[4,384]{1,0:T(4,128)} %single_any.3, f32[3,4]{1,0:T(4,128)} %quats_any.1, f32[3,4]{1,0:T(4,128)} %translate_any.1, s32[4]{0:T(128)} %mask_any.1, s32[4]{0:T(128)} %chain_any.1), custom_call_target="tpu_custom_call" | custom-call | tf_op jit(solution)/shard_map/gate/pallas_call | solution.py:623
  3.1 7.3 %all-to-all-start = ((bf16[32,8,640]{2,1,0:T(8,128)(2,1)}), bf16[32,8,640]{2,1,0:T(8,128)(2,1)S(1)}, u32[]{:S(2)}, u32[]{:S(2)}) async-start(bf16[32,8,640]{2,1,0:T(8,128)(2,1)} %bitcast.17), calls=%async_computation | async-start | bytes 655360 | tf_op jit(solution)/shard_map/all_to_all | solution.py:649
  10.4 0.7 %broadcast_multiply_fusion = f32[12]{0:T(128)S(1)} fusion(f32[12]{0:T(128)} %param.28), kind=kLoop, calls=%fused_computation.1 | loop fusion | flops 12 | bytes 96 | tf_op jit(solution)/shard_map/mul | solution.py:677
  11.1 0.1 broadcast_in_dim.7
  11.2 0.1 reshape.95
  11.2 0.8 %copy.20 = f32[12,2]{1,0:T(8,128)S(1)} copy(f32[12,2]{0,1:T(2,128)} %bitcast.20) | data formatting | bytes 192 | tf_op jit(solution)/shard_map/transpose | solution.py:678
  12.0 0.1 pad.11
  12.1 0.1 scatter.6
  12.2 0.1 scatter.9.columns_any
  12.3 0.0 copy-start.6
  12.3 0.6 %copy-done.6 = f32[136,128]{1,0:T(8,128)} copy-done((f32[136,128]{1,0:T(8,128)}, f32[136,128]{1,0:T(8,128)S(1)}, u32[]{:S(2)}) %copy-start.6) | copy-done | bytes 69656
  13.0 0.0 copy-start.1
  13.0 3.0 %own.1 = (bf16[640,128]{1,0:T(8,128)(2,1)}, f32[96,896]{1,0:T(8,128)}, f32[192,128]{1,0:T(8,128)}, f32[4,128,128]{2,1,0:T(8,128)}) custom-call(f32[4,128,128]{2,1,0:T(8,128)} %pair_any.3, bf16[128,640]{1,0:T(8,128)(2,1)} %tri_any.3, bf16[384,1152]{1,0:T(8,128)(2,1)} %qkv_ref.3, f32[4,384]{1,0:T(4,128)} %single_any.3, f32[8,128]{1,0:T(8,128)} %get-tuple-element.53.frame_any, ...), custom_call_target="tpu_custom_call" | custom-call | flops 16777216 | bytes 16777216 | tf_op jit(solution)/shard_map/own/pallas_call | solution.py:623
  16.0 0.0 copy-start.3
  16.0 0.0 copy-start.5
  16.0 6.4 %all-to-all-done = bf16[32,8,640]{2,1,0:T(8,128)(2,1)S(1)} async-done(((bf16[32,8,640]{2,1,0:T(8,128)(2,1)}), bf16[32,8,640]{2,1,0:T(8,128)(2,1)S(1)}, u32[]{:S(2)}, u32[]{:S(2)}) %all-to-all-start) | async-done | bytes 327712 | tf_op jit(solution)/shard_map/all_to_all | solution.py:649
  22.4 1.3 %product.1 = (bf16[256,256]{1,0:T(8,128)(2,1)}, bf16[256,128]{1,0:T(8,128)(2,1)S(1)}) custom-call(bf16[256,640]{1,0:T(8,128)(2,1)S(1)} %bitcast.13), custom_call_target="tpu_custom_call" | custom-call | tf_op jit(solution)/shard_map/product/pallas_call | solution.py:623
  23.7 2.6 %all-to-all-start.1 = ((bf16[32,8,256]{2,1,0:T(8,128)(2,1)}), bf16[32,8,256]{2,1,0:T(8,128)(2,1)S(1)}, u32[]{:S(2)}, u32[]{:S(2)}) async-start(bf16[32,8,256]{2,1,0:T(8,128)(2,1)} %bitcast.7), calls=%async_computation.1 | async-start | bytes 262144 | tf_op jit(solution)/shard_map/all_to_all | solution.py:649
  26.2 0.2 collective-permute-start
  26.4 1.1 %collective-permute-done.other_ref = bf16[256,128]{1,0:T(8,128)(2,1)S(1)} collective-permute-done((bf16[256,128]{1,0:T(8,128)(2,1)S(1)}, bf16[256,128]{1,0:T(8,128)(2,1)S(1)}, u32[]{:S(2)}, u32[]{:S(2)}) %collective-permute-start) | collective-permute-done | bytes 65568 | tf_op jit(solution)/shard_map/ppermute | solution.py:720
  27.6 0.0 copy-done
  27.6 0.0 copy-start.2
  27.6 0.9 %copy-done.2 = f32[192,128]{1,0:T(8,128)S(1)} copy-done((f32[192,128]{1,0:T(8,128)S(1)}, f32[192,128]{1,0:T(8,128)}, u32[]{:S(2)}) %copy-start.2) | copy-done | bytes 98328
  28.5 0.0 copy-start.4
  28.5 1.0 %copy-done.4 = f32[96,896]{1,0:T(8,128)S(1)} copy-done((f32[96,896]{1,0:T(8,128)S(1)}, f32[96,896]{1,0:T(8,128)}, u32[]{:S(2)}) %copy-start.4) | copy-done | bytes 344088
  29.4 1.3 %prepare.1 = (f32[96,128]{1,0:T(8,128)S(1)}, f32[128,640]{1,0:T(8,128)S(1)}) custom-call(bf16[256,128]{1,0:T(8,128)(2,1)S(1)} %get-tuple-element.62.mine_ref, bf16[256,128]{1,0:T(8,128)(2,1)S(1)} %collective-permute-done.other_ref, f32[96,896]{1,0:T(8,128)S(1)} %copy-done.4, bf16[384,1152]{1,0:T(8,128)(2,1)S(1)} %copy-done, f32[192,128]{1,0:T(8,128)S(1)} %copy-done.2), custom_call_target="tpu_custom_call" | custom-call | flops 113246208 | bytes 8388608 | tf_op jit(solution)/shard_map/prepare/pallas_call | solution.py:623
  30.8 3.7 %all-to-all-done.1 = bf16[32,8,256]{2,1,0:T(8,128)(2,1)S(1)} async-done(((bf16[32,8,256]{2,1,0:T(8,128)(2,1)}), bf16[32,8,256]{2,1,0:T(8,128)(2,1)S(1)}, u32[]{:S(2)}, u32[]{:S(2)}) %all-to-all-start.1) | async-done | bytes 131104 | tf_op jit(solution)/shard_map/all_to_all | solution.py:649
  34.5 0.0 copy-done.1
  34.5 0.0 copy-done.3
  34.5 0.0 copy-done.5
  34.5 2.5 %update.1 = (f32[4,128,128]{2,1,0:T(8,128)}, bf16[512,128]{1,0:T(8,128)(2,1)S(1)}, f32[96,128]{1,0:T(8,128)S(1)}, f32[8,384]{1,0:T(8,128)S(1)}, f32[8,128]{1,0:T(8,128)S(1)}, /*index=5*/bf16[256,256]{1,0:T(8,128)(2,1)S(1)}) custom-call(bf16[256,256]{1,0:T(8,128)(2,1)S(1)} %bitcast.15, ...), custom_call_target="tpu_custom_call", output_to_operand_aliasing={{0}: (1, {})} | custom-call | tf_op jit(solution)/shard_map/update/pallas_call | solution.py:623
  37.0 10.2 %all_to_all.15 = bf16[32,8,256]{2,1,0:T(8,128)(2,1)S(1)} all-to-all(bf16[32,8,256]{2,1,0:T(8,128)(2,1)S(1)} %bitcast.16), channel_id=1, replica_groups=mesh['grp'=1,'row'=32] {'row'}, dimensions={0} | all-to-all | bytes 262144 | tf_op jit(solution)/shard_map/all_to_all | solution.py:649
  47.2 2.7 %last.1 = (f32[4,384]{1,0:T(4,128)}, f32[4,9]{1,0:T(4,128)}, f32[3,4]{1,0:T(4,128)}) custom-call(bf16[256,256]{1,0:T(8,128)(2,1)S(1)} %bitcast.14, bf16[512,128]{1,0:T(8,128)(2,1)S(1)} %get-tuple-element.69.half_ref, f32[96,128]{1,0:T(8,128)S(1)} %get-tuple-element.70.bias_ref, f32[8,384]{1,0:T(8,128)S(1)} %get-tuple-element.71.state_ref, ...), custom_call_target="tpu_custom_call" | custom-call | tf_op jit(solution)/shard_map/last/pallas_call | solution.py:623
  (1 shorter events, 0.0 us)
Async XLA Ops:
  0.6 26.9 %copy-start = (bf16[384,1152]{1,0:T(8,128)(2,1)S(1)}, bf16[384,1152]{1,0:T(8,128)(2,1)}, u32[]{:S(2)}) copy-start(bf16[384,1152]{1,0:T(8,128)(2,1)} %qkv_ref.3) | copy-start | bytes 2654212
  3.1 19.3 %all-to-all-start = ((bf16[32,8,640]{2,1,0:T(8,128)(2,1)}), bf16[32,8,640]{2,1,0:T(8,128)(2,1)S(1)}, u32[]{:S(2)}, u32[]{:S(2)}) async-start(bf16[32,8,640]{2,1,0:T(8,128)(2,1)} %bitcast.17), calls=%async_computation | async-start | bytes 655360 | tf_op jit(solution)/shard_map/all_to_all | solution.py:649
  12.3 0.6 %copy-start.6 = (f32[136,128]{1,0:T(8,128)}, f32[136,128]{1,0:T(8,128)S(1)}, u32[]{:S(2)}) copy-start(f32[136,128]{1,0:T(8,128)S(1)} %scatter.9.columns_any) | copy-start | bytes 208900
  13.0 21.5 %copy-start.1 = (bf16[2112,384]{1,0:T(8,128)(2,1)S(1)}, bf16[2112,384]{1,0:T(8,128)(2,1)}, u32[]{:S(2)}) copy-start(bf16[2112,384]{1,0:T(8,128)(2,1)} %out_weight_ref.3) | copy-start | bytes 4866052
  16.0 18.5 %copy-start.3 = (f32[192,128]{1,0:T(8,128)S(1)}, f32[192,128]{1,0:T(8,128)}, u32[]{:S(2)}) copy-start(f32[192,128]{1,0:T(8,128)} %get-tuple-element.64.pack_ref) | copy-start | bytes 294916
  16.0 18.5 %copy-start.5 = (bf16[640,128]{1,0:T(8,128)(2,1)S(1)}, bf16[640,128]{1,0:T(8,128)(2,1)}, u32[]{:S(2)}) copy-start(bf16[640,128]{1,0:T(8,128)(2,1)} %get-tuple-element.61.gate_ref) | copy-start | bytes 491524
  23.7 10.8 %all-to-all-start.1 = ((bf16[32,8,256]{2,1,0:T(8,128)(2,1)}), bf16[32,8,256]{2,1,0:T(8,128)(2,1)S(1)}, u32[]{:S(2)}, u32[]{:S(2)}) async-start(bf16[32,8,256]{2,1,0:T(8,128)(2,1)} %bitcast.7), calls=%async_computation.1 | async-start | bytes 262144 | tf_op jit(solution)/shard_map/all_to_all | solution.py:649
  26.2 1.3 %collective-permute-start = (bf16[256,128]{1,0:T(8,128)(2,1)S(1)}, bf16[256,128]{1,0:T(8,128)(2,1)S(1)}, u32[]{:S(2)}, u32[]{:S(2)}) collective-permute-start(bf16[256,128]{1,0:T(8,128)(2,1)S(1)} %get-tuple-element.62.mine_ref), channel_id=1, source_target_pairs={{0,1},{1,0},{2,3},{3,2},{4,5},{5,4},{6,7},{7,6},{8,9},{9,8},{10,11... | collective-permute-start | bytes 196616 | tf_op jit(solution)/shard_map/ppermute | solution.py:720
  27.6 0.9 %copy-start.2 = (f32[192,128]{1,0:T(8,128)S(1)}, f32[192,128]{1,0:T(8,128)}, u32[]{:S(2)}) copy-start(f32[192,128]{1,0:T(8,128)} %get-tuple-element.64.pack_ref) | copy-start | bytes 294916
  28.5 1.0 %copy-start.4 = (f32[96,896]{1,0:T(8,128)S(1)}, f32[96,896]{1,0:T(8,128)}, u32[]{:S(2)}) copy-start(f32[96,896]{1,0:T(8,128)} %get-tuple-element.63.rows_ref) | copy-start | bytes 1032196

commit v8 on v7

--- a/solution.py
+++ b/solution.py
@@ -224,13 +224,13 @@
     r, count, _ = pair_ref.shape
     loads = copies(
         sems,
+        (pair_any, pair_ref),
+        (tri_any.at[:, 0 : 4 * CH], tri_ref),
+        (single_any, single_ref),
         (quats_any, quats_ref),
         (translate_any, translate_ref),
         (mask_any, mask_ref),
         (chain_any, chain_ref),
-        (single_any, single_ref),
-        (tri_any.at[:, 0 : 4 * CH], tri_ref),
-        (pair_any, pair_ref),
     )
     row, column = grid_of((2 * CH, 2 * CH))
     d = row >> log2(2 * w)
@@ -599,9 +599,18 @@
 
 def last_kernel(
     w, n, r, recv_ref, half_ref, bias_ref, state_ref, frame_ref, pack_ref, qkv_ref, out_weight_ref,
-    single_out_ref, rotation_ref, translation_ref, scr,
+    single_out_ref, rotation_ref, translation_ref, scr, wide_ref, slots_ref,
 ):
-    slots = natural_rows(recv_ref, 0, w, r, n)
+    if by_channel(w, n * r):
+        for low in range(2):
+            wide_ref[low] = recv_ref[:, low * 128 : (low + 1) * 128].astype(f32)
+        for quarter in range(4):
+            for i in range(r):
+                part = wide_ref[quarter & 1, pl.ds((quarter >> 1) * r + i, n, stride=2 * w), :]
+                slots_ref[quarter, pl.ds(i, n, stride=r), :] = part
+        slots = jnp.concatenate([slots_ref[quarter] for quarter in range(4)], axis=1)
+    else:
+        slots = natural_rows(recv_ref, 0, w, r, n)
     state, frame = state_ref[...], frame_ref[...]
     own = own_side(state, frame, qkv_ref, pack_ref[POINT_WEIGHT : POINT_WEIGHT + 1])
     logits, values = logits_and_values(slots, own, frame, qkv_ref[...], pack_ref[BIAS : BIAS + ROWS])
@@ -751,7 +760,7 @@
         "last",
         [((r, CS), f32), ((r, 9), f32), ((3, r), f32)],
         [received, pair_half, bias, state, frame, pack, qkv_weight, out_weight],
-        scratch=[pltpu.VMEM((128, 128), f32)],
+        scratch=[pltpu.VMEM((128, 128), f32), pltpu.VMEM((2, 256, 128), f32), pltpu.VMEM((4, 128, 128), f32)],
         limit=limit,
     )
     return (pair_out, single_out, rotation.T, translation)

time: 50.4 us -> 50.2 us (level)
  no operation moved by 1% of the time
where the time goes in v8:
time: 50.2 us; the launch traced here: 49.8 us
  Pallas kernels  13.2 us (26%)
  waiting for transfers between devices  11.2 us (22%)
  blocking collectives  10.2 us (20%)
  starting transfers between devices  10 us (20%)
  local copies, waits for them, and re-layouts  3.74 us (7%)
  between operations  0.74 us (1%)
  other arithmetic  0.66 us (1%)
    pallas_call x6, Pallas kernels, call(): pl.pallas_call(body, name=name, out_shape=[jax.ShapeDtypeStruct(s, d) for...  13.2 us
    all_to_all x1, blocking collectives, exchange(): got = lax.all_to_all(sent.reshape(n, rows, width), 'row', 0, 0, tiled=True)  10.2 us
    all_to_all x2, waiting for transfers between devices, exchange(): got = lax.all_to_all(sent.reshape(n, rows, width), 'row', 0, 0, tiled=True)  10.1 us
    all_to_all x2, starting transfers between devices, exchange(): got = lax.all_to_all(sent.reshape(n, rows, width), 'row', 0, 0, tiled=True)  9.86 us
    unnamed x14, local copies, waits for them, and re-layouts  2.52 us
    ppermute x1, waiting for transfers between devices, local(): other = lax.ppermute(slots, 'row', [(i, i ^ 1) for i in range(n)])  1.14 us
  transfers between devices with their start and end apart: 3, of which 3 were waited for; matrix products, arithmetic and copies ran while one was open for 4% of the time, Pallas kernels for 9%

profile of v8, /device:TPU:0, one launch (start us, length us, event | category | flops | bytes accessed | tf_op | source)
XLA Modules:
  0.0 49.8 jit_solution(12464238181030806206)
XLA Ops:
  0.6 0.0 copy-start
  0.6 2.4 %gate.1 = (bf16[256,640]{1,0:T(8,128)(2,1)}, f32[8,128]{1,0:T(8,128)}) custom-call(f32[4,128,128]{2,1,0:T(8,128)} %pair_any.3, bf16[128,640]{1,0:T(8,128)(2,1)} %tri_any.3, f32[4,384]{1,0:T(4,128)} %single_any.3, f32[3,4]{1,0:T(4,128)} %quats_any.1, f32[3,4]{1,0:T(4,128)} %translate_any.1, s32[4]{0:T(128)} %mask_any.1, s32[4]{0:T(128)} %chain_any.1), custom_call_target="tpu_custom_call" | custom-call | tf_op jit(solution)/shard_map/gate/pallas_call | solution.py:632
  3.1 7.3 %all-to-all-start = ((bf16[32,8,640]{2,1,0:T(8,128)(2,1)}), bf16[32,8,640]{2,1,0:T(8,128)(2,1)S(1)}, u32[]{:S(2)}, u32[]{:S(2)}) async-start(bf16[32,8,640]{2,1,0:T(8,128)(2,1)} %bitcast.17), calls=%async_computation | async-start | bytes 655360 | tf_op jit(solution)/shard_map/all_to_all | solution.py:658
  10.4 0.7 %broadcast_multiply_fusion = f32[12]{0:T(128)S(1)} fusion(f32[12]{0:T(128)} %param.28), kind=kLoop, calls=%fused_computation.1 | loop fusion | flops 12 | bytes 96 | tf_op jit(solution)/shard_map/mul | solution.py:686
  11.0 0.1 broadcast_in_dim.7
  11.1 0.1 reshape.95
  11.2 0.8 %copy.20 = f32[12,2]{1,0:T(8,128)S(1)} copy(f32[12,2]{0,1:T(2,128)} %bitcast.20) | data formatting | bytes 192 | tf_op jit(solution)/shard_map/transpose | solution.py:687
  12.0 0.1 pad.11
  12.0 0.1 scatter.6
  12.2 0.1 scatter.9.columns_any
  12.3 0.0 copy-start.6
  12.3 0.6 %copy-done.6 = f32[136,128]{1,0:T(8,128)} copy-done((f32[136,128]{1,0:T(8,128)}, f32[136,128]{1,0:T(8,128)S(1)}, u32[]{:S(2)}) %copy-start.6) | copy-done | bytes 69656
  12.9 0.0 copy-start.1
  12.9 3.0 %own.1 = (bf16[640,128]{1,0:T(8,128)(2,1)}, f32[96,896]{1,0:T(8,128)}, f32[192,128]{1,0:T(8,128)}, f32[4,128,128]{2,1,0:T(8,128)}) custom-call(f32[4,128,128]{2,1,0:T(8,128)} %pair_any.3, bf16[128,640]{1,0:T(8,128)(2,1)} %tri_any.3, bf16[384,1152]{1,0:T(8,128)(2,1)} %qkv_ref.3, f32[4,384]{1,0:T(4,128)} %single_any.3, f32[8,128]{1,0:T(8,128)} %get-tuple-element.53.frame_any, ...), custom_call_target="tpu_custom_call" | custom-call | flops 16777216 | bytes 16777216 | tf_op jit(solution)/shard_map/own/pallas_call | solution.py:632
  15.9 0.0 copy-start.3
  15.9 0.0 copy-start.5
  16.0 6.4 %all-to-all-done = bf16[32,8,640]{2,1,0:T(8,128)(2,1)S(1)} async-done(((bf16[32,8,640]{2,1,0:T(8,128)(2,1)}), bf16[32,8,640]{2,1,0:T(8,128)(2,1)S(1)}, u32[]{:S(2)}, u32[]{:S(2)}) %all-to-all-start) | async-done | bytes 327712 | tf_op jit(solution)/shard_map/all_to_all | solution.py:658
  22.4 1.3 %product.1 = (bf16[256,256]{1,0:T(8,128)(2,1)}, bf16[256,128]{1,0:T(8,128)(2,1)S(1)}) custom-call(bf16[256,640]{1,0:T(8,128)(2,1)S(1)} %bitcast.13), custom_call_target="tpu_custom_call" | custom-call | tf_op jit(solution)/shard_map/product/pallas_call | solution.py:632
  23.6 2.6 %all-to-all-start.1 = ((bf16[32,8,256]{2,1,0:T(8,128)(2,1)}), bf16[32,8,256]{2,1,0:T(8,128)(2,1)S(1)}, u32[]{:S(2)}, u32[]{:S(2)}) async-start(bf16[32,8,256]{2,1,0:T(8,128)(2,1)} %bitcast.7), calls=%async_computation.1 | async-start | bytes 262144 | tf_op jit(solution)/shard_map/all_to_all | solution.py:658
  26.2 0.2 collective-permute-start
  26.4 1.1 %collective-permute-done.other_ref = bf16[256,128]{1,0:T(8,128)(2,1)S(1)} collective-permute-done((bf16[256,128]{1,0:T(8,128)(2,1)S(1)}, bf16[256,128]{1,0:T(8,128)(2,1)S(1)}, u32[]{:S(2)}, u32[]{:S(2)}) %collective-permute-start) | collective-permute-done | bytes 65568 | tf_op jit(solution)/shard_map/ppermute | solution.py:729
  27.5 0.0 copy-done
  27.5 0.0 copy-start.2
  27.5 0.9 %copy-done.2 = f32[192,128]{1,0:T(8,128)S(1)} copy-done((f32[192,128]{1,0:T(8,128)S(1)}, f32[192,128]{1,0:T(8,128)}, u32[]{:S(2)}) %copy-start.2) | copy-done | bytes 98328
  28.4 0.0 copy-start.4
  28.4 1.0 %copy-done.4 = f32[96,896]{1,0:T(8,128)S(1)} copy-done((f32[96,896]{1,0:T(8,128)S(1)}, f32[96,896]{1,0:T(8,128)}, u32[]{:S(2)}) %copy-start.4) | copy-done | bytes 344088
  29.4 1.3 %prepare.1 = (f32[96,128]{1,0:T(8,128)S(1)}, f32[128,640]{1,0:T(8,128)S(1)}) custom-call(bf16[256,128]{1,0:T(8,128)(2,1)S(1)} %get-tuple-element.62.mine_ref, bf16[256,128]{1,0:T(8,128)(2,1)S(1)} %collective-permute-done.other_ref, f32[96,896]{1,0:T(8,128)S(1)} %copy-done.4, bf16[384,1152]{1,0:T(8,128)(2,1)S(1)} %copy-done, f32[192,128]{1,0:T(8,128)S(1)} %copy-done.2), custom_call_target="tpu_custom_call" | custom-call | flops 113246208 | bytes 8388608 | tf_op jit(solution)/shard_map/prepare/pallas_call | solution.py:632
  30.7 3.7 %all-to-all-done.1 = bf16[32,8,256]{2,1,0:T(8,128)(2,1)S(1)} async-done(((bf16[32,8,256]{2,1,0:T(8,128)(2,1)}), bf16[32,8,256]{2,1,0:T(8,128)(2,1)S(1)}, u32[]{:S(2)}, u32[]{:S(2)}) %all-to-all-start.1) | async-done | bytes 131104 | tf_op jit(solution)/shard_map/all_to_all | solution.py:658
  34.4 0.0 copy-done.1
  34.4 0.0 copy-done.3
  34.4 0.0 copy-done.5
  34.4 2.5 %update.1 = (f32[4,128,128]{2,1,0:T(8,128)}, bf16[512,128]{1,0:T(8,128)(2,1)S(1)}, f32[96,128]{1,0:T(8,128)S(1)}, f32[8,384]{1,0:T(8,128)S(1)}, f32[8,128]{1,0:T(8,128)S(1)}, /*index=5*/bf16[256,256]{1,0:T(8,128)(2,1)S(1)}) custom-call(bf16[256,256]{1,0:T(8,128)(2,1)S(1)} %bitcast.15, ...), custom_call_target="tpu_custom_call", output_to_operand_aliasing={{0}: (1, {})} | custom-call | tf_op jit(solution)/shard_map/update/pallas_call | solution.py:632
  37.0 10.2 %all_to_all.15 = bf16[32,8,256]{2,1,0:T(8,128)(2,1)S(1)} all-to-all(bf16[32,8,256]{2,1,0:T(8,128)(2,1)S(1)} %bitcast.16), channel_id=1, replica_groups=mesh['grp'=1,'row'=32] {'row'}, dimensions={0} | all-to-all | bytes 262144 | tf_op jit(solution)/shard_map/all_to_all | solution.py:658
  47.2 2.6 %last.1 = (f32[4,384]{1,0:T(4,128)}, f32[4,9]{1,0:T(4,128)}, f32[3,4]{1,0:T(4,128)}) custom-call(bf16[256,256]{1,0:T(8,128)(2,1)S(1)} %bitcast.14, bf16[512,128]{1,0:T(8,128)(2,1)S(1)} %get-tuple-element.69.half_ref, f32[96,128]{1,0:T(8,128)S(1)} %get-tuple-element.70.bias_ref, f32[8,384]{1,0:T(8,128)S(1)} %get-tuple-element.71.state_ref, ...), custom_call_target="tpu_custom_call" | custom-call | tf_op jit(solution)/shard_map/last/pallas_call | solution.py:632
  (1 shorter events, 0.0 us)
Async XLA Ops:
  0.6 26.9 %copy-start = (bf16[384,1152]{1,0:T(8,128)(2,1)S(1)}, bf16[384,1152]{1,0:T(8,128)(2,1)}, u32[]{:S(2)}) copy-start(bf16[384,1152]{1,0:T(8,128)(2,1)} %qkv_ref.3) | copy-start | bytes 2654212
  3.1 19.3 %all-to-all-start = ((bf16[32,8,640]{2,1,0:T(8,128)(2,1)}), bf16[32,8,640]{2,1,0:T(8,128)(2,1)S(1)}, u32[]{:S(2)}, u32[]{:S(2)}) async-start(bf16[32,8,640]{2,1,0:T(8,128)(2,1)} %bitcast.17), calls=%async_computation | async-start | bytes 655360 | tf_op jit(solution)/shard_map/all_to_all | solution.py:658
  12.3 0.6 %copy-start.6 = (f32[136,128]{1,0:T(8,128)}, f32[136,128]{1,0:T(8,128)S(1)}, u32[]{:S(2)}) copy-start(f32[136,128]{1,0:T(8,128)S(1)} %scatter.9.columns_any) | copy-start | bytes 208900
  12.9 21.5 %copy-start.1 = (bf16[2112,384]{1,0:T(8,128)(2,1)S(1)}, bf16[2112,384]{1,0:T(8,128)(2,1)}, u32[]{:S(2)}) copy-start(bf16[2112,384]{1,0:T(8,128)(2,1)} %out_weight_ref.3) | copy-start | bytes 4866052
  15.9 18.5 %copy-start.3 = (f32[192,128]{1,0:T(8,128)S(1)}, f32[192,128]{1,0:T(8,128)}, u32[]{:S(2)}) copy-start(f32[192,128]{1,0:T(8,128)} %get-tuple-element.64.pack_ref) | copy-start | bytes 294916
  15.9 18.5 %copy-start.5 = (bf16[640,128]{1,0:T(8,128)(2,1)S(1)}, bf16[640,128]{1,0:T(8,128)(2,1)}, u32[]{:S(2)}) copy-start(bf16[640,128]{1,0:T(8,128)(2,1)} %get-tuple-element.61.gate_ref) | copy-start | bytes 491524
  23.6 10.8 %all-to-all-start.1 = ((bf16[32,8,256]{2,1,0:T(8,128)(2,1)}), bf16[32,8,256]{2,1,0:T(8,128)(2,1)S(1)}, u32[]{:S(2)}, u32[]{:S(2)}) async-start(bf16[32,8,256]{2,1,0:T(8,128)(2,1)} %bitcast.7), calls=%async_computation.1 | async-start | bytes 262144 | tf_op jit(solution)/shard_map/all_to_all | solution.py:658
  26.2 1.3 %collective-permute-start = (bf16[256,128]{1,0:T(8,128)(2,1)S(1)}, bf16[256,128]{1,0:T(8,128)(2,1)S(1)}, u32[]{:S(2)}, u32[]{:S(2)}) collective-permute-start(bf16[256,128]{1,0:T(8,128)(2,1)S(1)} %get-tuple-element.62.mine_ref), channel_id=1, source_target_pairs={{0,1},{1,0},{2,3},{3,2},{4,5},{5,4},{6,7},{7,6},{8,9},{9,8},{10,11... | collective-permute-start | bytes 196616 | tf_op jit(solution)/shard_map/ppermute | solution.py:729
  27.5 0.9 %copy-start.2 = (f32[192,128]{1,0:T(8,128)S(1)}, f32[192,128]{1,0:T(8,128)}, u32[]{:S(2)}) copy-start(f32[192,128]{1,0:T(8,128)} %get-tuple-element.64.pack_ref) | copy-start | bytes 294916
  28.4 1.0 %copy-start.4 = (f32[96,896]{1,0:T(8,128)S(1)}, f32[96,896]{1,0:T(8,128)}, u32[]{:S(2)}) copy-start(f32[96,896]{1,0:T(8,128)} %get-tuple-element.63.rows_ref) | copy-start | bytes 1032196

commit v9 on v8

--- a/solution.py
+++ b/solution.py
@@ -224,7 +224,7 @@
     r, count, _ = pair_ref.shape
     loads = copies(
         sems,
-        (pair_any, pair_ref),
+        *((pair_any.at[i], pair_ref.at[i]) for i in range(r)),
         (tri_any.at[:, 0 : 4 * CH], tri_ref),
         (single_any, single_ref),
         (quats_any, quats_ref),
@@ -547,8 +547,7 @@
     pair_out_any, half_ref, bias_ref, state_ref, new_frame_ref, send_ref, pair_ref, wide_ref, sems,
 ):
     r, count, _ = pair_ref.shape
-    load = pltpu.make_async_copy(pair_any, pair_ref, sems.at[0])
-    load.start()
+    loads = copies(sems, *((pair_any.at[i], pair_ref.at[i]) for i in range(r)))
     tri_out = gate_ref[r * count :, :]
     row, column = grid_of((2 * CH, 2 * CH))
     c = row & (CH - 1)
@@ -575,11 +574,12 @@
     bias_weight = jnp.concatenate(
         [jnp.where(((lane & (IP - 1)) == i) & (lane < ROWS), bias_weight, 0.0) for i in range(r)], axis=0
     )
-    load.wait()
+    for load in loads:
+        load.wait()
     pair = pair_ref[...].reshape(r * count, CH)
     pair_out = pair + gate_ref[0 : r * count, :].astype(f32) * update
     pair_ref[...] = pair_out.reshape(r, count, CH)
-    store = pltpu.make_async_copy(pair_ref, pair_out_any, sems.at[1])
+    store = pltpu.make_async_copy(pair_ref, pair_out_any, sems.at[r])
     store.start()
     normed_pair = layer_norm(pair_out)
     halves = normed_pair.astype(bf16)
@@ -677,7 +677,7 @@
             pltpu.SMEM((r,), jnp.int32),
             pltpu.SMEM((r,), jnp.int32),
             pltpu.VMEM((128, 128), f32),
-            dma((7,)),
+            dma((r + 6,)),
         ],
         limit=60,
     )
@@ -751,7 +751,7 @@
         outside=(1,),
         outside_outs=(0,),
         alias={1: 0},
-        scratch=[like(pair), pltpu.VMEM((2, 2 * CH, 128), f32), dma((2,))],
+        scratch=[like(pair), pltpu.VMEM((2, 2 * CH, 128), f32), dma((r + 1,))],
         limit=limit,
     )
     received = exchange(sent)

time: 50.2 us -> 50.3 us (level)
  no operation moved by 1% of the time
where the time goes in v9:
time: 50.3 us; the launch traced here: 49.9 us
  Pallas kernels  13.2 us (26%)
  waiting for transfers between devices  11.2 us (22%)
  blocking collectives  10.2 us (20%)
  starting transfers between devices  10 us (20%)
  local copies, waits for them, and re-layouts  3.74 us (7%)
  between operations  0.74 us (1%)
  other arithmetic  0.66 us (1%)
    pallas_call x6, Pallas kernels, call(): pl.pallas_call(body, name=name, out_shape=[jax.ShapeDtypeStruct(s, d) for...  13.2 us
    all_to_all x1, blocking collectives, exchange(): got = lax.all_to_all(sent.reshape(n, rows, width), 'row', 0, 0, tiled=True)  10.2 us
    all_to_all x2, waiting for transfers between devices, exchange(): got = lax.all_to_all(sent.reshape(n, rows, width), 'row', 0, 0, tiled=True)  10.1 us
    all_to_all x2, starting transfers between devices, exchange(): got = lax.all_to_all(sent.reshape(n, rows, width), 'row', 0, 0, tiled=True)  9.86 us
    unnamed x14, local copies, waits for them, and re-layouts  2.52 us
    ppermute x1, waiting for transfers between devices, local(): other = lax.ppermute(slots, 'row', [(i, i ^ 1) for i in range(n)])  1.14 us
  transfers between devices with their start and end apart: 3, of which 3 were waited for; matrix products, arithmetic and copies ran while one was open for 4% of the time, Pallas kernels for 9%

profile of v9, /device:TPU:0, one launch (start us, length us, event | category | flops | bytes accessed | tf_op | source)
XLA Modules:
  0.0 49.9 jit_solution(11658158757960073292)
XLA Ops:
  0.6 0.0 copy-start
  0.6 2.5 %gate.1 = (bf16[256,640]{1,0:T(8,128)(2,1)}, f32[8,128]{1,0:T(8,128)}) custom-call(f32[4,128,128]{2,1,0:T(8,128)} %pair_any.3, bf16[128,640]{1,0:T(8,128)(2,1)} %tri_any.3, f32[4,384]{1,0:T(4,128)} %single_any.3, f32[3,4]{1,0:T(4,128)} %quats_any.1, f32[3,4]{1,0:T(4,128)} %translate_any.1, s32[4]{0:T(128)} %mask_any.1, s32[4]{0:T(128)} %chain_any.1), custom_call_target="tpu_custom_call" | custom-call | tf_op jit(solution)/shard_map/gate/pallas_call | solution.py:632
  3.1 7.3 %all-to-all-start = ((bf16[32,8,640]{2,1,0:T(8,128)(2,1)}), bf16[32,8,640]{2,1,0:T(8,128)(2,1)S(1)}, u32[]{:S(2)}, u32[]{:S(2)}) async-start(bf16[32,8,640]{2,1,0:T(8,128)(2,1)} %bitcast.17), calls=%async_computation | async-start | bytes 655360 | tf_op jit(solution)/shard_map/all_to_all | solution.py:658
  10.4 0.7 %broadcast_multiply_fusion = f32[12]{0:T(128)S(1)} fusion(f32[12]{0:T(128)} %param.28), kind=kLoop, calls=%fused_computation.1 | loop fusion | flops 12 | bytes 96 | tf_op jit(solution)/shard_map/mul | solution.py:686
  11.1 0.1 broadcast_in_dim.7
  11.2 0.1 reshape.95
  11.3 0.8 %copy.20 = f32[12,2]{1,0:T(8,128)S(1)} copy(f32[12,2]{0,1:T(2,128)} %bitcast.20) | data formatting | bytes 192 | tf_op jit(solution)/shard_map/transpose | solution.py:687
  12.0 0.1 pad.11
  12.1 0.1 scatter.6
  12.3 0.1 scatter.9.columns_any
  12.3 0.0 copy-start.6
  12.4 0.6 %copy-done.6 = f32[136,128]{1,0:T(8,128)} copy-done((f32[136,128]{1,0:T(8,128)}, f32[136,128]{1,0:T(8,128)S(1)}, u32[]{:S(2)}) %copy-start.6) | copy-done | bytes 69656
  13.0 0.0 copy-start.1
  13.0 3.0 %own.1 = (bf16[640,128]{1,0:T(8,128)(2,1)}, f32[96,896]{1,0:T(8,128)}, f32[192,128]{1,0:T(8,128)}, f32[4,128,128]{2,1,0:T(8,128)}) custom-call(f32[4,128,128]{2,1,0:T(8,128)} %pair_any.3, bf16[128,640]{1,0:T(8,128)(2,1)} %tri_any.3, bf16[384,1152]{1,0:T(8,128)(2,1)} %qkv_ref.3, f32[4,384]{1,0:T(4,128)} %single_any.3, f32[8,128]{1,0:T(8,128)} %get-tuple-element.53.frame_any, ...), custom_call_target="tpu_custom_call" | custom-call | flops 16777216 | bytes 16777216 | tf_op jit(solution)/shard_map/own/pallas_call | solution.py:632
  16.0 0.0 copy-start.3
  16.0 0.0 copy-start.5
  16.0 6.4 %all-to-all-done = bf16[32,8,640]{2,1,0:T(8,128)(2,1)S(1)} async-done(((bf16[32,8,640]{2,1,0:T(8,128)(2,1)}), bf16[32,8,640]{2,1,0:T(8,128)(2,1)S(1)}, u32[]{:S(2)}, u32[]{:S(2)}) %all-to-all-start) | async-done | bytes 327712 | tf_op jit(solution)/shard_map/all_to_all | solution.py:658
  22.4 1.3 %product.1 = (bf16[256,256]{1,0:T(8,128)(2,1)}, bf16[256,128]{1,0:T(8,128)(2,1)S(1)}) custom-call(bf16[256,640]{1,0:T(8,128)(2,1)S(1)} %bitcast.13), custom_call_target="tpu_custom_call" | custom-call | tf_op jit(solution)/shard_map/product/pallas_call | solution.py:632
  23.7 2.6 %all-to-all-start.1 = ((bf16[32,8,256]{2,1,0:T(8,128)(2,1)}), bf16[32,8,256]{2,1,0:T(8,128)(2,1)S(1)}, u32[]{:S(2)}, u32[]{:S(2)}) async-start(bf16[32,8,256]{2,1,0:T(8,128)(2,1)} %bitcast.7), calls=%async_computation.1 | async-start | bytes 262144 | tf_op jit(solution)/shard_map/all_to_all | solution.py:658
  26.3 0.2 collective-permute-start
  26.4 1.1 %collective-permute-done.other_ref = bf16[256,128]{1,0:T(8,128)(2,1)S(1)} collective-permute-done((bf16[256,128]{1,0:T(8,128)(2,1)S(1)}, bf16[256,128]{1,0:T(8,128)(2,1)S(1)}, u32[]{:S(2)}, u32[]{:S(2)}) %collective-permute-start) | collective-permute-done | bytes 65568 | tf_op jit(solution)/shard_map/ppermute | solution.py:729
  27.6 0.0 copy-done
  27.6 0.0 copy-start.2
  27.6 0.9 %copy-done.2 = f32[192,128]{1,0:T(8,128)S(1)} copy-done((f32[192,128]{1,0:T(8,128)S(1)}, f32[192,128]{1,0:T(8,128)}, u32[]{:S(2)}) %copy-start.2) | copy-done | bytes 98328
  28.5 0.0 copy-start.4
  28.5 1.0 %copy-done.4 = f32[96,896]{1,0:T(8,128)S(1)} copy-done((f32[96,896]{1,0:T(8,128)S(1)}, f32[96,896]{1,0:T(8,128)}, u32[]{:S(2)}) %copy-start.4) | copy-done | bytes 344088
  29.4 1.3 %prepare.1 = (f32[96,128]{1,0:T(8,128)S(1)}, f32[128,640]{1,0:T(8,128)S(1)}) custom-call(bf16[256,128]{1,0:T(8,128)(2,1)S(1)} %get-tuple-element.62.mine_ref, bf16[256,128]{1,0:T(8,128)(2,1)S(1)} %collective-permute-done.other_ref, f32[96,896]{1,0:T(8,128)S(1)} %copy-done.4, bf16[384,1152]{1,0:T(8,128)(2,1)S(1)} %copy-done, f32[192,128]{1,0:T(8,128)S(1)} %copy-done.2), custom_call_target="tpu_custom_call" | custom-call | flops 113246208 | bytes 8388608 | tf_op jit(solution)/shard_map/prepare/pallas_call | solution.py:632
  30.8 3.7 %all-to-all-done.1 = bf16[32,8,256]{2,1,0:T(8,128)(2,1)S(1)} async-done(((bf16[32,8,256]{2,1,0:T(8,128)(2,1)}), bf16[32,8,256]{2,1,0:T(8,128)(2,1)S(1)}, u32[]{:S(2)}, u32[]{:S(2)}) %all-to-all-start.1) | async-done | bytes 131104 | tf_op jit(solution)/shard_map/all_to_all | solution.py:658
  34.5 0.0 copy-done.1
  34.5 0.0 copy-done.3
  34.5 0.0 copy-done.5
  34.5 2.5 %update.1 = (f32[4,128,128]{2,1,0:T(8,128)}, bf16[512,128]{1,0:T(8,128)(2,1)S(1)}, f32[96,128]{1,0:T(8,128)S(1)}, f32[8,384]{1,0:T(8,128)S(1)}, f32[8,128]{1,0:T(8,128)S(1)}, /*index=5*/bf16[256,256]{1,0:T(8,128)(2,1)S(1)}) custom-call(bf16[256,256]{1,0:T(8,128)(2,1)S(1)} %bitcast.15, ...), custom_call_target="tpu_custom_call", output_to_operand_aliasing={{0}: (1, {})} | custom-call | tf_op jit(solution)/shard_map/update/pallas_call | solution.py:632
  37.0 10.2 %all_to_all.15 = bf16[32,8,256]{2,1,0:T(8,128)(2,1)S(1)} all-to-all(bf16[32,8,256]{2,1,0:T(8,128)(2,1)S(1)} %bitcast.16), channel_id=1, replica_groups=mesh['grp'=1,'row'=32] {'row'}, dimensions={0} | all-to-all | bytes 262144 | tf_op jit(solution)/shard_map/all_to_all | solution.py:658
  47.2 2.6 %last.1 = (f32[4,384]{1,0:T(4,128)}, f32[4,9]{1,0:T(4,128)}, f32[3,4]{1,0:T(4,128)}) custom-call(bf16[256,256]{1,0:T(8,128)(2,1)S(1)} %bitcast.14, bf16[512,128]{1,0:T(8,128)(2,1)S(1)} %get-tuple-element.69.half_ref, f32[96,128]{1,0:T(8,128)S(1)} %get-tuple-element.70.bias_ref, f32[8,384]{1,0:T(8,128)S(1)} %get-tuple-element.71.state_ref, ...), custom_call_target="tpu_custom_call" | custom-call | tf_op jit(solution)/shard_map/last/pallas_call | solution.py:632
  (1 shorter events, 0.0 us)
Async XLA Ops:
  0.6 26.9 %copy-start = (bf16[384,1152]{1,0:T(8,128)(2,1)S(1)}, bf16[384,1152]{1,0:T(8,128)(2,1)}, u32[]{:S(2)}) copy-start(bf16[384,1152]{1,0:T(8,128)(2,1)} %qkv_ref.3) | copy-start | bytes 2654212
  3.1 19.3 %all-to-all-start = ((bf16[32,8,640]{2,1,0:T(8,128)(2,1)}), bf16[32,8,640]{2,1,0:T(8,128)(2,1)S(1)}, u32[]{:S(2)}, u32[]{:S(2)}) async-start(bf16[32,8,640]{2,1,0:T(8,128)(2,1)} %bitcast.17), calls=%async_computation | async-start | bytes 655360 | tf_op jit(solution)/shard_map/all_to_all | solution.py:658
  12.3 0.6 %copy-start.6 = (f32[136,128]{1,0:T(8,128)}, f32[136,128]{1,0:T(8,128)S(1)}, u32[]{:S(2)}) copy-start(f32[136,128]{1,0:T(8,128)S(1)} %scatter.9.columns_any) | copy-start | bytes 208900
  13.0 21.5 %copy-start.1 = (bf16[2112,384]{1,0:T(8,128)(2,1)S(1)}, bf16[2112,384]{1,0:T(8,128)(2,1)}, u32[]{:S(2)}) copy-start(bf16[2112,384]{1,0:T(8,128)(2,1)} %out_weight_ref.3) | copy-start | bytes 4866052
  16.0 18.5 %copy-start.3 = (f32[192,128]{1,0:T(8,128)S(1)}, f32[192,128]{1,0:T(8,128)}, u32[]{:S(2)}) copy-start(f32[192,128]{1,0:T(8,128)} %get-tuple-element.64.pack_ref) | copy-start | bytes 294916
  16.0 18.5 %copy-start.5 = (bf16[640,128]{1,0:T(8,128)(2,1)S(1)}, bf16[640,128]{1,0:T(8,128)(2,1)}, u32[]{:S(2)}) copy-start(bf16[640,128]{1,0:T(8,128)(2,1)} %get-tuple-element.61.gate_ref) | copy-start | bytes 491524
  23.7 10.8 %all-to-all-start.1 = ((bf16[32,8,256]{2,1,0:T(8,128)(2,1)}), bf16[32,8,256]{2,1,0:T(8,128)(2,1)S(1)}, u32[]{:S(2)}, u32[]{:S(2)}) async-start(bf16[32,8,256]{2,1,0:T(8,128)(2,1)} %bitcast.7), calls=%async_computation.1 | async-start | bytes 262144 | tf_op jit(solution)/shard_map/all_to_all | solution.py:658
  26.3 1.3 %collective-permute-start = (bf16[256,128]{1,0:T(8,128)(2,1)S(1)}, bf16[256,128]{1,0:T(8,128)(2,1)S(1)}, u32[]{:S(2)}, u32[]{:S(2)}) collective-permute-start(bf16[256,128]{1,0:T(8,128)(2,1)S(1)} %get-tuple-element.62.mine_ref), channel_id=1, source_target_pairs={{0,1},{1,0},{2,3},{3,2},{4,5},{5,4},{6,7},{7,6},{8,9},{9,8},{10,11... | collective-permute-start | bytes 196616 | tf_op jit(solution)/shard_map/ppermute | solution.py:729
  27.6 0.9 %copy-start.2 = (f32[192,128]{1,0:T(8,128)S(1)}, f32[192,128]{1,0:T(8,128)}, u32[]{:S(2)}) copy-start(f32[192,128]{1,0:T(8,128)} %get-tuple-element.64.pack_ref) | copy-start | bytes 294916
  28.5 1.0 %copy-start.4 = (f32[96,896]{1,0:T(8,128)S(1)}, f32[96,896]{1,0:T(8,128)}, u32[]{:S(2)}) copy-start(f32[96,896]{1,0:T(8,128)} %get-tuple-element.63.rows_ref) | copy-start | bytes 1032196
